TPU v7x, 32 devices: a whole 2x2x4 slice. The times are simulated.
32 devices in a mesh: batch: 16 (over z, y, core), head: 2 (over x).
Axes of the slice: x: 2, y: 2, z: 4, core: 2. Of those that a mesh axis runs over, the one named last changes fastest.
Arguments:
- inputs: bfloat16 [4, 32, 392, 768], P(None, ('batch', 'head')), may hold values from -6 to 6
- qkv_weight: bfloat16 [768, 8, 288], P(None, 'head'), may hold values from -0.21875 to 0.21875
- proj_weight: bfloat16 [8, 96, 768], P('head'), may hold values from -0.21875 to 0.21875
- pool_weight: bfloat16 [8, 4, 96], P('head'), may hold values from 0.29882812 to 0.8984375
- gain_one: float32 [768], replicated, may hold values from 0.5 to 1.5
- gain_two: float32 [768], replicated, may hold values from 0.5 to 1.5
- hidden_weight: bfloat16 [768, 3072], P(('batch', 'head')), may hold values from -0.21875 to 0.21875
- output_weight: bfloat16 [3072, 768], P(('batch', 'head')), may hold values from -0.109375 to 0.109375
- memory: bfloat16 [4, 32, 392, 8, 192], P(None, 'batch', None, 'head'), may hold values from -6 to 6
- clip_index: int32 [4, 32], P(None, 'batch'), may hold values from 0 to 11
- cotangent: bfloat16 [4, 32, 392, 768], P(None, ('batch', 'head')), may hold values from -6 to 6
Outputs:
- outputs: bfloat16 [4, 32, 392, 768], P(None, ('batch', 'head'))
- d_inputs: bfloat16 [4, 32, 392, 768], P(None, ('batch', 'head'))
- d_qkv_weight: float32 [768, 8, 288], P(None, 'head')
- d_proj_weight: float32 [8, 96, 768], P('head')
- d_pool_weight: float32 [8, 4, 96], P('head')
- d_gain_one: float32 [768], P(('batch', 'head'))
- d_gain_two: float32 [768], P(('batch', 'head'))
- d_hidden_weight: float32 [768, 3072], P(('batch', 'head'))
- d_output_weight: float32 [3072, 768], P(('batch', 'head'))
Inputs may be any that keep to these rules, and one draw needn't show every extreme that they name: `clip_index`: each clip's position in its video of 1 to 12 clips; memory slot r of a clip holds real data only when its index exceeds r, and other slots hold arbitrary values.
All inputs are finite; a program needn't handle non-finite values.
Results may differ from a plain program's by a relative error of at most 0.02.
Values may be sent and summed in bfloat16 or wider, within the bound.
A program may use at most 384 MiB of HBM per device.

v0:
```python
import jax
import jax.numpy as jnp
from jax import lax
from jax.sharding import PartitionSpec as P

HD = 96
FRAMES = 8
PTOK = 196
KEYS = 588


norm_eps = 1e-06
masked_score = -1000000000.0


def layer_norm(values, gain_vector):
    average = jnp.mean(values, axis=-1, keepdims=True)
    centered = values - average
    variance = jnp.mean(centered * centered, axis=-1, keepdims=True)
    return centered * lax.rsqrt(variance + norm_eps) * gain_vector


def pool_pairs(raw_rows, first_tap, second_tap):
    clip_total, token_total, head_total, head_width = raw_rows.shape
    paired = raw_rows.reshape(
        clip_total, FRAMES // 2, 2, token_total // FRAMES, head_total, head_width
    )
    merged = first_tap * paired[:, :, 0] + second_tap * paired[:, :, 1]
    return merged.reshape(clip_total, token_total // 2, head_total, head_width)


def key_mask(indices):
    position = lax.broadcasted_iota(jnp.int32, indices.shape + (KEYS,), indices.ndim)
    return indices[..., None] > position // PTOK - 1


def gelu_slope(values):
    cumulative = 0.5 * (1.0 + lax.erf(values * 0.7071067811865476))
    density = jnp.exp(-0.5 * values * values) * 0.3989422804014327
    return cumulative + values * density


def masked_scores(queries, key_all, key_valid):
    scores = jnp.einsum(
        "cqhe,ckhe->chqk", queries, key_all, preferred_element_type=jnp.float32
    ) * HD ** (-0.5)
    return jnp.where(key_valid[:, None, None, :], scores, masked_score)


def attend_forward(normed, qkv_local, taps, memory_rows, key_valid):
    packed = jnp.einsum("ctd,dhe->cthe", normed, qkv_local, preferred_element_type=jnp.float32)
    queries = packed[..., :HD].astype(jnp.bfloat16)
    pooled_keys = pool_pairs(packed[..., HD : 2 * HD], taps[:, 0], taps[:, 1]).astype(jnp.bfloat16)
    pooled_values = pool_pairs(packed[..., 2 * HD :], taps[:, 2], taps[:, 3]).astype(jnp.bfloat16)
    key_all = jnp.concatenate([pooled_keys, memory_rows[..., :HD]], axis=1)
    value_all = jnp.concatenate([pooled_values, memory_rows[..., HD:]], axis=1)
    scores = masked_scores(queries, key_all, key_valid)
    maxima = jnp.max(scores, axis=-1, keepdims=True)
    log_total = maxima + jnp.log(jnp.sum(jnp.exp(scores - maxima), axis=-1, keepdims=True))
    attention_low = jnp.exp(scores - log_total).astype(jnp.bfloat16)
    attended = (
        jnp.einsum("chqk,ckhe->cqhe", attention_low, value_all, preferred_element_type=jnp.float32)
        + packed[..., :HD]
    )
    return (attended.astype(jnp.bfloat16), (packed, queries, key_all, value_all, log_total))


def attend_backward(grad_out, taps, stored, key_valid):
    packed, queries, key_all, value_all, log_total = stored
    attention = jnp.exp(masked_scores(queries, key_all, key_valid) - log_total)
    grad_attention = jnp.einsum(
        "cqhe,ckhe->chqk", grad_out, value_all, preferred_element_type=jnp.float32
    )
    row_inner = jnp.sum(attention * grad_attention, axis=-1, keepdims=True)
    grad_scores = (attention * (grad_attention - row_inner)).astype(jnp.bfloat16)
    score_scale = HD ** (-0.5)
    grad_queries = jnp.einsum(
        "chqk,ckhe->cqhe", grad_scores, key_all, preferred_element_type=jnp.float32
    ) * score_scale + grad_out.astype(jnp.float32)
    grad_keys = (
        jnp.einsum(
            "chqk,cqhe->ckhe", grad_scores[..., :PTOK], queries, preferred_element_type=jnp.float32
        )
        * score_scale
    )
    grad_values = jnp.einsum(
        "chqk,cqhe->ckhe",
        attention.astype(jnp.bfloat16)[..., :PTOK],
        grad_out,
        preferred_element_type=jnp.float32,
    )
    keys_pooled, keys_pull = jax.vjp(pool_pairs, packed[..., HD : 2 * HD], taps[:, 0], taps[:, 1])
    values_pooled, values_pull = jax.vjp(pool_pairs, packed[..., 2 * HD :], taps[:, 2], taps[:, 3])
    grad_raw_keys, tap_zero, tap_one = keys_pull(grad_keys)
    grad_raw_values, tap_two, tap_three = values_pull(grad_values)
    grad_packed = jnp.concatenate([grad_queries, grad_raw_keys, grad_raw_values], axis=-1).astype(
        jnp.bfloat16
    )
    return (grad_packed, jnp.stack([tap_zero, tap_one, tap_two, tap_three], axis=1))


def fetch_mlp(hidden_weight, output_weight):
    return (
        lax.all_gather(hidden_weight, ("batch", "head"), axis=0, tiled=True),
        lax.all_gather(output_weight, ("batch", "head"), axis=0, tiled=True),
    )


def local(
    inputs,
    qkv_weight,
    proj_weight,
    pool_weight,
    gain_one,
    gain_two,
    hidden_weight,
    output_weight,
    memory,
    clip_index,
    cotangent,
):
    model_width = output_weight.shape[1]
    hidden_width = hidden_weight.shape[1]
    qkv_used, proj_used, pool_used = (qkv_weight, proj_weight, pool_weight)
    memory_used, index_used = (memory, clip_index)
    taps = pool_used.astype(jnp.float32)
    qkv_acc = jnp.zeros(qkv_used.shape, jnp.float32)
    proj_acc = jnp.zeros(proj_used.shape, jnp.float32)
    pool_acc = jnp.zeros(pool_used.shape, jnp.float32)
    gain_one_acc = jnp.zeros(gain_one.shape, jnp.float32)
    gain_two_acc = jnp.zeros(gain_two.shape, jnp.float32)
    hidden_acc = jnp.zeros((model_width, hidden_width), jnp.float32)
    output_acc = jnp.zeros((hidden_width, model_width), jnp.float32)
    outputs_list = []
    grads_list = []
    for micro_step in range(inputs.shape[0]):
        rows_in = inputs[micro_step].astype(jnp.float32)
        normed_float, norm_one_pull = jax.vjp(layer_norm, rows_in, gain_one)
        normed_one = normed_float.astype(jnp.bfloat16)
        key_valid = key_mask(index_used[micro_step])
        operand_rows = lax.all_gather(normed_one, "head", axis=0, tiled=True)
        attended, stored = attend_forward(
            operand_rows, qkv_used, taps, memory_used[micro_step], key_valid
        )
        branch = lax.psum_scatter(
            jnp.einsum(
                "cthe,hed->ctd", attended, proj_used, preferred_element_type=jnp.float32
            ).astype(jnp.bfloat16),
            "head",
            scatter_dimension=0,
            tiled=True,
        ).astype(jnp.float32)
        middle = rows_in + branch
        normed_second, norm_two_pull = jax.vjp(layer_norm, middle, gain_two)
        normed_two = normed_second.astype(jnp.bfloat16).reshape(-1, model_width)
        first_full, second_full = fetch_mlp(hidden_weight, output_weight)
        hidden = jnp.dot(normed_two, first_full, preferred_element_type=jnp.float32)
        active = jax.nn.gelu(hidden, approximate=False).astype(jnp.bfloat16)
        feed_out = jnp.dot(active, second_full, preferred_element_type=jnp.float32)
        outputs_list.append((middle + feed_out.reshape(middle.shape)).astype(jnp.bfloat16))
        first_full, second_full = fetch_mlp(hidden_weight, output_weight)
        grad_rows_out = cotangent[micro_step].reshape(-1, model_width)
        grad_active = jnp.einsum(
            "rd,fd->rf", grad_rows_out, second_full, preferred_element_type=jnp.float32
        )
        output_acc = output_acc + jnp.einsum(
            "rf,rd->fd", active, grad_rows_out, preferred_element_type=jnp.float32
        )
        grad_hidden = (gelu_slope(hidden) * grad_active).astype(jnp.bfloat16)
        hidden_acc = hidden_acc + jnp.einsum(
            "rd,rf->df", normed_two, grad_hidden, preferred_element_type=jnp.float32
        )
        grad_norm_two = jnp.einsum(
            "rf,df->rd", grad_hidden, first_full, preferred_element_type=jnp.float32
        )
        grad_middle_part, gain_two_part = norm_two_pull(grad_norm_two.reshape(middle.shape))
        gain_two_acc = gain_two_acc + gain_two_part
        grad_middle = cotangent[micro_step].astype(jnp.float32) + grad_middle_part
        grad_branch = grad_middle.astype(jnp.bfloat16)
        arrived = lax.all_gather(grad_branch, "head", axis=0, tiled=True)
        proj_sum = proj_acc
        grad_piece = jnp.einsum(
            "ctd,hed->cthe", arrived, proj_used, preferred_element_type=jnp.float32
        )
        grad_full = grad_piece
        proj_sum = proj_sum + jnp.einsum(
            "cthe,ctd->hed", attended, arrived, preferred_element_type=jnp.float32
        )
        grad_full, proj_acc = (grad_full, proj_sum)
        grad_attended = grad_full.astype(jnp.bfloat16)
        grad_packed, grad_taps = attend_backward(grad_attended, taps, stored, key_valid)
        pool_acc = pool_acc + grad_taps
        qkv_acc = qkv_acc + jnp.einsum(
            "ctd,cthe->dhe", operand_rows, grad_packed, preferred_element_type=jnp.float32
        )
        grad_norm_one = lax.psum_scatter(
            jnp.einsum(
                "cthe,dhe->ctd", grad_packed, qkv_used, preferred_element_type=jnp.float32
            ).astype(jnp.bfloat16),
            "head",
            scatter_dimension=0,
            tiled=True,
        ).astype(jnp.float32)
        grad_input_part, gain_one_part = norm_one_pull(grad_norm_one)
        gain_one_acc = gain_one_acc + gain_one_part
        grads_list.append((grad_middle + grad_input_part).astype(jnp.bfloat16))
    qkv_acc, proj_acc, pool_acc = (
        lax.psum(qkv_acc.astype(jnp.bfloat16), "batch").astype(jnp.float32),
        lax.psum(proj_acc.astype(jnp.bfloat16), "batch").astype(jnp.float32),
        lax.psum(pool_acc.astype(jnp.bfloat16), "batch").astype(jnp.float32),
    )
    hidden_acc, output_acc, gain_one_acc, gain_two_acc = (
        lax.psum_scatter(hidden_acc, ("batch", "head"), scatter_dimension=0, tiled=True),
        lax.psum_scatter(output_acc, ("batch", "head"), scatter_dimension=0, tiled=True),
        lax.psum_scatter(gain_one_acc, ("batch", "head"), scatter_dimension=0, tiled=True),
        lax.psum_scatter(gain_two_acc, ("batch", "head"), scatter_dimension=0, tiled=True),
    )
    return (
        jnp.stack(outputs_list),
        jnp.stack(grads_list),
        qkv_acc,
        proj_acc,
        pool_acc,
        gain_one_acc,
        gain_two_acc,
        hidden_acc,
        output_acc,
    )


def solution(mesh):
    return jax.shard_map(
        local,
        mesh=mesh,
        in_specs=(
            P(None, ("batch", "head"), None, None),
            P(None, "head", None),
            P("head", None, None),
            P("head", None, None),
            P(),
            P(),
            P(("batch", "head"), None),
            P(("batch", "head"), None),
            P(None, "batch", None, "head", None),
            P(None, "batch"),
            P(None, ("batch", "head"), None, None),
        ),
        out_specs=(
            P(None, ("batch", "head"), None, None),
            P(None, ("batch", "head"), None, None),
            P(None, "head", None),
            P("head", None, None),
            P("head", None, None),
            P(("batch", "head")),
            P(("batch", "head")),
            P(("batch", "head"), None),
            P(("batch", "head"), None),
        ),
        check_vma=False,
    )
```

profile of v0, /device:TPU:0, one launch (start us, length us, event | category | flops | bytes accessed | tf_op | source)
XLA Modules:
  0.0 1186.5 jit_solution(5449269584461418051)
XLA Ops:
  19.0 19.3 %all-gather.19.cloned.1.call-done = bf16[2,392,768]{2,1,0:T(8,128)(2,1)} async-done(((bf16[1,392,768]{2,1,0:T(8,128)(2,1)}), bf16[2,392,768]{2,1,0:T(8,128)(2,1)}) %all-gather.19.cloned.1.call-update) | async-done | bytes 1204240 | tf_op jit(solution)/shard_map/all_gather | solution.py:141
  83.6 21.8 %reduce-scatter.15.cloned.1.call-done = bf16[1,392,768]{2,1,0:T(8,128)(2,1)} async-done(((bf16[2,392,768]{2,1,0:T(8,128)(2,1)}), bf16[1,392,768]{2,1,0:T(8,128)(2,1)}) %reduce-scatter.15.cloned.1.call-update) | async-done | bytes 602128 | tf_op jit(solution)/shard_map/reduce_scatter | solution.py:145
  118.4 15.8 %all-gather.17.cloned.1.call-done = bf16[2,392,768]{2,1,0:T(8,128)(2,1)} async-done(((bf16[1,392,768]{2,1,0:T(8,128)(2,1)}), bf16[2,392,768]{2,1,0:T(8,128)(2,1)}) %all-gather.17.cloned.1.call-update) | async-done | bytes 1204240 | tf_op jit(solution)/shard_map/all_gather | solution.py:141
  150.9 7.8 all-gather.21.cloned.1.call-done
  175.3 7.9 all-gather.11.cloned.1.call-done
  237.5 13.5 %exponential_reduce_fusion = f32[2,4,392]{2,1,0:T(4,128)S(1)} fusion(f32[2,4,392,588]{3,2,1,0:T(8,128)S(1)} %get-tuple-element.173, f32[2,4,392]{2,1,0:T(4,128)S(1)} %get-tuple-element.172, pred[2,588]{1,0:T(4,128)(4,1)S(1)} %get-tuple-element.149), kind=kLoop, calls=%fused_computation.11 | loop fusion | flops 7372736 | bytes 7402136 | tf_op jit(solution)/shard_map/reduce_sum | solution.py:59
  292.7 15.3 %fusion.12 = (bf16[392,3072]{1,0:T(8,128)(2,1)}, f32[392,3072]{1,0:T(8,128)}) fusion(bf16[768,3072]{1,0:T(8,128)(2,1)} %all-gather.13.cloned.1.call-done, bf16[1,392,768]{2,1,0:T(8,128)(2,1)S(1)} %copy-done.70, f32[392]{0:T(512)S(1)} %fusion.322, f32[392]{0:T(512)S(1)} %broadcast_multiply_fusion.18, f32[768]{0:T(1024)S(1)} %copy-done.156, ...), kind=kOutput, calls=%fused_computation.42 | convolution fusion | flops 1930070016 | bytes 13154368 | tf_op jit(solution)/shard_map/dot_general | solution.py:157
  321.5 17.2 %reduce-scatter.17.cloned.1.call-done = bf16[1,392,768]{2,1,0:T(8,128)(2,1)} async-done(((bf16[2,392,768]{2,1,0:T(8,128)(2,1)}), bf16[1,392,768]{2,1,0:T(8,128)(2,1)}) %reduce-scatter.17.cloned.1.call-update) | async-done | bytes 602128 | tf_op jit(solution)/shard_map/reduce_scatter | solution.py:145
  338.7 24.3 %reduce-scatter.11.cloned.1.call-done = bf16[1,392,768]{2,1,0:T(8,128)(2,1)} async-done(((bf16[2,392,768]{2,1,0:T(8,128)(2,1)}), bf16[1,392,768]{2,1,0:T(8,128)(2,1)}) %reduce-scatter.11.cloned.1.call-update) | async-done | bytes 602128 | tf_op jit(solution)/shard_map/reduce_scatter | solution.py:145
  363.0 24.2 %reduce-scatter.13.cloned.1.call-done = bf16[1,392,768]{2,1,0:T(8,128)(2,1)} async-done(((bf16[2,392,768]{2,1,0:T(8,128)(2,1)}), bf16[1,392,768]{2,1,0:T(8,128)(2,1)}) %reduce-scatter.13.cloned.1.call-update) | async-done | bytes 602128 | tf_op jit(solution)/shard_map/reduce_scatter | solution.py:145
  387.2 7.4 fusion.233
  399.9 23.0 %all-gather.27.cloned.1.call-done = bf16[2,392,768]{2,1,0:T(8,128)(2,1)} async-done(((bf16[1,392,768]{2,1,0:T(8,128)(2,1)}), bf16[2,392,768]{2,1,0:T(8,128)(2,1)}) %all-gather.27.cloned.1.call-update) | async-done | bytes 1204240 | tf_op jit(solution)/shard_map/all_gather | solution.py:180
  453.2 21.9 %reduce-scatter.23.cloned.1.call-done = bf16[1,392,768]{2,1,0:T(8,128)(2,1)} async-done(((bf16[2,392,768]{2,1,0:T(8,128)(2,1)}), bf16[1,392,768]{2,1,0:T(8,128)(2,1)}) %reduce-scatter.23.cloned.1.call-update) | async-done | bytes 602128 | tf_op jit(solution)/shard_map/reduce_scatter | solution.py:196
  479.0 15.1 %fusion.15 = (bf16[392,3072]{1,0:T(8,128)(2,1)}, f32[392,3072]{1,0:T(8,128)S(1)}) fusion(bf16[768,3072]{1,0:T(8,128)(2,1)} %all-gather.13.cloned.1.call-done, bf16[1,392,768]{2,1,0:T(8,128)(2,1)S(1)} %copy-done.67, f32[392]{0:T(512)S(1)} %fusion.324, f32[392]{0:T(512)S(1)} %broadcast_multiply_fusion.16, f32[768]{0:T(1024)S(1)} %copy-done.156, ...), kind=kOutput, calls=%fused_computation.45 | convolution fusion | flops 1930070016 | bytes 13156352 | tf_op jit(solution)/shard_map/dot_general | solution.py:157
  494.1 13.1 %fusion.9 = (bf16[392,3072]{1,0:T(8,128)(2,1)}, f32[392,3072]{1,0:T(8,128)S(1)}) fusion(bf16[768,3072]{1,0:T(8,128)(2,1)S(1)} %bitcast.851, bf16[1,392,768]{2,1,0:T(8,128)(2,1)S(1)} %copy-done.105, f32[392]{0:T(512)S(1)} %fusion.320, f32[392]{0:T(512)S(1)} %broadcast_multiply_fusion.20, f32[768]{0:T(1024)S(1)} %copy-done.156, ...), kind=kOutput, calls=%fused_computation.39 | convolution fusion | flops 1930070016 | bytes 13156352 | tf_op jit(solution)/shard_map/dot_general | solution.py:157
  507.3 16.6 %fusion.6 = (bf16[392,3072]{1,0:T(8,128)(2,1)}, f32[392,3072]{1,0:T(8,128)}) fusion(bf16[768,3072]{1,0:T(8,128)(2,1)S(1)} %bitcast.851, bf16[1,392,768]{2,1,0:T(8,128)(2,1)S(1)} %copy-done.102, f32[768]{0:T(1024)S(1)} %copy-done.156, f32[392]{0:T(512)S(1)} %fusion.318, f32[392]{0:T(512)S(1)} %broadcast_multiply_fusion.22, ...), kind=kOutput, calls=%fused_computation.36 | convolution fusion | flops 1930070016 | bytes 13156352 | tf_op jit(solution)/shard_map/dot_general | solution.py:157
  554.6 15.3 %all-gather.29.cloned.1.call-done = bf16[2,392,768]{2,1,0:T(8,128)(2,1)} async-done(((bf16[1,392,768]{2,1,0:T(8,128)(2,1)}), bf16[2,392,768]{2,1,0:T(8,128)(2,1)}) %all-gather.29.cloned.1.call-update) | async-done | bytes 1204240 | tf_op jit(solution)/shard_map/all_gather | solution.py:180
  575.9 7.9 multiply_reduce_fusion
  583.8 10.6 all-gather.25.cloned.1.call-done
  600.3 7.5 multiply_reduce_fusion.2
  607.8 11.1 all-gather.23.cloned.1.call-done
  633.7 7.9 multiply_convert_fusion.2
  733.6 8.5 fusion.352
  745.1 8.4 fusion.360
  758.9 15.0 %add_add_fusion.1 = f32[768,3072]{1,0:T(8,128)} fusion(f32[768,3072]{1,0:T(8,128)} %fusion.352, f32[768,3072]{1,0:T(8,128)} %fusion.360, f32[768,3072]{1,0:T(8,128)} %fusion.356, bf16[392,3072]{1,0:T(8,128)(2,1)S(1)} %copy-done.101, bf16[1,392,768]{2,1,0:T(8,128)(2,1)S(1)} %copy-done.68, f32[392]{0:T(512)S(1)} %fusion.324, ...), kind=kOutput, calls=%fused_computation.1 | convolution fusion | flops 1858873344 | bytes 41369600 | tf_op jit(solution)/shard_map/rd,rf->df/dot_general | solution.py:170
  789.0 13.7 %add_add_fusion = f32[3072,768]{1,0:T(8,128)} fusion(f32[3072,768]{1,0:T(8,128)S(1)} %fusion.270, f32[3072,768]{1,0:T(8,128)} %fusion.276, f32[3072,768]{1,0:T(8,128)} %fusion.273, bf16[392,3072]{1,0:T(8,128)(2,1)} %get-tuple-element.181, bf16[4,1,392,768]{3,2,1,0:T(8,128)(2,1)S(1)} %copy-done.21), kind=kOutput, calls=%fused_computation | convolution fusion | flops 1856765952 | bytes 40759296 | tf_op jit(solution)/shard_map/rf,rd->fd/dot_general | solution.py:166
  820.5 33.6 %psum.23 = bf16[4,4,96]{2,1,0:T(4,128)(2,1)S(1)} all-reduce(bf16[4,4,96]{2,1,0:T(4,128)(2,1)S(1)} %fusion.309), channel_id=1, replica_groups=mesh['batch'=16,'head'=2] {'batch'}, use_global_device_ids=true, to_apply=%region_70.71 | all-reduce | flops 1536 | bytes 6144 | tf_op jit(solution)/shard_map/psum | solution.py:210
  859.5 11.4 reduce-scatter.21.cloned.1.call-done
  871.0 24.3 %reduce-scatter.25.cloned.1.call-done = bf16[1,392,768]{2,1,0:T(8,128)(2,1)} async-done(((bf16[2,392,768]{2,1,0:T(8,128)(2,1)}), bf16[1,392,768]{2,1,0:T(8,128)(2,1)}) %reduce-scatter.25.cloned.1.call-update) | async-done | bytes 602128 | tf_op jit(solution)/shard_map/reduce_scatter | solution.py:196
  901.7 39.5 %all-reduce.18 = (f32[768]{0:T(1024)S(1)}, f32[768]{0:T(1024)S(1)}) all-reduce(f32[768]{0:T(1024)S(1)} %add_add_fusion.11, f32[768]{0:T(1024)S(1)} %add_add_fusion.10), channel_id=10, replica_groups=mesh['batch'=16,'head'=2] {'batch','head'}, use_global_device_ids=true, to_apply=%region_75.76.clone | all-reduce | flops 1536 | bytes 12288
  951.1 86.1 %reduce-scatter.27.cloned.1.call-done = f32[24,3072]{1,0:T(8,128)} async-done(((f32[768,3072]{1,0:T(8,128)}), f32[24,3072]{1,0:T(8,128)}) %reduce-scatter.27.cloned.1.call-update) | async-done | bytes 294928 | tf_op jit(solution)/shard_map/reduce_scatter | solution.py:213
  1037.3 142.1 %reduce-scatter.29.cloned.1.call-done = f32[96,768]{1,0:T(8,128)} async-done(((f32[3072,768]{1,0:T(8,128)}), f32[96,768]{1,0:T(8,128)}) %reduce-scatter.29.cloned.1.call-update) | async-done | bytes 294928 | tf_op jit(solution)/shard_map/reduce_scatter | solution.py:214
  (771 shorter events, 461.4 us)
Async XLA Ops:
  7.2 31.1 %all-gather.19.cloned.1.call-start = ((), (), s32[]{:S(2)}) async-start(), calls=%async_computation.16 | async-start | bytes 1806336 | tf_op jit(solution)/shard_map/all_gather | solution.py:141
  12.4 93.1 %reduce-scatter.15.cloned.1.call-start = ((), (), s32[]{:S(2)}) async-start(), calls=%async_computation.17 | async-start | bytes 1806336 | tf_op jit(solution)/shard_map/reduce_scatter | solution.py:145
  12.7 430.7 %copy-start.161 = (f32[4,1,96]{2,1,0:T(1,128)}, f32[4,1,96]{2,1,0:T(1,128)S(1)}, u32[]{:S(2)}) copy-start(f32[4,1,96]{2,1,0:T(1,128)S(1)} %get-tuple-element.166) | copy-start | bytes 4612
  12.7 430.7 %copy-start.163 = (f32[4,1,96]{2,1,0:T(1,128)}, f32[4,1,96]{2,1,0:T(1,128)S(1)}, u32[]{:S(2)}) copy-start(f32[4,1,96]{2,1,0:T(1,128)S(1)} %get-tuple-element.167) | copy-start | bytes 4612
  12.8 433.4 %copy-start.157 = (f32[4,1,96]{2,1,0:T(1,128)}, f32[4,1,96]{2,1,0:T(1,128)S(1)}, u32[]{:S(2)}) copy-start(f32[4,1,96]{2,1,0:T(1,128)S(1)} %get-tuple-element.168) | copy-start | bytes 4612
  12.8 433.4 %copy-start.159 = (f32[4,1,96]{2,1,0:T(1,128)}, f32[4,1,96]{2,1,0:T(1,128)S(1)}, u32[]{:S(2)}) copy-start(f32[4,1,96]{2,1,0:T(1,128)S(1)} %get-tuple-element.169) | copy-start | bytes 4612
  12.9 239.6 %copy-start.141 = (pred[2,588]{1,0:T(4,128)(4,1)}, pred[2,588]{1,0:T(4,128)(4,1)S(1)}, u32[]{:S(2)}) copy-start(pred[2,588]{1,0:T(4,128)(4,1)S(1)} %get-tuple-element.149) | copy-start | bytes 3532
  12.9 254.2 %copy-start.145 = (pred[2,588]{1,0:T(4,128)(4,1)}, pred[2,588]{1,0:T(4,128)(4,1)S(1)}, u32[]{:S(2)}) copy-start(pred[2,588]{1,0:T(4,128)(4,1)S(1)} %get-tuple-element.151) | copy-start | bytes 3532
  12.9 269.7 %copy-start.143 = (pred[2,588]{1,0:T(4,128)(4,1)}, pred[2,588]{1,0:T(4,128)(4,1)S(1)}, u32[]{:S(2)}) copy-start(pred[2,588]{1,0:T(4,128)(4,1)S(1)} %get-tuple-element.148) | copy-start | bytes 3532
  83.3 50.9 %all-gather.17.cloned.1.call-start = ((), (), s32[]{:S(2)}) async-start(), calls=%async_computation.14 | async-start | bytes 1806336 | tf_op jit(solution)/shard_map/all_gather | solution.py:141
  108.9 285.8 %copy-start.173 = (f32[392]{0:T(512)}, f32[392]{0:T(512)S(1)}, u32[]{:S(2)}) copy-start(f32[392]{0:T(512)S(1)} %broadcast_multiply_fusion.18) | copy-start | bytes 4708
  111.0 47.7 %all-gather.21.cloned.1.call-start = ((), (), s32[]{:S(2)}) async-start(), calls=%async_computation.18 | async-start | bytes 1806336 | tf_op jit(solution)/shard_map/all_gather | solution.py:141
  111.6 71.6 %all-gather.11.cloned.1.call-start = ((), (), s32[]{:S(2)}) async-start(), calls=%async_computation.10 | async-start | bytes 1806336 | tf_op jit(solution)/shard_map/all_gather | solution.py:141
  112.1 180.6 %all-gather.13.cloned.1.call-start = ((), (), s32[]{:S(2)}) async-start(), calls=%async_computation.12 | async-start | bytes 4866048 | tf_op jit(solution)/shard_map/all_gather | solution.py:104
  112.7 202.3 %all-gather.15.cloned.1.call-start = ((), (), s32[]{:S(2)}) async-start(), calls=%async_computation.13 | async-start | bytes 4866048 | tf_op jit(solution)/shard_map/all_gather | solution.py:105
  113.5 225.2 %reduce-scatter.17.cloned.1.call-start = ((), (), s32[]{:S(2)}) async-start(), calls=%async_computation.19 | async-start | bytes 1806336 | tf_op jit(solution)/shard_map/reduce_scatter | solution.py:145
  117.3 152.5 %copy-start.30 = (bf16[2,392,4,96]{1,3,2,0:T(8,128)(2,1)}, bf16[2,392,4,96]{1,3,2,0:T(8,128)(2,1)S(1)}, u32[]{:S(2)}) copy-start(bf16[2,392,4,96]{1,3,2,0:T(8,128)(2,1)S(1)} %get-tuple-element.126) | copy-start | bytes 1806340
  118.4 166.8 %copy-start.32 = (bf16[2,392,4,96]{1,3,2,0:T(8,128)(2,1)}, bf16[2,392,4,96]{1,3,2,0:T(8,128)(2,1)S(1)}, u32[]{:S(2)}) copy-start(bf16[2,392,4,96]{1,3,2,0:T(8,128)(2,1)S(1)} %get-tuple-element.124) | copy-start | bytes 1806340
  118.4 276.2 %copy-start.210 = (f32[392]{0:T(512)}, f32[392]{0:T(512)S(1)}, u32[]{:S(2)}) copy-start(f32[392]{0:T(512)S(1)} %fusion.322) | copy-start | bytes 4708
  261.1 101.9 %reduce-scatter.11.cloned.1.call-start = ((), (), s32[]{:S(2)}) async-start(), calls=%async_computation.11 | async-start | bytes 1806336 | tf_op jit(solution)/shard_map/reduce_scatter | solution.py:145
  276.8 110.4 %reduce-scatter.13.cloned.1.call-start = ((), (), s32[]{:S(2)}) async-start(), calls=%async_computation.15 | async-start | bytes 1806336 | tf_op jit(solution)/shard_map/reduce_scatter | solution.py:145
  292.2 130.6 %all-gather.27.cloned.1.call-start = ((), (), s32[]{:S(2)}) async-start(), calls=%async_computation.24 | async-start | bytes 1806336 | tf_op jit(solution)/shard_map/all_gather | solution.py:180
  399.7 75.4 %reduce-scatter.23.cloned.1.call-start = ((), (), s32[]{:S(2)}) async-start(), calls=%async_computation.25 | async-start | bytes 1806336 | tf_op jit(solution)/shard_map/reduce_scatter | solution.py:196
  452.9 117.0 %all-gather.29.cloned.1.call-start = ((), (), s32[]{:S(2)}) async-start(), calls=%async_computation.26 | async-start | bytes 1806336 | tf_op jit(solution)/shard_map/all_gather | solution.py:180
  546.7 47.7 %all-gather.25.cloned.1.call-start = ((), (), s32[]{:S(2)}) async-start(), calls=%async_computation.22 | async-start | bytes 1806336 | tf_op jit(solution)/shard_map/all_gather | solution.py:180
  547.3 71.6 %all-gather.23.cloned.1.call-start = ((), (), s32[]{:S(2)}) async-start(), calls=%async_computation.20 | async-start | bytes 1806336 | tf_op jit(solution)/shard_map/all_gather | solution.py:180
  554.5 300.1 %all-reduce.22.cloned.1.call-start = ((), (), s32[]{:S(2)}) async-start(), calls=%async_computation.30 | async-start | bytes 4718592 | tf_op jit(solution)/shard_map/psum | solution.py:208
  724.2 135.4 %reduce-scatter.19.cloned.1.call-start = ((), (), s32[]{:S(2)}) async-start(), calls=%async_computation.21 | async-start | bytes 1806336 | tf_op jit(solution)/shard_map/reduce_scatter | solution.py:196
  728.7 142.2 %reduce-scatter.21.cloned.1.call-start = ((), (), s32[]{:S(2)}) async-start(), calls=%async_computation.23 | async-start | bytes 1806336 | tf_op jit(solution)/shard_map/reduce_scatter | solution.py:196
  733.5 161.8 %reduce-scatter.25.cloned.1.call-start = ((), (), s32[]{:S(2)}) async-start(), calls=%async_computation.27 | async-start | bytes 1806336 | tf_op jit(solution)/shard_map/reduce_scatter | solution.py:196
  745.0 292.3 %reduce-scatter.27.cloned.1.call-start = ((), (), s32[]{:S(2)}) async-start(), calls=%async_computation.28 | async-start | bytes 9732096 | tf_op jit(solution)/shard_map/reduce_scatter | solution.py:213
  773.9 405.5 %reduce-scatter.29.cloned.1.call-start = ((), (), s32[]{:S(2)}) async-start(), calls=%async_computation.29 | async-start | bytes 9732096 | tf_op jit(solution)/shard_map/reduce_scatter | solution.py:214
  (239 other events, 1999.4 us)
Sparse Core Ops, SparseCore 0:
  12.5 25.7 all-gather.18
  83.4 22.0 reduce-scatter.14
  111.1 23.0 all-gather.16
  135.6 23.0 all-gather.20
  160.1 23.0 all-gather.10
  185.9 63.6 all-gather.12
  252.5 62.4 all-gather.14
  317.8 20.8 reduce-scatter.16
  341.0 22.0 reduce-scatter.10
  365.1 22.0 reduce-scatter.12
  399.8 23.0 all-gather.26
  453.0 22.0 reduce-scatter.22
  546.8 23.0 all-gather.28
  571.3 23.0 all-gather.24
  595.8 23.0 all-gather.22
  724.3 98.9 all-reduce.21
  825.4 21.3 reduce-scatter.18
  848.9 22.0 reduce-scatter.20
  873.2 22.0 reduce-scatter.24
  901.6 135.6 reduce-scatter.26
  1044.7 134.5 reduce-scatter.28
where the time goes:
time: 1200 us; the launch traced here: 1190 us
  waiting for transfers between devices  494 us (41%)
  matrix products  340 us (28%)
  local copies, waits for them, and re-layouts  158 us (13%)
  other arithmetic  101 us (8%)
  blocking collectives  73 us (6%)
  between operations  18 us (2%)
    reduce_scatter x1, waiting for transfers between devices, local(): lax.psum_scatter(output_acc, ('batch', 'head'), scatter_dimension=0, tile...  142 us
    reduce_scatter x4, waiting for transfers between devices, local(): lax.psum_scatter(jnp.einsum('cthe,hed->ctd', attended, proj_used, preferr...  87.5 us
    reduce_scatter x1, waiting for transfers between devices, local(): lax.psum_scatter(hidden_acc, ('batch', 'head'), scatter_dimension=0, tile...  86.1 us
    dot_general x4, matrix products, local(): hidden = jnp.dot(normed_two, first_full, preferred_element_type=jnp.float32)  60.2 us
    all_gather x4, waiting for transfers between devices, local(): arrived = lax.all_gather(grad_branch, 'head', axis=0, tiled=True)  60 us
    reduce_scatter x4, waiting for transfers between devices, local(): lax.psum_scatter(jnp.einsum('cthe,dhe->ctd', grad_packed, qkv_used, prefe...  57.6 us
    all_gather x4, waiting for transfers between devices, local(): operand_rows = lax.all_gather(normed_one, 'head', axis=0, tiled=True)  50.7 us
    unnamed x1, blocking collectives  39.5 us
  transfers between devices with their start and end apart: 21, of which 18 were waited for; matrix products, arithmetic and copies ran while one was open for 27% of the time, Pallas kernels for 0%

commit v1 on v0

v1 whole, which is shorter than its diff:
```python
import functools
import math

import jax
import jax.numpy as jnp
from jax import lax
from jax.experimental import pallas as pl
from jax.experimental.pallas import tpu as pltpu
from jax.sharding import PartitionSpec as P

HD = 96
WIDE = 128
FRAMES = 8
TPC = 392
PTOK = 196
SPOT = TPC // FRAMES
HALF = 200
ROWS = 2 * HALF
MAIN = 384
REST = TPC - MAIN
SIDE = 256
PAIR = 2
PIECES = 3 * PAIR

NORM_EPS = 1e-06
NEG = -1e30
LOG2E = 1.4426950408889634
SCORE = HD ** (-0.5)

F32 = jnp.float32
BF16 = jnp.bfloat16


def dot(a, b):
    return lax.dot_general(a, b, (((1,), (0,)), ((), ())), preferred_element_type=F32)


def dot_nt(a, b):
    return lax.dot_general(a, b, (((1,), (1,)), ((), ())), preferred_element_type=F32)


def dot_tn(a, b):
    return lax.dot_general(a, b, (((0,), (0,)), ((), ())), preferred_element_type=F32)


def reorder(shape, row_dim):
    rows = lax.broadcasted_iota(jnp.int32, shape, row_dim)
    tokens = lax.broadcasted_iota(jnp.int32, shape, 1 - row_dim)
    odd = (rows >= HALF).astype(jnp.int32)
    spot = rows - HALF * odd
    frame = sum((spot >= SPOT * step).astype(jnp.int32) for step in range(1, FRAMES // 2))
    return ((tokens == spot + SPOT * (frame + odd)) & (spot < PTOK)).astype(BF16)


def norm_parts(values):
    average = jnp.mean(values, axis=-1, keepdims=True)
    centered = values - average
    spread = lax.rsqrt(jnp.mean(centered * centered, axis=-1, keepdims=True) + NORM_EPS)
    return centered * spread, spread


def norm_pull(values, gain, grad):
    unit, spread = norm_parts(values)
    scaled = grad * gain
    inner = jnp.mean(scaled * unit, axis=-1, keepdims=True)
    pulled = spread * (scaled - jnp.mean(scaled, axis=-1, keepdims=True) - unit * inner)
    return pulled, jnp.sum(grad * unit, axis=0, keepdims=True)


def value_columns(memory_t):
    return jnp.concatenate([memory_t[HD:], jnp.zeros((WIDE - HD, memory_t.shape[1]), BF16)], axis=0)


def forward_kernel(
    x_ref, w_ref, mem_ref, tail_ref, side_ref, main_ref, taps_ref, proj_ref, gain_one_ref, gain_two_ref,
    packed_ref, keys_ref, att_ref, log_ref, normed_ref, middle_ref, normed_two_ref,
    x_rows, normed_rows, branch,
):
    pair, clip = pl.program_id(0), pl.program_id(1)
    here = pl.ds(clip, 1)

    @pl.when(pair == 0)
    def _():
        rows = dot(reorder((ROWS, TPC), 0), x_ref[0])
        x_rows[here] = rows.astype(BF16)[None]
        unit, _ = norm_parts(rows)
        normed_rows[here] = (unit * gain_one_ref[...]).astype(BF16)[None]

    normed = normed_rows[here][0]
    normed_ref[0] = normed
    packed = dot_nt(normed, w_ref[0])
    packed_ref[0, 0] = packed.astype(BF16)
    logs = []
    outs = []
    for head in range(PAIR):
        base = 3 * WIDE * head
        query = packed[:, base : base + WIDE]
        key = packed[:, base + WIDE : base + 2 * WIDE]
        value = packed[:, base + 2 * WIDE : base + 3 * WIDE]
        query_low = query.astype(BF16)
        taps = taps_ref[0, head]
        zeros = jnp.zeros((SIDE - HALF - REST, WIDE), F32)
        pooled_key = taps[0:1] * key[:HALF] + taps[1:2] * key[HALF:]
        pooled_value = taps[2:3] * value[:HALF] + taps[3:4] * value[HALF:]
        side_key = jnp.concatenate([pooled_key, tail_ref[0, head, 0], zeros], axis=0).astype(BF16)
        side_value = jnp.concatenate([pooled_value, tail_ref[0, head, 1], zeros], axis=0).astype(BF16)
        keys_ref[0, 0, head, 0] = side_key
        keys_ref[0, 0, head, 1] = side_value
        memory_t = mem_ref[0, head]
        score_side = dot_nt(query_low, side_key) * (SCORE * LOG2E) + side_ref[0]
        score_main = dot(query_low, memory_t[:WIDE]) * (SCORE * LOG2E) + main_ref[0]
        top = jnp.maximum(
            jnp.max(score_side, axis=-1, keepdims=True), jnp.max(score_main, axis=-1, keepdims=True)
        )
        weight_side = jnp.exp2(score_side - top)
        weight_main = jnp.exp2(score_main - top)
        total = jnp.sum(weight_side, axis=-1, keepdims=True) + jnp.sum(weight_main, axis=-1, keepdims=True)
        mixed = dot(weight_side.astype(BF16), side_value) + dot_nt(
            weight_main.astype(BF16), value_columns(memory_t)
        )
        outs.append(mixed / total + query)
        logs.append(top + jnp.log2(total))
    attended = jnp.concatenate(outs, axis=1).astype(BF16)
    att_ref[0, 0] = attended
    lane = lax.broadcasted_iota(jnp.int32, (ROWS, WIDE), 1)
    log_ref[0, 0] = jnp.where(lane == 0, logs[0], logs[1])
    part = dot(attended, proj_ref[0])[None]

    @pl.when(pair == 0)
    def _():
        branch[here] = part

    @pl.when(pair > 0)
    def _():
        branch[here] += part

    @pl.when(pair == pl.num_programs(0) - 1)
    def _():
        middle = x_rows[here][0].astype(F32) + branch[here][0]
        middle_ref[0] = middle
        unit, _ = norm_parts(middle)
        normed_two_ref[0] = (unit * gain_two_ref[...]).astype(BF16)


def mlp_kernel(
    normed_ref, cot_ref, first_ref, second_ref, middle_ref, gain_ref,
    out_ref, grad_ref, grad_low_ref, d_first_ref, d_second_ref, d_gain_ref,
    cot_rows, cot_t, normed_t, total, grad_normed, active, grad_hidden,
):
    tile = pl.program_id(0)
    clips = cot_ref.shape[0]
    wide = normed_ref.shape[1]

    @pl.when(tile == 0)
    def _():
        swap = reorder((ROWS, TPC), 0)

        @pl.loop(0, clips)
        def _(clip):
            here = pl.ds(pl.multiple_of(clip * ROWS, ROWS), ROWS)
            cot_rows[here, :] = dot(swap, cot_ref[clip]).astype(BF16)
            total[here, :] = middle_ref[here, :]
            grad_normed[here, :] = jnp.zeros((ROWS, wide), F32)

        for lanes in range(0, wide, WIDE):
            cot_t[lanes : lanes + WIDE, :] = cot_rows[:, lanes : lanes + WIDE].T
            normed_t[lanes : lanes + WIDE, :] = normed_ref[:, lanes : lanes + WIDE].T

    first = first_ref[...]
    second = second_ref[...]

    @pl.loop(0, clips)
    def _(clip):
        here = pl.ds(pl.multiple_of(clip * ROWS, ROWS), ROWS)
        hidden = dot(normed_ref[here, :], first)
        grad_active = dot_nt(cot_rows[here, :], second)
        bell = jnp.exp2(hidden * hidden * (-0.5 * LOG2E))
        step = 1.0 / (1.0 + (0.3275911 * math.sqrt(0.5)) * jnp.abs(hidden))
        tail = step * (0.5 * 1.061405429) + (0.5 * -1.453152027)
        tail = step * tail + (0.5 * 1.421413741)
        tail = step * tail + (0.5 * -0.284496736)
        tail = step * tail + (0.5 * 0.254829592)
        tail = step * tail * bell
        cumulative = jnp.where(hidden < 0.0, tail, 1.0 - tail)
        slope = cumulative + hidden * bell * 0.3989422804014327
        active_low = (hidden * cumulative).astype(BF16)
        hidden_low = (slope * grad_active).astype(BF16)
        active[here, :] = active_low
        grad_hidden[here, :] = hidden_low
        total[here, :] += dot(active_low, second)
        grad_normed[here, :] += dot_nt(hidden_low, first)

    d_first_ref[...] = dot(normed_t[...], grad_hidden[...]).astype(BF16)
    d_second_ref[...] = dot(cot_t[...], active[...]).astype(BF16).T

    @pl.when(tile == pl.num_programs(0) - 1)
    def _():
        back = reorder((TPC, ROWS), 1)
        d_gain_ref[...] = jnp.zeros_like(d_gain_ref)

        @pl.loop(0, clips)
        def _(clip):
            here = pl.ds(pl.multiple_of(clip * ROWS, ROWS), ROWS)
            out_ref[clip] = dot(back, total[here, :].astype(BF16)).astype(BF16)
            pulled, d_gain = norm_pull(middle_ref[here, :], gain_ref[...], grad_normed[here, :])
            grad = cot_rows[here, :].astype(F32) + pulled
            grad_ref[here, :] = grad
            grad_low_ref[here, :] = grad.astype(BF16)
            d_gain_ref[...] += d_gain


def backward_kernel(
    x_ref, w_ref, mem_ref, side_ref, main_ref, taps_ref, proj_ref, gain_ref,
    packed_ref, keys_ref, att_ref, log_ref, normed_ref, grad_ref, grad_low_ref,
    d_x_ref, d_w_ref, d_proj_ref, d_taps_ref, d_gain_ref,
    grad_normed,
):
    pair, clip = pl.program_id(0), pl.program_id(1)
    here = pl.ds(clip, 1)

    @pl.when(clip == 0)
    def _():
        d_w_ref[...] = jnp.zeros_like(d_w_ref)
        d_proj_ref[...] = jnp.zeros_like(d_proj_ref)
        d_taps_ref[...] = jnp.zeros_like(d_taps_ref)

    grad_branch = grad_low_ref[...]
    grad_out = dot_nt(grad_branch, proj_ref[0])
    d_proj_ref[0] += dot_tn(att_ref[0, 0], grad_branch)
    pieces = []
    for head in range(PAIR):
        base = 3 * WIDE * head
        query = packed_ref[0, 0, :, base : base + WIDE]
        key = packed_ref[0, 0, :, base + WIDE : base + 2 * WIDE].astype(F32)
        value = packed_ref[0, 0, :, base + 2 * WIDE : base + 3 * WIDE].astype(F32)
        out_grad = grad_out[:, WIDE * head : WIDE * (head + 1)].astype(BF16)
        taps = taps_ref[0, head]
        side_key = keys_ref[0, 0, head, 0]
        side_value = keys_ref[0, 0, head, 1]
        memory_t = mem_ref[0, head]
        log = log_ref[0, 0, :, head : head + 1]
        score_side = dot_nt(query, side_key) * (SCORE * LOG2E) + side_ref[0]
        score_main = dot(query, memory_t[:WIDE]) * (SCORE * LOG2E) + main_ref[0]
        weight_side = jnp.exp2(score_side - log)
        weight_main = jnp.exp2(score_main - log)
        grad_side = dot_nt(out_grad, side_value)
        grad_main = dot(out_grad, value_columns(memory_t))
        inner = jnp.sum(weight_side * grad_side, axis=-1, keepdims=True) + jnp.sum(
            weight_main * grad_main, axis=-1, keepdims=True
        )
        score_grad_side = (weight_side * (grad_side - inner)).astype(BF16)
        score_grad_main = (weight_main * (grad_main - inner)).astype(BF16)
        grad_query = (
            dot(score_grad_side, side_key) + dot_nt(score_grad_main, memory_t[:WIDE])
        ) * SCORE + out_grad.astype(F32)
        grad_key = dot_tn(score_grad_side, query)[:HALF] * SCORE
        grad_value = dot_tn(weight_side.astype(BF16), out_grad)[:HALF]
        pieces += [
            grad_query,
            jnp.concatenate([taps[0:1] * grad_key, taps[1:2] * grad_key], axis=0),
            jnp.concatenate([taps[2:3] * grad_value, taps[3:4] * grad_value], axis=0),
        ]
        d_taps_ref[0, head] += jnp.concatenate(
            [
                jnp.sum(part * grad, axis=0, keepdims=True)
                for part, grad in (
                    (key[:HALF], grad_key),
                    (key[HALF:], grad_key),
                    (value[:HALF], grad_value),
                    (value[HALF:], grad_value),
                )
            ],
            axis=0,
        )
    grad_packed = jnp.concatenate(pieces, axis=1).astype(BF16)
    d_w_ref[0] += dot_tn(grad_packed, normed_ref[0])
    part = dot(grad_packed, w_ref[0])[None]

    @pl.when(pair == 0)
    def _():
        grad_normed[here] = part

    @pl.when(pair > 0)
    def _():
        grad_normed[here] += part

    @pl.when(pair == pl.num_programs(0) - 1)
    def _():
        rows = dot(reorder((ROWS, TPC), 0), x_ref[0])
        pulled, d_gain = norm_pull(rows, gain_ref[...], grad_normed[here][0])
        d_x = (grad_ref[...] + pulled).astype(BF16)
        d_x_ref[0] = dot(reorder((TPC, ROWS), 1), d_x).astype(BF16)

        @pl.when(clip == 0)
        def _():
            d_gain_ref[...] = d_gain

        @pl.when(clip > 0)
        def _():
            d_gain_ref[...] += d_gain


VMEM_LIMIT = 60 << 20


def compiler_params(dims):
    return pltpu.CompilerParams(
        dimension_semantics=("arbitrary",) * dims, vmem_limit_bytes=VMEM_LIMIT
    )


def shaped(shape, dtype):
    return jax.ShapeDtypeStruct(shape, dtype)


def attention_forward(x, w, mem, tail, side, main, taps, proj, gain_one, gain_two):
    clips, pairs = x.shape[0], w.shape[0]
    width = x.shape[2]
    packed_width = w.shape[1]
    late = lambda p, c: jnp.where(p == pairs - 1, c, 0)
    early = lambda p, c: jnp.where(p == 0, c, clips - 1)
    per_step = lambda p, c: (p, c)
    return pl.pallas_call(
        forward_kernel,
        grid=(pairs, clips),
        in_specs=[
            pl.BlockSpec((1, TPC, width), lambda p, c: (early(p, c), 0, 0)),
            pl.BlockSpec((1, packed_width, width), lambda p, c: (p, 0, 0)),
            pl.BlockSpec((1, PAIR, 2 * HD, MAIN), lambda p, c: (c, p, 0, 0)),
            pl.BlockSpec((1, PAIR, 2, REST, WIDE), lambda p, c: (c, p, 0, 0, 0)),
            pl.BlockSpec((1, 1, SIDE), lambda p, c: (c, 0, 0)),
            pl.BlockSpec((1, 1, MAIN), lambda p, c: (c, 0, 0)),
            pl.BlockSpec((1, PAIR, 4, WIDE), lambda p, c: (p, 0, 0, 0)),
            pl.BlockSpec((1, PAIR * WIDE, width), lambda p, c: (p, 0, 0)),
            pl.BlockSpec((1, width), lambda p, c: (0, 0)),
            pl.BlockSpec((1, width), lambda p, c: (0, 0)),
        ],
        out_specs=[
            pl.BlockSpec((1, 1, ROWS, packed_width), lambda p, c: (p, c, 0, 0)),
            pl.BlockSpec((1, 1, PAIR, 2, SIDE, WIDE), lambda p, c: (p, c, 0, 0, 0, 0)),
            pl.BlockSpec((1, 1, ROWS, PAIR * WIDE), lambda p, c: (p, c, 0, 0)),
            pl.BlockSpec((1, 1, ROWS, WIDE), lambda p, c: (p, c, 0, 0)),
            pl.BlockSpec((1, ROWS, width), lambda p, c: (c, 0, 0)),
            pl.BlockSpec((1, ROWS, width), lambda p, c: (late(p, c), 0, 0)),
            pl.BlockSpec((1, ROWS, width), lambda p, c: (late(p, c), 0, 0)),
        ],
        out_shape=[
            shaped((pairs, clips, ROWS, packed_width), BF16),
            shaped((pairs, clips, PAIR, 2, SIDE, WIDE), BF16),
            shaped((pairs, clips, ROWS, PAIR * WIDE), BF16),
            shaped((pairs, clips, ROWS, WIDE), F32),
            shaped((clips, ROWS, width), BF16),
            shaped((clips, ROWS, width), F32),
            shaped((clips, ROWS, width), BF16),
        ],
        scratch_shapes=[
            pltpu.VMEM((clips, ROWS, width), BF16),
            pltpu.VMEM((clips, ROWS, width), BF16),
            pltpu.VMEM((clips, ROWS, width), F32),
        ],
        compiler_params=compiler_params(2),
        name="attention_forward",
    )(x, w, mem, tail, side, main, taps, proj, gain_one, gain_two)


def once(shape):
    return pl.BlockSpec(shape, lambda t: (0,) * len(shape), pipeline_mode=pl.Buffered(1))


def mlp(normed, cot, first, second, middle, gain):
    rows, width = normed.shape
    hidden = first.shape[1]
    clips = cot.shape[0]
    tile = 512
    return pl.pallas_call(
        mlp_kernel,
        grid=(hidden // tile,),
        in_specs=[
            once((rows, width)),
            once((clips, TPC, width)),
            pl.BlockSpec((width, tile), lambda t: (0, t)),
            pl.BlockSpec((tile, width), lambda t: (t, 0)),
            once((rows, width)),
            once((1, width)),
        ],
        out_specs=[
            once((clips, TPC, width)),
            once((rows, width)),
            once((rows, width)),
            pl.BlockSpec((width, tile), lambda t: (0, t)),
            pl.BlockSpec((tile, width), lambda t: (t, 0)),
            once((1, width)),
        ],
        out_shape=[
            shaped((clips, TPC, width), BF16),
            shaped((rows, width), F32),
            shaped((rows, width), BF16),
            shaped((width, hidden), BF16),
            shaped((hidden, width), BF16),
            shaped((1, width), F32),
        ],
        scratch_shapes=[
            pltpu.VMEM((rows, width), BF16),
            pltpu.VMEM((width, rows), BF16),
            pltpu.VMEM((width, rows), BF16),
            pltpu.VMEM((rows, width), F32),
            pltpu.VMEM((rows, width), F32),
            pltpu.VMEM((rows, tile), BF16),
            pltpu.VMEM((rows, tile), BF16),
        ],
        compiler_params=compiler_params(1),
        name="mlp",
    )(normed, cot, first, second, middle, gain)


def attention_backward(x, w, mem, side, main, taps, proj, gain, packed, keys, att, log, normed, grad, grad_low):
    clips, pairs = x.shape[0], w.shape[0]
    width = x.shape[2]
    packed_width = w.shape[1]
    late = lambda p, c: jnp.where(p == pairs - 1, c, 0)
    return pl.pallas_call(
        backward_kernel,
        grid=(pairs, clips),
        in_specs=[
            pl.BlockSpec((1, TPC, width), lambda p, c: (late(p, c), 0, 0)),
            pl.BlockSpec((1, packed_width, width), lambda p, c: (p, 0, 0)),
            pl.BlockSpec((1, PAIR, 2 * HD, MAIN), lambda p, c: (c, p, 0, 0)),
            pl.BlockSpec((1, 1, SIDE), lambda p, c: (c, 0, 0)),
            pl.BlockSpec((1, 1, MAIN), lambda p, c: (c, 0, 0)),
            pl.BlockSpec((1, PAIR, 4, WIDE), lambda p, c: (p, 0, 0, 0)),
            pl.BlockSpec((1, PAIR * WIDE, width), lambda p, c: (p, 0, 0)),
            pl.BlockSpec((1, width), lambda p, c: (0, 0)),
            pl.BlockSpec((1, 1, ROWS, packed_width), lambda p, c: (p, c, 0, 0)),
            pl.BlockSpec((1, 1, PAIR, 2, SIDE, WIDE), lambda p, c: (p, c, 0, 0, 0, 0)),
            pl.BlockSpec((1, 1, ROWS, PAIR * WIDE), lambda p, c: (p, c, 0, 0)),
            pl.BlockSpec((1, 1, ROWS, WIDE), lambda p, c: (p, c, 0, 0)),
            pl.BlockSpec((1, ROWS, width), lambda p, c: (c, 0, 0)),
            pl.BlockSpec((ROWS, width), lambda p, c: (late(p, c), 0)),
            pl.BlockSpec((ROWS, width), lambda p, c: (c, 0)),
        ],
        out_specs=[
            pl.BlockSpec((1, TPC, width), lambda p, c: (late(p, c), 0, 0)),
            pl.BlockSpec((1, packed_width, width), lambda p, c: (p, 0, 0)),
            pl.BlockSpec((1, PAIR * WIDE, width), lambda p, c: (p, 0, 0)),
            pl.BlockSpec((1, PAIR, 4, WIDE), lambda p, c: (p, 0, 0, 0)),
            pl.BlockSpec((1, width), lambda p, c: (0, 0)),
        ],
        out_shape=[
            shaped((clips, TPC, width), BF16),
            shaped((pairs, packed_width, width), F32),
            shaped((pairs, PAIR * WIDE, width), F32),
            shaped((pairs, PAIR, 4, WIDE), F32),
            shaped((1, width), F32),
        ],
        scratch_shapes=[pltpu.VMEM((clips, ROWS, width), F32)],
        compiler_params=compiler_params(2),
        name="attention_backward",
    )(x, w, mem, side, main, taps, proj, gain, packed, keys, att, log, normed, grad, grad_low)


def group_gather(own, heads, fetch=None):
    blocks = [fetch(own, 0) if fetch else own]
    for shift in range(1, heads):
        sent = fetch(own, -shift) if fetch else own
        blocks.append(lax.ppermute(sent, "head", [(src, (src - shift) % heads) for src in range(heads)]))
    return blocks


def group_sum(blocks, heads):
    total = blocks[0]
    for shift in range(1, heads):
        total = total + lax.ppermute(
            blocks[shift].astype(BF16), "head", [(src, (src + shift) % heads) for src in range(heads)]
        ).astype(F32)
    return total


def local(
    heads,
    inputs,
    qkv_weight,
    proj_weight,
    pool_weight,
    gain_one,
    gain_two,
    hidden_weight,
    output_weight,
    memory,
    clip_index,
    cotangent,
):
    width = inputs.shape[3]
    micro, own_clips = inputs.shape[:2]
    clips = micro * own_clips
    own_heads = qkv_weight.shape[1]
    all_heads = own_heads * heads
    pairs = all_heads // PAIR
    me = lax.axis_index("head")

    def mine(array, shift):
        start = lax.rem(me + shift + heads, heads) * own_clips
        return lax.dynamic_slice_in_dim(array, start, own_clips, axis=1)

    w_own = qkv_weight.transpose(1, 2, 0)
    w_all = jnp.concatenate(group_gather(w_own, heads), axis=0)
    proj_all = jnp.concatenate(group_gather(proj_weight, heads), axis=0)
    taps_all = jnp.concatenate(group_gather(pool_weight, heads), axis=0)
    memory_t = memory.transpose(0, 1, 3, 4, 2)
    mem_all = jnp.concatenate(group_gather(memory_t, heads, mine), axis=2)
    mem_all = mem_all.reshape(clips, all_heads, 2 * HD, TPC)

    first = lax.all_gather(hidden_weight, ("batch", "head"), axis=0, tiled=True)
    second = lax.all_gather(output_weight, ("batch", "head"), axis=0, tiled=True)

    pad = WIDE - HD
    w_all = jnp.pad(w_all.reshape(all_heads, 3, HD, width), ((0, 0), (0, 0), (0, pad), (0, 0)))
    w_all = w_all.reshape(pairs, PIECES * WIDE, width)
    proj_all = jnp.pad(proj_all, ((0, 0), (0, pad), (0, 0))).reshape(pairs, PAIR * WIDE, width)
    taps_all = jnp.pad(taps_all.astype(F32), ((0, 0), (0, 0), (0, pad))).reshape(pairs, PAIR, 4, WIDE)
    tail = mem_all[..., MAIN:].reshape(clips, all_heads, 2, HD, REST).swapaxes(3, 4)
    tail = jnp.pad(tail.astype(F32), ((0, 0),) * 4 + ((0, pad),))

    index = mine(clip_index, 0).reshape(clips, 1, 1)
    main_slot = lax.broadcasted_iota(jnp.int32, (1, 1, MAIN), 2) // PTOK
    main_mask = jnp.where(index > main_slot, 0.0, NEG).astype(F32)
    spot = lax.broadcasted_iota(jnp.int32, (1, 1, SIDE), 2)
    tail_open = (spot >= HALF) & (spot < HALF + REST) & (index > (TPC - 1) // PTOK)
    side_mask = jnp.where((spot < PTOK) | tail_open, 0.0, NEG).astype(F32)

    x = inputs.reshape(clips, TPC, width)
    gain_one = gain_one.reshape(1, width)
    gain_two = gain_two.reshape(1, width)
    packed, keys, att, log, normed, middle, normed_two = attention_forward(
        x, w_all, mem_all, tail, side_mask, main_mask, taps_all, proj_all, gain_one, gain_two
    )
    outputs, grad, grad_low, d_first, d_second, d_gain_two = mlp(
        normed_two.reshape(clips * ROWS, width),
        cotangent.reshape(clips, TPC, width),
        first,
        second,
        middle.reshape(clips * ROWS, width),
        gain_two,
    )
    d_x, d_w, d_proj, d_taps, d_gain_one = attention_backward(
        x, w_all, mem_all, side_mask, main_mask, taps_all, proj_all, gain_one,
        packed, keys, att, log, normed, grad, grad_low,
    )
    d_w = d_w.reshape(heads, own_heads, 3, WIDE, width)[:, :, :, :HD].reshape(heads, own_heads, 3 * HD, width)
    d_proj = d_proj.reshape(heads, own_heads, WIDE, width)[:, :, :HD]
    d_taps = d_taps.reshape(heads, own_heads, 4, WIDE)[..., :HD]
    d_w, d_proj, d_taps = (
        lax.psum(group_sum(list(grads), heads).astype(BF16), "batch").astype(F32)
        for grads in (d_w, d_proj, d_taps)
    )
    both = ("batch", "head")
    d_first = lax.psum_scatter(d_first, both, scatter_dimension=0, tiled=True).astype(F32)
    d_second = lax.psum_scatter(d_second, both, scatter_dimension=0, tiled=True).astype(F32)
    d_gains = lax.psum_scatter(
        jnp.concatenate([d_gain_one, d_gain_two], axis=0), both, scatter_dimension=1, tiled=True
    )
    return (
        outputs.reshape(inputs.shape),
        d_x.reshape(inputs.shape),
        d_w.transpose(2, 0, 1),
        d_proj,
        d_taps,
        d_gains[0],
        d_gains[1],
        d_first,
        d_second,
    )


def solution(mesh):
    return jax.shard_map(
        functools.partial(local, mesh.shape["head"]),
        mesh=mesh,
        in_specs=(
            P(None, ("batch", "head"), None, None),
            P(None, "head", None),
            P("head", None, None),
            P("head", None, None),
            P(),
            P(),
            P(("batch", "head"), None),
            P(("batch", "head"), None),
            P(None, "batch", None, "head", None),
            P(None, "batch"),
            P(None, ("batch", "head"), None, None),
        ),
        out_specs=(
            P(None, ("batch", "head"), None, None),
            P(None, ("batch", "head"), None, None),
            P(None, "head", None),
            P("head", None, None),
            P("head", None, None),
            P(("batch", "head")),
            P(("batch", "head")),
            P(("batch", "head"), None),
            P(("batch", "head"), None),
        ),
        check_vma=False,
    )
```

time: 1200 us -> 760 us (0.63); the launches traced: 1190 us -> 759 us
  matrix products: 340 us -> 0 us
  Pallas kernels: 0 us -> 197 us
  local copies, waits for them, and re-layouts: 158 us -> 16.5 us
  other arithmetic: 101 us -> 16.1 us
  waiting for transfers between devices: 494 us -> 434 us
    dot_general x72 -> x0, matrix products: 340 us -> none  [the longest x4 60.2 us: local(): hidden = jnp.dot(normed_two, first_full, preferred_element_type=jnp.float32)]
    pallas_call x0 -> x3, Pallas kernels: none -> 197 us  [the longest x1 81 us: mlp(): pl.pallas_call(mlp_kernel, grid=(hidden // tile,), in_specs=[once((rows,...]
    ppermute x0 -> x7, waiting for transfers between devices: none -> 189 us  [the longest x4 141 us: group_gather(): lax.ppermute(sent, 'head', [(src, (src - shift) % heads) for src in range...]
    reduce_scatter x10 -> x2, waiting for transfers between devices: 373 us -> 218 us  [the longest x1 111 us: local(): lax.psum_scatter(d_second, both, scatter_dimension=0, tiled=True)]
    all_gather x10 -> x2, waiting for transfers between devices: 118 us -> 0.04 us  [the longest x1 0.02 us: local(): first = lax.all_gather(hidden_weight, ('batch', 'head'), axis=0, tiled=True)]
    slice x26 -> x1, local copies, waits for them, and re-layouts: 58 us -> 0.29 us  [local(): mem_all[..., MAIN:].reshape(clips, all_heads, 2, HD, REST).swapaxes(3, 4)]
    squeeze x17 -> x1, local copies, waits for them, and re-layouts: 41.9 us -> 0.52 us  [local(): d_gains[1]]
    reduce_sum x13 -> x0, other arithmetic: 38.6 us -> none  [the longest x4 19.8 us: attend_forward(): jnp.sum(jnp.exp(scores - maxima), axis=-1, keepdims=True)]
  transfers between devices with their start and end apart: 21 -> 12, of which waited for: 18 -> 5; matrix products, arithmetic and copies ran while one was open for 27% -> 3% of each run, Pallas kernels for 0% -> 6%
where the time goes in v1:
time: 760 us; the launch traced here: 759 us
  waiting for transfers between devices  434 us (57%)
  Pallas kernels  197 us (26%)
  blocking collectives  72.2 us (10%)
  local copies, waits for them, and re-layouts  16.5 us (2%)
  other arithmetic  16.1 us (2%)
  between operations  14 us (2%)
  starting transfers between devices  9.13 us (1%)
    ppermute x4, waiting for transfers between devices, group_gather(): lax.ppermute(sent, 'head', [(src, (src - shift) % heads) for src in range...  141 us
    reduce_scatter x1, waiting for transfers between devices, local(): lax.psum_scatter(d_second, both, scatter_dimension=0, tiled=True)  111 us
    reduce_scatter x1, waiting for transfers between devices, local(): lax.psum_scatter(d_first, both, scatter_dimension=0, tiled=True).astype(F32)  107 us
    pallas_call x1, Pallas kernels, mlp(): pl.pallas_call(mlp_kernel, grid=(hidden // tile,), in_specs=[once((rows,...  81 us
    pallas_call x1, Pallas kernels, attention_backward(): pl.pallas_call(backward_kernel, grid=(pairs, clips), in_specs=[pl.BlockSp...  71 us
    ppermute x3, waiting for transfers between devices, group_sum(): lax.ppermute(blocks[shift].astype(BF16), 'head', [(src, (src + shift) % h...  47.9 us
    pallas_call x1, Pallas kernels, attention_forward(): pl.pallas_call(forward_kernel, grid=(pairs, clips), in_specs=[pl.BlockSpe...  45.1 us
    unnamed x1, blocking collectives  39.9 us
  transfers between devices with their start and end apart: 12, of which 5 were waited for; matrix products, arithmetic and copies ran while one was open for 3% of the time, Pallas kernels for 6%

profile of v1, /device:TPU:0, one launch (start us, length us, event | category | flops | bytes accessed | tf_op | source)
XLA Modules:
  0.0 759.4 jit_solution(4930992175957670401)
XLA Ops:
  7.2 0.7 all-gather.3.cloned.1.call-update
  8.0 0.7 all-gather.5.cloned.1.call-update
  8.8 3.6 dynamic-slice_bitcast_fusion.1
  12.4 3.0 collective-permute-start.1
  15.5 1.9 collective-permute-start.3
  17.6 0.7 compare_select_fusion.main_ref
  18.2 0.7 or_select_fusion.side_ref
  20.1 141.5 %collective-permute-done.2 = bf16[4,4,96]{2,1,0:T(4,128)(2,1)S(1)} collective-permute-done((bf16[4,4,96]{2,1,0:T(4,128)(2,1)S(1)}, bf16[4,4,96]{2,1,0:T(4,128)(2,1)S(1)}, u32[]{:S(2)}, u32[]{:S(2)}) %collective-permute-start.2) | collective-permute-done | bytes 3104 | tf_op jit(solution)/shard_map/ppermute | solution.py:465
  162.1 1.3 fusion.3
  163.7 2.6 pad.19
  167.0 2.6 copy-done
  170.0 0.8 copy.27
  170.8 0.7 pad_convert_fusion.tail_ref
  171.5 45.1 %attention_forward.1 = (bf16[4,4,400,768]{3,2,1,0:T(8,128)(2,1)}, bf16[4,4,2,2,256,128]{5,4,3,2,1,0:T(8,128)(2,1)}, bf16[4,4,400,256]{3,2,1,0:T(8,128)(2,1)}, f3...) custom-call(bf16[4,392,768]{2,1,0:T(8,128)(2,1)} %bitcast.66, ...), custom_call_target="tpu_custom_call" | custom-call | tf_op jit(solution)/shard_map/attention_forward/pallas_call | solution.py:323
  216.7 81.0 %mlp.1 = (bf16[4,392,768]{2,1,0:T(8,128)(2,1)}, f32[1600,768]{1,0:T(8,128)}, bf16[1600,768]{1,0:T(8,128)(2,1)}, bf16[768,3072]{1,0:T(8,128)(2,1)}, bf16[3072,768]{1,0:T(8,128)(2,1)}, /*index=5*/f32[1,768]{1,0:T(1,128)}) custom-call(bf16[1600,768]{1,0:T(8,128)(2,1)} %bitcast.72, bf16[4,392,768]{2,1,0:T(8,128)(2,1)} %bitcast.73, ...), custom_call_target="tpu_custom_call" | custom-call | tf_op jit(solution)/shard_map/mlp/pallas_call | solution.py:375
  297.7 71.0 %attention_backward.1 = (bf16[4,392,768]{2,1,0:T(8,128)(2,1)}, f32[4,768,768]{2,1,0:T(8,128)}, f32[4,256,768]{2,1,0:T(8,128)}, f32[4,2,4,128]{3,2,1,0:T(4,128)}, f32[1,768]{1,0:T(1,128)}) custom-call(bf16[4,392,768]{2,1,0:T(8,128)(2,1)} %bitcast.67, bf16[4,768,768]{2,1,0:T(8,128)(2,1)} %bitcast.61, bf16[4,8,192,392]{3,2,1,0:T(8,128)(2,1)} %copy-done, ...), custom_call_target="tpu_custom_call" | custom-call | tf_op jit(solution)/shard_map/attention_backward/pallas_call | solution.py:421
  368.7 2.4 unstack.64
  371.0 1.8 collective-permute-start.4
  373.5 2.2 unstack.41
  375.7 47.9 %collective-permute-done.5 = bf16[4,96,768]{2,1,0:T(8,128)(2,1)S(1)} collective-permute-done((bf16[4,96,768]{2,1,0:T(8,128)(2,1)S(1)}, bf16[4,96,768]{2,1,0:T(8,128)(2,1)S(1)}, u32[]{:S(2)}, u32[]{:S(2)}) %collective-permute-start.5) | collective-permute-done | bytes 589856 | tf_op jit(solution)/shard_map/ppermute | solution.py:472
  423.6 1.0 fusion.5
  424.6 1.6 fusion.2
  427.5 1.4 collective-permute-start.6
  429.0 39.9 %all-reduce.4 = f32[2,768]{1,0:T(2,128)S(1)} all-reduce(f32[2,768]{1,0:T(2,128)S(1)} %pad_maximum_fusion.1), channel_id=2, replica_groups=mesh['batch'=16,'head'=2] {'batch','head'}, use_global_device_ids=true, to_apply=%region_3.4.clone | all-reduce | flops 1536 | bytes 12288
  469.4 32.3 %psum.23 = bf16[4,4,96]{2,1,0:T(4,128)(2,1)S(1)} all-reduce(bf16[4,4,96]{2,1,0:T(4,128)(2,1)S(1)} %fusion.11), channel_id=1, replica_groups=mesh['batch'=16,'head'=2] {'batch'}, use_global_device_ids=true, to_apply=%region_2.3 | all-reduce | flops 1536 | bytes 6144 | tf_op jit(solution)/shard_map/psum | solution.py:552
  502.3 24.8 %all-reduce.8.cloned.1.call-done = (bf16[768,4,288]{0,2,1:T(8,128)(2,1)}, bf16[4,96,768]{2,1,0:T(8,128)(2,1)}) async-done(((bf16[768,4,288]{0,2,1:T(8,128)(2,1)}, bf16[4,96,768]{2,1,0:T(8,128)(2,1)}), (bf16[768,4,288]{0,2,1:T(8,128)(2,1)}, bf16[4,96,768]{2,1,0:T(8,128)(2,1)})) %all-reduce.8.cloned.1.call-update) | async-done | bytes 2359312 | tf_op jit(solution)/shard_map/psum | solution.py:552
  527.1 3.6 transpose.26
  530.8 1.1 convert_element_type.67
  531.9 107.0 %reduce-scatter.4.cloned.1.call-done = bf16[24,3072]{1,0:T(8,128)(2,1)} async-done(((bf16[768,3072]{1,0:T(8,128)(2,1)}), bf16[24,3072]{1,0:T(8,128)(2,1)}) %reduce-scatter.4.cloned.1.call-update) | async-done | bytes 147472 | tf_op jit(solution)/shard_map/reduce_scatter | solution.py:556
  638.9 1.6 convert_element_type.72
  640.5 110.7 %reduce-scatter.6.cloned.1.call-done = bf16[96,768]{1,0:T(8,128)(2,1)} async-done(((bf16[3072,768]{1,0:T(8,128)(2,1)}), bf16[96,768]{1,0:T(8,128)(2,1)}) %reduce-scatter.6.cloned.1.call-update) | async-done | bytes 147472 | tf_op jit(solution)/shard_map/reduce_scatter | solution.py:557
  751.2 1.6 convert_element_type.73
  (58 shorter events, 6.5 us)
Async XLA Ops:
  7.2 209.5 %all-gather.3.cloned.1.call-start = ((), (), s32[]{:S(2)}) async-start(), calls=%async_computation.2 | async-start | bytes 4866048 | tf_op jit(solution)/shard_map/all_gather | solution.py:512
  7.9 208.8 %all-gather.5.cloned.1.call-start = ((), (), s32[]{:S(2)}) async-start(), calls=%async_computation.3 | async-start | bytes 4866048 | tf_op jit(solution)/shard_map/all_gather | solution.py:513
  8.7 518.5 %all-reduce.8.cloned.1.call-start = ((), (), s32[]{:S(2)}) async-start(), calls=%async_computation.6 | async-start | bytes 4718592 | tf_op jit(solution)/shard_map/psum | solution.py:552
  8.7 6.7 copy-start.1
  8.7 6.7 copy-start.4
  8.7 8.7 %copy-start.8 = (bf16[4,4,96]{2,1,0:T(4,128)(2,1)S(1)}, bf16[4,4,96]{2,1,0:T(4,128)(2,1)}, u32[]{:S(2)}) copy-start(bf16[4,4,96]{2,1,0:T(4,128)(2,1)} %param.14) | copy-start | bytes 9220
  8.8 8.8 %copy-start.11 = (s32[4,2]{0,1:T(2,128)S(1)}, s32[4,2]{0,1:T(2,128)}, u32[]{:S(2)}) copy-start(s32[4,2]{0,1:T(2,128)} %param.20) | copy-start | bytes 100
  8.8 10.1 %copy-start.6 = (f32[768]{0:T(1024)S(1)}, f32[768]{0:T(1024)}, u32[]{:S(2)}) copy-start(f32[768]{0:T(1024)} %param.15) | copy-start | bytes 9220
  8.8 10.7 %copy-start.7 = (f32[768]{0:T(1024)S(1)}, f32[768]{0:T(1024)}, u32[]{:S(2)}) copy-start(f32[768]{0:T(1024)} %param.16) | copy-start | bytes 9220
  12.4 154.0 %collective-permute-start.1 = (bf16[4,1,4,192,392]{4,3,2,0,1:T(8,128)(2,1)S(1)}, bf16[4,1,4,192,392]{4,3,2,0,1:T(8,128)(2,1)S(1)}, u32[]{:S(2)}, u32[]{:S(2)}) collective-permute-start(bf16[4,1,4,192,392]{4,3,2,0,1:T(8,128)(2,1)S(1)} %get-tuple-element.68), channel_id=1, source_target_pairs={{0,1},{1,0},{2,3},{3,2},{4,5},{5,4},{6,7},{7,6},{8,9},{9,8},{10,11... | collective-permute-start | bytes 7225352 | tf_op jit(solution)/shard_map/ppermute | solution.py:465
  15.4 148.0 %collective-permute-start = (bf16[4,288,768]{2,1,0:T(8,128)(2,1)S(1)}, bf16[4,288,768]{2,1,0:T(8,128)(2,1)S(1)}, u32[]{:S(2)}, u32[]{:S(2)}) collective-permute-start(bf16[4,288,768]{2,1,0:T(8,128)(2,1)S(1)} %bitcast.74), channel_id=1, source_target_pairs={{0,1},{1,0},{2,3},{3,2},{4,5},{5,4},{6,7},{7,6},{8,9},{9,8},{10,11... | collective-permute-start | bytes 5308424 | tf_op jit(solution)/shard_map/ppermute | solution.py:465
  15.5 146.7 %collective-permute-start.3 = (bf16[4,96,768]{2,1,0:T(8,128)(2,1)S(1)}, bf16[4,96,768]{2,1,0:T(8,128)(2,1)S(1)}, u32[]{:S(2)}, u32[]{:S(2)}) collective-permute-start(bf16[4,96,768]{2,1,0:T(8,128)(2,1)S(1)} %copy-done.4), channel_id=1, source_target_pairs={{0,1},{1,0},{2,3},{3,2},{4,5},{5,4},{6,7},{7,6},{8,9},{9,8},{10,11... | collective-permute-start | bytes 1769480 | tf_op jit(solution)/shard_map/ppermute | solution.py:465
  17.4 144.1 %collective-permute-start.2 = (bf16[4,4,96]{2,1,0:T(4,128)(2,1)S(1)}, bf16[4,4,96]{2,1,0:T(4,128)(2,1)S(1)}, u32[]{:S(2)}, u32[]{:S(2)}) collective-permute-start(bf16[4,4,96]{2,1,0:T(4,128)(2,1)S(1)} %copy-done.8), channel_id=1, source_target_pairs={{0,1},{1,0},{2,3},{3,2},{4,5},{5,4},{6,7},{7,6},{8,9},{9,8},{10,11... | collective-permute-start | bytes 9224 | tf_op jit(solution)/shard_map/ppermute | solution.py:465
  167.0 2.7 copy-start
  368.6 4.2 copy-start.2
  371.0 53.6 %collective-permute-start.4 = (bf16[4,288,768]{2,1,0:T(8,128)(2,1)S(1)}, bf16[4,288,768]{2,1,0:T(8,128)(2,1)S(1)}, u32[]{:S(2)}, u32[]{:S(2)}) collective-permute-start(bf16[4,288,768]{2,1,0:T(8,128)(2,1)S(1)} %bitcast.76), channel_id=1, source_target_pairs={{0,1},{1,0},{2,3},{3,2},{4,5},{5,4},{6,7},{7,6},{8,9},{9,8},{10,11... | collective-permute-start | bytes 5308424 | tf_op jit(solution)/shard_map/ppermute | solution.py:472
  372.9 50.7 %collective-permute-start.5 = (bf16[4,96,768]{2,1,0:T(8,128)(2,1)S(1)}, bf16[4,96,768]{2,1,0:T(8,128)(2,1)S(1)}, u32[]{:S(2)}, u32[]{:S(2)}) collective-permute-start(bf16[4,96,768]{2,1,0:T(8,128)(2,1)S(1)} %fusion.6), channel_id=1, source_target_pairs={{0,1},{1,0},{2,3},{3,2},{4,5},{5,4},{6,7},{7,6},{8,9},{9,8},{10,11... | collective-permute-start | bytes 1769480 | tf_op jit(solution)/shard_map/ppermute | solution.py:472
  426.2 212.6 %reduce-scatter.4.cloned.1.call-start = ((), (), s32[]{:S(2)}) async-start(), calls=%async_computation.4 | async-start | bytes 4866048 | tf_op jit(solution)/shard_map/reduce_scatter | solution.py:556
  426.8 0.7 copy-start.5
  426.8 2.1 copy-start.9
  426.8 2.1 copy-start.10
  426.8 324.4 %reduce-scatter.6.cloned.1.call-start = ((), (), s32[]{:S(2)}) async-start(), calls=%async_computation.5 | async-start | bytes 4866048 | tf_op jit(solution)/shard_map/reduce_scatter | solution.py:557
  427.5 41.9 %collective-permute-start.6 = (bf16[4,4,96]{2,1,0:T(4,128)(2,1)S(1)}, bf16[4,4,96]{2,1,0:T(4,128)(2,1)S(1)}, u32[]{:S(2)}, u32[]{:S(2)}) collective-permute-start(bf16[4,4,96]{2,1,0:T(4,128)(2,1)S(1)} %fusion.12), channel_id=1, source_target_pairs={{0,1},{1,0},{2,3},{3,2},{4,5},{5,4},{6,7},{7,6},{8,9},{9,8},{10,11... | collective-permute-start | bytes 9224 | tf_op jit(solution)/shard_map/ppermute | solution.py:472
  527.1 3.6 copy-start.3
Sparse Core Ops, SparseCore 0:
  10.9 77.8 all-gather.2
  91.8 74.0 all-gather.4
  426.3 100.7 all-reduce.7
  532.5 106.3 reduce-scatter.3
  645.1 106.1 reduce-scatter.5

commit v2 on v1

--- a/solution.py
+++ b/solution.py
@@ -72,11 +72,26 @@
 
 
 def forward_kernel(
-    x_ref, w_ref, mem_ref, tail_ref, side_ref, main_ref, taps_ref, proj_ref, gain_one_ref, gain_two_ref,
+    x_ref, w_ref, mem_ref, tail_ref, side_ref, main_ref, taps_ref, gain_one_ref, gain_two_ref,
     packed_ref, keys_ref, att_ref, log_ref, normed_ref, middle_ref, normed_two_ref,
     x_rows, normed_rows, branch,
 ):
-    pair, clip = pl.program_id(0), pl.program_id(1)
+    forward_step(
+        pl.program_id(0), pl.program_id(1), pl.num_programs(0),
+        w_ref.at[0], mem_ref.at[0], tail_ref.at[0], taps_ref.at[0],
+        x_ref, side_ref, main_ref, gain_one_ref, gain_two_ref,
+        packed_ref, keys_ref, att_ref, log_ref, normed_ref, middle_ref, normed_two_ref,
+        x_rows, normed_rows, branch,
+    )
+
+
+def forward_step(
+    pair, clip, pairs,
+    w_ref, mem_ref, tail_ref, taps_ref,
+    x_ref, side_ref, main_ref, gain_one_ref, gain_two_ref,
+    packed_ref, keys_ref, att_ref, log_ref, normed_ref, middle_ref, normed_two_ref,
+    x_rows, normed_rows, branch,
+):
     here = pl.ds(clip, 1)
 
     @pl.when(pair == 0)
@@ -84,11 +99,12 @@
         rows = dot(reorder((ROWS, TPC), 0), x_ref[0])
         x_rows[here] = rows.astype(BF16)[None]
         unit, _ = norm_parts(rows)
-        normed_rows[here] = (unit * gain_one_ref[...]).astype(BF16)[None]
+        low = (unit * gain_one_ref[...]).astype(BF16)
+        normed_rows[here] = low[None]
+        normed_ref[0] = low
 
     normed = normed_rows[here][0]
-    normed_ref[0] = normed
-    packed = dot_nt(normed, w_ref[0])
+    packed = dot_nt(normed, w_ref[: PIECES * WIDE])
     packed_ref[0, 0] = packed.astype(BF16)
     logs = []
     outs = []
@@ -98,15 +114,16 @@
         key = packed[:, base + WIDE : base + 2 * WIDE]
         value = packed[:, base + 2 * WIDE : base + 3 * WIDE]
         query_low = query.astype(BF16)
-        taps = taps_ref[0, head]
+        taps = taps_ref[head]
         zeros = jnp.zeros((SIDE - HALF - REST, WIDE), F32)
         pooled_key = taps[0:1] * key[:HALF] + taps[1:2] * key[HALF:]
         pooled_value = taps[2:3] * value[:HALF] + taps[3:4] * value[HALF:]
-        side_key = jnp.concatenate([pooled_key, tail_ref[0, head, 0], zeros], axis=0).astype(BF16)
-        side_value = jnp.concatenate([pooled_value, tail_ref[0, head, 1], zeros], axis=0).astype(BF16)
+        tail = tail_ref[head].astype(F32)
+        side_key = jnp.concatenate([pooled_key, tail[:REST], zeros], axis=0).astype(BF16)
+        side_value = jnp.concatenate([pooled_value, tail[REST:], zeros], axis=0).astype(BF16)
         keys_ref[0, 0, head, 0] = side_key
         keys_ref[0, 0, head, 1] = side_value
-        memory_t = mem_ref[0, head]
+        memory_t = mem_ref[head]
         score_side = dot_nt(query_low, side_key) * (SCORE * LOG2E) + side_ref[0]
         score_main = dot(query_low, memory_t[:WIDE]) * (SCORE * LOG2E) + main_ref[0]
         top = jnp.maximum(
@@ -124,7 +141,7 @@
     att_ref[0, 0] = attended
     lane = lax.broadcasted_iota(jnp.int32, (ROWS, WIDE), 1)
     log_ref[0, 0] = jnp.where(lane == 0, logs[0], logs[1])
-    part = dot(attended, proj_ref[0])[None]
+    part = dot(attended, w_ref[PIECES * WIDE :])[None]
 
     @pl.when(pair == 0)
     def _():
@@ -134,7 +151,7 @@
     def _():
         branch[here] += part
 
-    @pl.when(pair == pl.num_programs(0) - 1)
+    @pl.when(pair == pairs - 1)
     def _():
         middle = x_rows[here][0].astype(F32) + branch[here][0]
         middle_ref[0] = middle
@@ -210,9 +227,9 @@
 
 
 def backward_kernel(
-    x_ref, w_ref, mem_ref, side_ref, main_ref, taps_ref, proj_ref, gain_ref,
+    x_ref, w_ref, mem_ref, side_ref, main_ref, taps_ref, gain_ref,
     packed_ref, keys_ref, att_ref, log_ref, normed_ref, grad_ref, grad_low_ref,
-    d_x_ref, d_w_ref, d_proj_ref, d_taps_ref, d_gain_ref,
+    d_x_ref, d_w_ref, d_taps_ref, d_gain_ref,
     grad_normed,
 ):
     pair, clip = pl.program_id(0), pl.program_id(1)
@@ -221,12 +238,11 @@
     @pl.when(clip == 0)
     def _():
         d_w_ref[...] = jnp.zeros_like(d_w_ref)
-        d_proj_ref[...] = jnp.zeros_like(d_proj_ref)
         d_taps_ref[...] = jnp.zeros_like(d_taps_ref)
 
     grad_branch = grad_low_ref[...]
-    grad_out = dot_nt(grad_branch, proj_ref[0])
-    d_proj_ref[0] += dot_tn(att_ref[0, 0], grad_branch)
+    grad_out = dot_nt(grad_branch, w_ref[0, PIECES * WIDE :])
+    d_w_ref[0, PIECES * WIDE :] += dot_tn(att_ref[0, 0], grad_branch)
     pieces = []
     for head in range(PAIR):
         base = 3 * WIDE * head
@@ -273,8 +289,8 @@
             axis=0,
         )
     grad_packed = jnp.concatenate(pieces, axis=1).astype(BF16)
-    d_w_ref[0] += dot_tn(grad_packed, normed_ref[0])
-    part = dot(grad_packed, w_ref[0])[None]
+    d_w_ref[0, : PIECES * WIDE] += dot_tn(grad_packed, normed_ref[0])
+    part = dot(grad_packed, w_ref[0, : PIECES * WIDE])[None]
 
     @pl.when(pair == 0)
     def _():
@@ -313,10 +329,262 @@
     return jax.ShapeDtypeStruct(shape, dtype)
 
 
-def attention_forward(x, w, mem, tail, side, main, taps, proj, gain_one, gain_two):
+class Links:
+    def __init__(self, send, recv):
+        self.send, self.recv, self.made = send, recv, {}
+
+    def add(self, name, src, dst, device):
+        at = len(self.made)
+        self.made[name] = (src, dst, device, at)
+
+    def get(self, name):
+        src, dst, device, at = self.made[name]
+        return pltpu.make_async_remote_copy(
+            src_ref=src,
+            dst_ref=dst,
+            send_sem=self.send.at[at],
+            recv_sem=self.recv.at[at],
+            device_id=device,
+            device_id_type=pl.DeviceIdType.MESH,
+        )
+
+    def start(self, *names):
+        for name in names:
+            self.get(name).start()
+
+    def arrived(self, *names):
+        for name in names:
+            self.get(name).wait_recv()
+
+    def sent(self):
+        for name in self.made:
+            self.get(name).wait_send()
+
+
+def place():
+    batch, head = lax.axis_index("batch"), lax.axis_index("head")
+    z, y, core = batch // 4, lax.rem(batch // 2, 2), lax.rem(batch, 2)
+
+    def at(z, y, core, x):
+        return {"batch": (z * 2 + y) * 2 + core, "head": x}
+
+    return z, y, core, head, at
+
+
+def greet(devices):
+    barrier = pltpu.get_barrier_semaphore()
+    for device in devices:
+        pl.semaphore_signal(barrier, inc=1, device_id=device, device_id_type=pl.DeviceIdType.MESH)
+    pl.semaphore_wait(barrier, len(devices))
+
+
+def turn(z, shift):
+    return lax.rem(z + shift + 4, 4)
+
+
+FORWARD_COPIES = 48
+
+
+def forward_links_kernel(
+    x_ref, side_ref, main_ref, gain_one_ref, gain_two_ref,
+    w_own, mem_own, tail_own, taps_own, hidden_own, output_own,
+    packed_ref, keys_ref, att_ref, log_ref, normed_ref, middle_ref, normed_two_ref,
+    first_all, second_all, w_out, mem_out, taps_out,
+    x_rows, normed_rows, branch, w_all, mem_all, tail_all, taps_all,
+    send, recv, near, save,
+):
+    step = pl.program_id(0)
+    z, y, core, x, at = place()
+    links = Links(send, recv)
+    beside, above, sibling = at(z, y, core, 1 - x), at(z, 1 - y, core, x), at(z, y, 1 - core, x)
+    along = [at(turn(z, shift), y, core, x) for shift in (1, 2, 3)]
+    column = pl.ds(pl.multiple_of(core * MAIN, MAIN), MAIN)
+
+    def slab(z, y):
+        return (lax.div(2 * z + y, 4), pl.ds(pl.multiple_of(lax.rem(2 * z + y, 4) * 256, 256), 256), column)
+
+    def w_far(z, y):
+        pair, rows, lanes = slab(z, y)
+        return w_all.at[2 + pair, rows, lanes]
+
+    links.add("xw", w_own.at[slab(z, y)], w_far(z, y), beside)
+    for shift in (1, 2, 3):
+        links.add(f"zw{shift}", w_far(z, y), w_far(z, y), along[shift - 1])
+    for shift in range(4):
+        links.add(f"yw{shift}", w_far(turn(z, -shift), y), w_far(turn(z, -shift), y), above)
+    far = w_all.at[pl.ds(2, 2), :, column]
+    links.add("cw", far, far, sibling)
+    me = ((z * 2 + y) * 2 + core) * 2 + x
+    links.add("x0", hidden_own, first_all.at[me], beside)
+    links.add("x1", output_own, second_all.at[me], beside)
+
+    def group(which, z, y):
+        return (first_all, second_all)[which].at[pl.ds(((z * 2 + y) * 2 + core) * 2, 2)]
+
+    for which in (0, 1):
+        for shift in (1, 2, 3):
+            links.add(f"z{shift}{which}", group(which, z, y), group(which, z, y), along[shift - 1])
+        for shift in range(4):
+            from_z = turn(z, -shift)
+            links.add(f"y{shift}{which}", group(which, from_z, y), group(which, from_z, y), above)
+            links.add(f"c{shift}{which}", group(which, from_z, y), group(which, from_z, y), sibling)
+            links.add(f"d{shift}{which}", group(which, from_z, 1 - y), group(which, from_z, 1 - y), sibling)
+    clips = mem_own.shape[0]
+    for clip in range(clips):
+        links.add(f"m{clip}", mem_own.at[clip, 1 - x, :, :, pl.ds(0, MAIN)], mem_all.at[1, clip], beside)
+    links.add("tail", tail_own.at[:, 1 - x], tail_all.at[1], beside)
+    links.add("taps", taps_own, taps_all.at[pl.ds(2, 2)], beside)
+
+    local = [
+        (w_own, w_all.at[pl.ds(0, 2)]),
+        (tail_own.at[:, x], tail_all.at[0]),
+        (taps_own, taps_all.at[pl.ds(0, 2)]),
+        (hidden_own, first_all.at[me]),
+        (output_own, second_all.at[me]),
+    ] + [(mem_own.at[clip, x, :, :, pl.ds(0, MAIN)], mem_all.at[0, clip]) for clip in range(clips)]
+    local = [pltpu.make_async_copy(src, dst, near.at[i]) for i, (src, dst) in enumerate(local)]
+    saved = [
+        (w_all, w_out),
+        (taps_all, taps_out),
+        (mem_all.at[0], mem_out.at[0]),
+        (mem_all.at[1], mem_out.at[1]),
+    ]
+    saved = [pltpu.make_async_copy(src, dst, save.at[i]) for i, (src, dst) in enumerate(saved)]
+
+    @pl.when(step == 0)
+    def _():
+        greet([beside, above, sibling] + along)
+        links.start("xw", "taps", "tail", "x0", "x1")
+        for copy in local:
+            copy.start()
+        for copy in local:
+            copy.wait()
+
+    def both(*names):
+        return [name + str(which) for name in names for which in (0, 1)]
+
+    plan = {
+        2: (["xw"], ["zw1", "zw2", "zw3", "yw0"]),
+        3: (["x0", "x1"], both("z1", "z2", "z3", "y0", "c0") + ["m0", "m1"]),
+        5: (["zw1", "zw2", "zw3"], ["yw1", "yw2", "yw3"]),
+        6: ([], ["m2", "m3"]),
+        7: (["yw0", "yw1", "yw2", "yw3"], ["cw"]),
+        8: (["cw", "tail", "taps", "m0"], []),
+        9: (both("z1"), both("y1", "c1")),
+        10: (["m1"] + both("z2"), both("y2", "c2")),
+        12: (["m2"], []),
+        13: (both("y0", "y1"), both("d0", "d1")),
+        14: (["m3"] + both("z3"), both("y3", "c3")),
+    }
+    for when, (awaited, started) in plan.items():
+
+        @pl.when(step == when)
+        def _(awaited=awaited, started=started):
+            links.arrived(*awaited)
+            links.start(*started)
+
+    @pl.when(step == 14)
+    def _():
+        for copy in saved:
+            copy.start()
+
+    pair, clip = pair_of(step), clip_of(step)
+    side = lax.div(pair, 2)
+    heads = pl.ds(lax.rem(pair, 2) * PAIR, PAIR)
+    forward_step(
+        pair, clip, 4,
+        w_all.at[pair], mem_all.at[side, clip, heads], tail_all.at[side, clip, heads], taps_all.at[pair],
+        x_ref, side_ref, main_ref, gain_one_ref, gain_two_ref,
+        packed_ref, keys_ref, att_ref, log_ref, normed_ref, middle_ref, normed_two_ref,
+        x_rows, normed_rows, branch,
+    )
+
+    @pl.when(step == pl.num_programs(0) - 1)
+    def _():
+        links.arrived(*both("y2", "y3"))
+        links.start(*both("d2", "d3"))
+        for copy in saved:
+            copy.wait()
+        links.arrived(*both("c0", "c1", "c2", "c3", "d0", "d1", "d2", "d3"))
+        links.sent()
+
+
+def pair_of(step):
+    return jnp.where(step < 8, lax.div(step, 4), 2 + lax.rem(step, 2))
+
+
+def clip_of(step):
+    return jnp.where(step < 8, lax.rem(step, 4), lax.div(step, 2) - 4)
+
+
+def attention_forward_links(x, w, mem, tail, side, main, taps, gain_one, gain_two, hidden_weight, output_weight):
+    clips, width = x.shape[0], x.shape[2]
+    packed_width = PIECES * WIDE
+    devices = 32
+    early = lambda s: jnp.where(s < 4, s, clips - 1)
+    late = lambda s: jnp.where(s < 8, 0, clip_of(s))
+    anywhere = pl.BlockSpec(memory_space=pl.ANY)
+    return pl.pallas_call(
+        forward_links_kernel,
+        grid=(4 * clips,),
+        in_specs=[
+            pl.BlockSpec((1, TPC, width), lambda s: (early(s), 0, 0)),
+            pl.BlockSpec((1, 1, SIDE), lambda s: (clip_of(s), 0, 0)),
+            pl.BlockSpec((1, 1, MAIN), lambda s: (clip_of(s), 0, 0)),
+            pl.BlockSpec((1, width), lambda s: (0, 0)),
+            pl.BlockSpec((1, width), lambda s: (0, 0)),
+        ] + [anywhere] * 6,
+        out_specs=[
+            pl.BlockSpec((1, 1, ROWS, packed_width), lambda s: (pair_of(s), clip_of(s), 0, 0)),
+            pl.BlockSpec((1, 1, PAIR, 2, SIDE, WIDE), lambda s: (pair_of(s), clip_of(s), 0, 0, 0, 0)),
+            pl.BlockSpec((1, 1, ROWS, PAIR * WIDE), lambda s: (pair_of(s), clip_of(s), 0, 0)),
+            pl.BlockSpec((1, 1, ROWS, WIDE), lambda s: (pair_of(s), clip_of(s), 0, 0)),
+            pl.BlockSpec((1, ROWS, width), lambda s: (early(s), 0, 0)),
+            pl.BlockSpec((1, ROWS, width), lambda s: (late(s), 0, 0)),
+            pl.BlockSpec((1, ROWS, width), lambda s: (late(s), 0, 0)),
+        ] + [anywhere] * 5,
+        out_shape=[
+            shaped((4, clips, ROWS, packed_width), BF16),
+            shaped((4, clips, PAIR, 2, SIDE, WIDE), BF16),
+            shaped((4, clips, ROWS, PAIR * WIDE), BF16),
+            shaped((4, clips, ROWS, WIDE), F32),
+            shaped((clips, ROWS, width), BF16),
+            shaped((clips, ROWS, width), F32),
+            shaped((clips, ROWS, width), BF16),
+            shaped((devices,) + hidden_weight.shape, BF16),
+            shaped((devices,) + output_weight.shape, BF16),
+            shaped((4,) + w.shape[1:], BF16),
+            shaped((2, clips, 4, 2 * HD, MAIN), BF16),
+            shaped((4,) + taps.shape[1:], F32),
+        ],
+        scratch_shapes=[
+            pltpu.VMEM((clips, ROWS, width), BF16),
+            pltpu.VMEM((clips, ROWS, width), BF16),
+            pltpu.VMEM((clips, ROWS, width), F32),
+            pltpu.VMEM((4,) + w.shape[1:], BF16),
+            pltpu.VMEM((2, clips, 4, 2 * HD, MAIN), BF16),
+            pltpu.VMEM((2, clips, 4, 2 * REST, WIDE), BF16),
+            pltpu.VMEM((4,) + taps.shape[1:], F32),
+            pltpu.SemaphoreType.DMA((FORWARD_COPIES,)),
+            pltpu.SemaphoreType.DMA((FORWARD_COPIES,)),
+            pltpu.SemaphoreType.DMA((5 + clips,)),
+            pltpu.SemaphoreType.DMA((4,)),
+        ],
+        compiler_params=pltpu.CompilerParams(
+            dimension_semantics=("arbitrary",),
+            vmem_limit_bytes=VMEM_LIMIT,
+            collective_id=0,
+            has_side_effects=True,
+        ),
+        name="attention_forward_links",
+    )(x, side, main, gain_one, gain_two, w, mem, tail, taps, hidden_weight, output_weight)
+
+
+def attention_forward(x, w, mem, tail, side, main, taps, gain_one, gain_two):
     clips, pairs = x.shape[0], w.shape[0]
     width = x.shape[2]
-    packed_width = w.shape[1]
+    packed_width = PIECES * WIDE
+    weight_rows = w.shape[1]
     late = lambda p, c: jnp.where(p == pairs - 1, c, 0)
     early = lambda p, c: jnp.where(p == 0, c, clips - 1)
     per_step = lambda p, c: (p, c)
@@ -325,13 +593,12 @@
         grid=(pairs, clips),
         in_specs=[
             pl.BlockSpec((1, TPC, width), lambda p, c: (early(p, c), 0, 0)),
-            pl.BlockSpec((1, packed_width, width), lambda p, c: (p, 0, 0)),
+            pl.BlockSpec((1, weight_rows, width), lambda p, c: (p, 0, 0)),
             pl.BlockSpec((1, PAIR, 2 * HD, MAIN), lambda p, c: (c, p, 0, 0)),
-            pl.BlockSpec((1, PAIR, 2, REST, WIDE), lambda p, c: (c, p, 0, 0, 0)),
+            pl.BlockSpec((1, PAIR, 2 * REST, WIDE), lambda p, c: (c, p, 0, 0)),
             pl.BlockSpec((1, 1, SIDE), lambda p, c: (c, 0, 0)),
             pl.BlockSpec((1, 1, MAIN), lambda p, c: (c, 0, 0)),
             pl.BlockSpec((1, PAIR, 4, WIDE), lambda p, c: (p, 0, 0, 0)),
-            pl.BlockSpec((1, PAIR * WIDE, width), lambda p, c: (p, 0, 0)),
             pl.BlockSpec((1, width), lambda p, c: (0, 0)),
             pl.BlockSpec((1, width), lambda p, c: (0, 0)),
         ],
@@ -340,7 +607,7 @@
             pl.BlockSpec((1, 1, PAIR, 2, SIDE, WIDE), lambda p, c: (p, c, 0, 0, 0, 0)),
             pl.BlockSpec((1, 1, ROWS, PAIR * WIDE), lambda p, c: (p, c, 0, 0)),
             pl.BlockSpec((1, 1, ROWS, WIDE), lambda p, c: (p, c, 0, 0)),
-            pl.BlockSpec((1, ROWS, width), lambda p, c: (c, 0, 0)),
+            pl.BlockSpec((1, ROWS, width), lambda p, c: (early(p, c), 0, 0)),
             pl.BlockSpec((1, ROWS, width), lambda p, c: (late(p, c), 0, 0)),
             pl.BlockSpec((1, ROWS, width), lambda p, c: (late(p, c), 0, 0)),
         ],
@@ -360,7 +627,7 @@
         ],
         compiler_params=compiler_params(2),
         name="attention_forward",
-    )(x, w, mem, tail, side, main, taps, proj, gain_one, gain_two)
+    )(x, w, mem, tail, side, main, taps, gain_one, gain_two)
 
 
 def once(shape):
@@ -413,22 +680,26 @@
     )(normed, cot, first, second, middle, gain)
 
 
-def attention_backward(x, w, mem, side, main, taps, proj, gain, packed, keys, att, log, normed, grad, grad_low):
+def attention_backward(x, w, mem, side, main, taps, gain, packed, keys, att, log, normed, grad, grad_low):
     clips, pairs = x.shape[0], w.shape[0]
     width = x.shape[2]
-    packed_width = w.shape[1]
+    packed_width = PIECES * WIDE
+    weight_rows = w.shape[1]
     late = lambda p, c: jnp.where(p == pairs - 1, c, 0)
     return pl.pallas_call(
         backward_kernel,
         grid=(pairs, clips),
         in_specs=[
             pl.BlockSpec((1, TPC, width), lambda p, c: (late(p, c), 0, 0)),
-            pl.BlockSpec((1, packed_width, width), lambda p, c: (p, 0, 0)),
-            pl.BlockSpec((1, PAIR, 2 * HD, MAIN), lambda p, c: (c, p, 0, 0)),
+            pl.BlockSpec((1, weight_rows, width), lambda p, c: (p, 0, 0)),
+            pl.BlockSpec((1, PAIR, 2 * HD, MAIN), lambda p, c: (c, p, 0, 0))
+            if mem.ndim == 4
+            else pl.BlockSpec(
+                (None, 1, PAIR, 2 * HD, MAIN), lambda p, c: (lax.div(p, 2), c, lax.rem(p, 2), 0, 0)
+            ),
             pl.BlockSpec((1, 1, SIDE), lambda p, c: (c, 0, 0)),
             pl.BlockSpec((1, 1, MAIN), lambda p, c: (c, 0, 0)),
             pl.BlockSpec((1, PAIR, 4, WIDE), lambda p, c: (p, 0, 0, 0)),
-            pl.BlockSpec((1, PAIR * WIDE, width), lambda p, c: (p, 0, 0)),
             pl.BlockSpec((1, width), lambda p, c: (0, 0)),
             pl.BlockSpec((1, 1, ROWS, packed_width), lambda p, c: (p, c, 0, 0)),
             pl.BlockSpec((1, 1, PAIR, 2, SIDE, WIDE), lambda p, c: (p, c, 0, 0, 0, 0)),
@@ -440,22 +711,20 @@
         ],
         out_specs=[
             pl.BlockSpec((1, TPC, width), lambda p, c: (late(p, c), 0, 0)),
-            pl.BlockSpec((1, packed_width, width), lambda p, c: (p, 0, 0)),
-            pl.BlockSpec((1, PAIR * WIDE, width), lambda p, c: (p, 0, 0)),
+            pl.BlockSpec((1, weight_rows, width), lambda p, c: (p, 0, 0)),
             pl.BlockSpec((1, PAIR, 4, WIDE), lambda p, c: (p, 0, 0, 0)),
             pl.BlockSpec((1, width), lambda p, c: (0, 0)),
         ],
         out_shape=[
             shaped((clips, TPC, width), BF16),
-            shaped((pairs, packed_width, width), F32),
-            shaped((pairs, PAIR * WIDE, width), F32),
+            shaped((pairs, weight_rows, width), F32),
             shaped((pairs, PAIR, 4, WIDE), F32),
             shaped((1, width), F32),
         ],
         scratch_shapes=[pltpu.VMEM((clips, ROWS, width), F32)],
         compiler_params=compiler_params(2),
         name="attention_backward",
-    )(x, w, mem, side, main, taps, proj, gain, packed, keys, att, log, normed, grad, grad_low)
+    )(x, w, mem, side, main, taps, gain, packed, keys, att, log, normed, grad, grad_low)
 
 
 def group_gather(own, heads, fetch=None):
@@ -477,6 +746,7 @@
 
 def local(
     heads,
+    batches,
     inputs,
     qkv_weight,
     proj_weight,
@@ -496,29 +766,21 @@
     all_heads = own_heads * heads
     pairs = all_heads // PAIR
     me = lax.axis_index("head")
+    linked = (heads, batches, micro, own_clips) == (2, 16, 4, 1)
 
     def mine(array, shift):
         start = lax.rem(me + shift + heads, heads) * own_clips
         return lax.dynamic_slice_in_dim(array, start, own_clips, axis=1)
 
-    w_own = qkv_weight.transpose(1, 2, 0)
-    w_all = jnp.concatenate(group_gather(w_own, heads), axis=0)
-    proj_all = jnp.concatenate(group_gather(proj_weight, heads), axis=0)
-    taps_all = jnp.concatenate(group_gather(pool_weight, heads), axis=0)
+    pad = WIDE - HD
+    qkv_rows = jnp.pad(
+        qkv_weight.transpose(1, 2, 0).reshape(own_heads, 3, HD, width), ((0, 0), (0, 0), (0, pad), (0, 0))
+    )
+    proj_rows = jnp.pad(proj_weight, ((0, 0), (0, pad), (0, 0)))
+    taps_own = jnp.pad(pool_weight.astype(F32), ((0, 0), (0, 0), (0, pad)))
     memory_t = memory.transpose(0, 1, 3, 4, 2)
-    mem_all = jnp.concatenate(group_gather(memory_t, heads, mine), axis=2)
-    mem_all = mem_all.reshape(clips, all_heads, 2 * HD, TPC)
-
-    first = lax.all_gather(hidden_weight, ("batch", "head"), axis=0, tiled=True)
-    second = lax.all_gather(output_weight, ("batch", "head"), axis=0, tiled=True)
-
-    pad = WIDE - HD
-    w_all = jnp.pad(w_all.reshape(all_heads, 3, HD, width), ((0, 0), (0, 0), (0, pad), (0, 0)))
-    w_all = w_all.reshape(pairs, PIECES * WIDE, width)
-    proj_all = jnp.pad(proj_all, ((0, 0), (0, pad), (0, 0))).reshape(pairs, PAIR * WIDE, width)
-    taps_all = jnp.pad(taps_all.astype(F32), ((0, 0), (0, 0), (0, pad))).reshape(pairs, PAIR, 4, WIDE)
-    tail = mem_all[..., MAIN:].reshape(clips, all_heads, 2, HD, REST).swapaxes(3, 4)
-    tail = jnp.pad(tail.astype(F32), ((0, 0),) * 4 + ((0, pad),))
+    tail_own = memory_t[..., MAIN:].reshape(memory_t.shape[:3] + (2, HD, REST)).swapaxes(4, 5)
+    tail_own = jnp.pad(tail_own, ((0, 0),) * 5 + ((0, pad),)).reshape(memory_t.shape[:3] + (2 * REST, WIDE))
 
     index = mine(clip_index, 0).reshape(clips, 1, 1)
     main_slot = lax.broadcasted_iota(jnp.int32, (1, 1, MAIN), 2) // PTOK
@@ -530,9 +792,43 @@
     x = inputs.reshape(clips, TPC, width)
     gain_one = gain_one.reshape(1, width)
     gain_two = gain_two.reshape(1, width)
-    packed, keys, att, log, normed, middle, normed_two = attention_forward(
-        x, w_all, mem_all, tail, side_mask, main_mask, taps_all, proj_all, gain_one, gain_two
-    )
+    w_own = jnp.concatenate(
+        [
+            qkv_rows.reshape(-1, PIECES * WIDE, width),
+            proj_rows.reshape(-1, PAIR * WIDE, width),
+        ],
+        axis=1,
+    ) if own_heads % PAIR == 0 else None
+    if linked:
+        (packed, keys, att, log, normed, middle, normed_two, first, second, w_all, mem_all, taps_all) = (
+            attention_forward_links(
+                x, w_own, memory_t, tail_own, side_mask, main_mask,
+                taps_own.reshape(-1, PAIR, 4, WIDE), gain_one, gain_two, hidden_weight, output_weight,
+            )
+        )
+        first = first.reshape(width, -1)
+        second = second.reshape(-1, width)
+    else:
+        qkv_all = jnp.concatenate(group_gather(qkv_rows, heads), axis=0)
+        proj_all = jnp.concatenate(group_gather(proj_rows, heads), axis=0)
+        w_all = jnp.concatenate(
+            [
+                qkv_all.reshape(pairs, PIECES * WIDE, width),
+                proj_all.reshape(pairs, PAIR * WIDE, width),
+            ],
+            axis=1,
+        )
+        taps_all = jnp.concatenate(group_gather(taps_own, heads), axis=0).reshape(pairs, PAIR, 4, WIDE)
+        mem_all = jnp.concatenate(group_gather(memory_t, heads, mine), axis=2)
+        mem_all = mem_all.reshape(clips, all_heads, 2 * HD, TPC)
+        tail = jnp.concatenate(group_gather(tail_own, heads, mine), axis=2)
+        tail = tail.reshape(clips, all_heads, 2 * REST, WIDE)
+
+        first = lax.all_gather(hidden_weight, ("batch", "head"), axis=0, tiled=True)
+        second = lax.all_gather(output_weight, ("batch", "head"), axis=0, tiled=True)
+        packed, keys, att, log, normed, middle, normed_two = attention_forward(
+            x, w_all, mem_all, tail, side_mask, main_mask, taps_all, gain_one, gain_two
+        )
     outputs, grad, grad_low, d_first, d_second, d_gain_two = mlp(
         normed_two.reshape(clips * ROWS, width),
         cotangent.reshape(clips, TPC, width),
@@ -541,12 +837,13 @@
         middle.reshape(clips * ROWS, width),
         gain_two,
     )
-    d_x, d_w, d_proj, d_taps, d_gain_one = attention_backward(
-        x, w_all, mem_all, side_mask, main_mask, taps_all, proj_all, gain_one,
+    d_x, d_w, d_taps, d_gain_one = attention_backward(
+        x, w_all, mem_all, side_mask, main_mask, taps_all, gain_one,
         packed, keys, att, log, normed, grad, grad_low,
     )
-    d_w = d_w.reshape(heads, own_heads, 3, WIDE, width)[:, :, :, :HD].reshape(heads, own_heads, 3 * HD, width)
-    d_proj = d_proj.reshape(heads, own_heads, WIDE, width)[:, :, :HD]
+    d_proj = d_w[:, PIECES * WIDE :].reshape(heads, own_heads, WIDE, width)[:, :, :HD]
+    d_w = d_w[:, : PIECES * WIDE].reshape(heads, own_heads, 3, WIDE, width)[:, :, :, :HD]
+    d_w = d_w.reshape(heads, own_heads, 3 * HD, width)
     d_taps = d_taps.reshape(heads, own_heads, 4, WIDE)[..., :HD]
     d_w, d_proj, d_taps = (
         lax.psum(group_sum(list(grads), heads).astype(BF16), "batch").astype(F32)
@@ -573,7 +870,7 @@
 
 def solution(mesh):
     return jax.shard_map(
-        functools.partial(local, mesh.shape["head"]),
+        functools.partial(local, mesh.shape["head"], mesh.shape["batch"]),
         mesh=mesh,
         in_specs=(
             P(None, ("batch", "head"), None, None),

time: 760 us -> 599 us (0.79)
  waiting for transfers between devices: 434 us -> 195 us
  Pallas kernels: 197 us -> 274 us
  blocking collectives: 72.2 us -> 80.5 us
    ppermute x4 -> x0, waiting for transfers between devices: 141 us -> none  [group_gather(): lax.ppermute(sent, 'head', [(src, (src - shift) % heads) for src in range...]
    reduce_scatter x1, waiting for transfers between devices: 107 us -> 0.01 us  [local(): lax.psum_scatter(d_first, both, scatter_dimension=0, tiled=True).astype(F32)]
    pallas_call x1, Pallas kernels: 45.1 us -> 122 us  [attention_forward_links(): pl.pallas_call(forward_links_kernel, grid=(4 * clips,), in_specs=[pl.Bloc...]
    psum x1, waiting for transfers between devices: 24.8 us -> 37.1 us  [local(): lax.psum(group_sum(list(grads), heads).astype(BF16), 'batch').astype(F32)]
    unnamed x1, blocking collectives: 39.9 us -> 47.9 us
    slice x1 -> x3, local copies, waits for them, and re-layouts: 0.29 us -> 8.05 us  [the longest x1 4.29 us: local(): d_w[:, :PIECES * WIDE].reshape(heads, own_heads, 3, WIDE, width)]
  transfers between devices with their start and end apart: 12 -> 6, of which waited for: 5 -> 3; matrix products, arithmetic and copies ran while one was open for 3% -> 2% of each run, Pallas kernels for 6% -> 0%
where the time goes in v2:
time: 599 us
  Pallas kernels  274 us (46%)
  waiting for transfers between devices  195 us (33%)
  blocking collectives  80.5 us (13%)
  between operations  15.7 us (3%)
  other arithmetic  15 us (3%)
  local copies, waits for them, and re-layouts  14.8 us (2%)
    pallas_call x1, Pallas kernels, attention_forward_links(): pl.pallas_call(forward_links_kernel, grid=(4 * clips,), in_specs=[pl.Bloc...  122 us
    reduce_scatter x1, waiting for transfers between devices, local(): lax.psum_scatter(d_second, both, scatter_dimension=0, tiled=True)  108 us
    pallas_call x1, Pallas kernels, mlp(): pl.pallas_call(mlp_kernel, grid=(hidden // tile,), in_specs=[once((rows,...  80.9 us
    pallas_call x1, Pallas kernels, attention_backward(): pl.pallas_call(backward_kernel, grid=(pairs, clips), in_specs=[pl.BlockSp...  71.1 us
    ppermute x3, waiting for transfers between devices, group_sum(): lax.ppermute(blocks[shift].astype(BF16), 'head', [(src, (src + shift) % h...  48.8 us
    unnamed x1, blocking collectives  47.9 us
    psum x1, waiting for transfers between devices, local(): lax.psum(group_sum(list(grads), heads).astype(BF16), 'batch').astype(F32)  37.1 us
    psum x1, blocking collectives, local(): lax.psum(group_sum(list(grads), heads).astype(BF16), 'batch').astype(F32)  32.6 us
  transfers between devices with their start and end apart: 6, of which 3 were waited for; matrix products, arithmetic and copies ran while one was open for 2% of the time, Pallas kernels for 0%

profile of v2, /device:TPU:0, one launch (start us, length us, event | category | flops | bytes accessed | tf_op | source)
XLA Modules:
  0.0 598.5 jit_solution(7620261927566448697)
XLA Ops:
  8.1 1.6 slice.32
  9.7 0.7 copy.23
  10.4 0.7 pad_bitcast_fusion.tail_own
  11.1 0.6 reshape.267.gain_one_ref.gain_ref
  11.6 0.6 reshape.268.gain_two_ref.gain_ref
  12.2 1.7 pad.17
  13.9 1.1 pad.18
  15.1 0.6 convert.16.taps_own
  15.7 0.7 compare_select_fusion.main_ref
  16.4 1.9 pad_maximum_fusion.w_own
  18.2 0.7 or_select_fusion.side_ref
  18.9 122.0 %attention_forward_links.1 = (bf16[4,4,400,768]{3,2,1,0:T(8,128)(2,1)}, bf16[4,4,2,2,256,128]{5,4,3,2,1,0:T(8,128)(2,1)}, bf16[4,4,400,256]{3,2,1,0:T(8,128)(2,1...) custom-call(bf16[4,392,768]{2,1,0:T(8,128)(2,1)} %bitcast.61, ...), custom_call_target="tpu_custom_call" | custom-call | tf_op jit(solution)/shard_map/attention_forward_links/pallas_call | solution.py:527
  140.9 80.9 %mlp.1 = (bf16[4,392,768]{2,1,0:T(8,128)(2,1)}, f32[1600,768]{1,0:T(8,128)}, bf16[1600,768]{1,0:T(8,128)(2,1)}, bf16[768,3072]{1,0:T(8,128)(2,1)}, bf16[3072,768]{1,0:T(8,128)(2,1)}, /*index=5*/f32[1,768]{1,0:T(1,128)}) custom-call(bf16[1600,768]{1,0:T(8,128)(2,1)} %bitcast.71, bf16[4,392,768]{2,1,0:T(8,128)(2,1)} %bitcast.72, bf16[768,3072]{1,0:T(8,128)(2,1)} %bitcast.68, ...), custom_call_target="tpu_custom_call" | custom-call | tf_op jit(solution)/shard_map/mlp/pallas_call | solution.py:642
  221.8 71.1 %attention_backward.1 = (bf16[4,392,768]{2,1,0:T(8,128)(2,1)}, f32[4,1024,768]{2,1,0:T(8,128)}, f32[4,2,4,128]{3,2,1,0:T(4,128)}, f32[1,768]{1,0:T(1,128)}) custom-call(bf16[4,392,768]{2,1,0:T(8,128)(2,1)} %bitcast.62, bf16[4,1024,768]{2,1,0:T(8,128)(2,1)} %get-tuple-element.36.w_ref, bf16[2,4,4,192,384]{4,3,2,1,0:T(8,128)(2,1)} %get-tuple-element.37.mem_ref, ...), custom_call_target="tpu_custom_call" | custom-call | tf_op jit(solution)/shard_map/attention_backward/pallas_call | solution.py:689
  292.9 4.3 slice.28
  297.4 1.6 collective-permute-start
  299.0 2.2 slice.29
  301.3 0.6 collective-permute-start.1
  302.3 48.7 %collective-permute-done.1 = bf16[4,96,768]{2,1,0:T(8,128)(2,1)S(1)} collective-permute-done((bf16[4,96,768]{2,1,0:T(8,128)(2,1)S(1)}, bf16[4,96,768]{2,1,0:T(8,128)(2,1)S(1)}, u32[]{:S(2)}, u32[]{:S(2)}) %collective-permute-start.1) | collective-permute-done | bytes 589856 | tf_op jit(solution)/shard_map/ppermute | solution.py:741
  351.0 1.0 fusion.2
  352.0 1.6 fusion
  354.3 0.5 reduce-scatter.6.cloned.1.call-update
  354.9 1.5 collective-permute-start.2
  356.4 47.9 %all-reduce.4 = f32[2,768]{1,0:T(2,128)S(1)} all-reduce(f32[2,768]{1,0:T(2,128)S(1)} %pad_maximum_fusion.1), channel_id=2, replica_groups=mesh['batch'=16,'head'=2] {'batch','head'}, use_global_device_ids=true, to_apply=%region_3.4.clone | all-reduce | flops 1536 | bytes 12288
  405.0 32.6 %psum.23 = bf16[4,4,96]{2,1,0:T(4,128)(2,1)S(1)} all-reduce(bf16[4,4,96]{2,1,0:T(4,128)(2,1)S(1)} %fusion.5), channel_id=1, replica_groups=mesh['batch'=16,'head'=2] {'batch'}, use_global_device_ids=true, to_apply=%region_2.3 | all-reduce | flops 1536 | bytes 6144 | tf_op jit(solution)/shard_map/psum | solution.py:849
  437.5 0.6 convert_element_type.62
  438.1 37.1 %all-reduce.8.cloned.1.call-done = (bf16[768,4,288]{0,2,1:T(8,128)(2,1)}, bf16[4,96,768]{2,1,0:T(8,128)(2,1)}) async-done(((bf16[768,4,288]{0,2,1:T(8,128)(2,1)}, bf16[4,96,768]{2,1,0:T(8,128)(2,1)}), (bf16[768,4,288]{0,2,1:T(8,128)(2,1)}, bf16[4,96,768]{2,1,0:T(8,128)(2,1)})) %all-reduce.8.cloned.1.call-update) | async-done | bytes 2359312 | tf_op jit(solution)/shard_map/psum | solution.py:849
  475.2 3.6 transpose.25
  478.8 1.1 convert_element_type.58
  480.0 1.6 convert_element_type.63
  481.6 107.8 %reduce-scatter.6.cloned.1.call-done = bf16[96,768]{1,0:T(8,128)(2,1)} async-done(((bf16[3072,768]{1,0:T(8,128)(2,1)}), bf16[96,768]{1,0:T(8,128)(2,1)}) %reduce-scatter.6.cloned.1.call-update) | async-done | bytes 147472 | tf_op jit(solution)/shard_map/reduce_scatter | solution.py:854
  589.4 1.6 convert_element_type.64
  (36 shorter events, 2.1 us)
Async XLA Ops:
  8.0 3.0 copy-start.2
  8.0 3.6 copy-start.3
  8.0 467.2 %all-reduce.8.cloned.1.call-start = ((), (), s32[]{:S(2)}) async-start(), calls=%async_computation.4 | async-start | bytes 4718592 | tf_op jit(solution)/shard_map/psum | solution.py:849
  10.3 4.7 copy-start.4
  10.4 5.3 copy-start.7
  297.4 54.6 %collective-permute-start = (bf16[4,288,768]{2,1,0:T(8,128)(2,1)S(1)}, bf16[4,288,768]{2,1,0:T(8,128)(2,1)S(1)}, u32[]{:S(2)}, u32[]{:S(2)}) collective-permute-start(bf16[4,288,768]{2,1,0:T(8,128)(2,1)S(1)} %bitcast.73), channel_id=1, source_target_pairs={{0,1},{1,0},{2,3},{3,2},{4,5},{5,4},{6,7},{7,6},{8,9},{9,8},{10,11... | collective-permute-start | bytes 5308424 | tf_op jit(solution)/shard_map/ppermute | solution.py:741
  301.3 49.7 %collective-permute-start.1 = (bf16[4,96,768]{2,1,0:T(8,128)(2,1)S(1)}, bf16[4,96,768]{2,1,0:T(8,128)(2,1)S(1)}, u32[]{:S(2)}, u32[]{:S(2)}) collective-permute-start(bf16[4,96,768]{2,1,0:T(8,128)(2,1)S(1)} %fusion.3), channel_id=1, source_target_pairs={{0,1},{1,0},{2,3},{3,2},{4,5},{5,4},{6,7},{7,6},{8,9},{9,8},{10,11... | collective-permute-start | bytes 1769480 | tf_op jit(solution)/shard_map/ppermute | solution.py:741
  353.6 126.4 %reduce-scatter.4.cloned.1.call-start = ((), (), s32[]{:S(2)}) async-start(), calls=%async_computation.2 | async-start | bytes 4866048 | tf_op jit(solution)/shard_map/reduce_scatter | solution.py:853
  354.2 0.7 copy-start.1
  354.2 2.2 copy-start.5
  354.2 2.2 copy-start.6
  354.2 235.2 %reduce-scatter.6.cloned.1.call-start = ((), (), s32[]{:S(2)}) async-start(), calls=%async_computation.3 | async-start | bytes 4866048 | tf_op jit(solution)/shard_map/reduce_scatter | solution.py:854
  354.9 50.0 %collective-permute-start.2 = (bf16[4,4,96]{2,1,0:T(4,128)(2,1)S(1)}, bf16[4,4,96]{2,1,0:T(4,128)(2,1)S(1)}, u32[]{:S(2)}, u32[]{:S(2)}) collective-permute-start(bf16[4,4,96]{2,1,0:T(4,128)(2,1)S(1)} %fusion.6), channel_id=1, source_target_pairs={{0,1},{1,0},{2,3},{3,2},{4,5},{5,4},{6,7},{7,6},{8,9},{9,8},{10,11... | collective-permute-start | bytes 9224 | tf_op jit(solution)/shard_map/ppermute | solution.py:741
  475.2 3.6 copy-start
Sparse Core Ops, SparseCore 0:
  353.7 121.4 all-reduce.7
Sparse Core Ops, SparseCore 1:
  359.5 117.7 reduce-scatter.3
  483.5 105.9 reduce-scatter.5

commit v3 on v2

--- a/solution.py
+++ b/solution.py
@@ -232,7 +232,22 @@
     d_x_ref, d_w_ref, d_taps_ref, d_gain_ref,
     grad_normed,
 ):
-    pair, clip = pl.program_id(0), pl.program_id(1)
+    backward_step(
+        pl.program_id(1), pl.program_id(0) == 0, pl.program_id(0) == pl.num_programs(0) - 1,
+        w_ref.at[0], d_w_ref.at[0], d_taps_ref.at[0],
+        x_ref, mem_ref, side_ref, main_ref, taps_ref, gain_ref,
+        packed_ref, keys_ref, att_ref, log_ref, normed_ref, grad_ref, grad_low_ref,
+        d_x_ref, d_gain_ref, grad_normed,
+    )
+
+
+def backward_step(
+    clip, first_pair, last_pair,
+    w_ref, d_w_ref, d_taps_ref,
+    x_ref, mem_ref, side_ref, main_ref, taps_ref, gain_ref,
+    packed_ref, keys_ref, att_ref, log_ref, normed_ref, grad_ref, grad_low_ref,
+    d_x_ref, d_gain_ref, grad_normed,
+):
     here = pl.ds(clip, 1)
 
     @pl.when(clip == 0)
@@ -241,8 +256,8 @@
         d_taps_ref[...] = jnp.zeros_like(d_taps_ref)
 
     grad_branch = grad_low_ref[...]
-    grad_out = dot_nt(grad_branch, w_ref[0, PIECES * WIDE :])
-    d_w_ref[0, PIECES * WIDE :] += dot_tn(att_ref[0, 0], grad_branch)
+    grad_out = dot_nt(grad_branch, w_ref[PIECES * WIDE :])
+    d_w_ref[PIECES * WIDE :] += dot_tn(att_ref[0, 0], grad_branch)
     pieces = []
     for head in range(PAIR):
         base = 3 * WIDE * head
@@ -276,7 +291,7 @@
             jnp.concatenate([taps[0:1] * grad_key, taps[1:2] * grad_key], axis=0),
             jnp.concatenate([taps[2:3] * grad_value, taps[3:4] * grad_value], axis=0),
         ]
-        d_taps_ref[0, head] += jnp.concatenate(
+        d_taps_ref[head] += jnp.concatenate(
             [
                 jnp.sum(part * grad, axis=0, keepdims=True)
                 for part, grad in (
@@ -289,18 +304,18 @@
             axis=0,
         )
     grad_packed = jnp.concatenate(pieces, axis=1).astype(BF16)
-    d_w_ref[0, : PIECES * WIDE] += dot_tn(grad_packed, normed_ref[0])
-    part = dot(grad_packed, w_ref[0, : PIECES * WIDE])[None]
-
-    @pl.when(pair == 0)
+    d_w_ref[: PIECES * WIDE] += dot_tn(grad_packed, normed_ref[0])
+    part = dot(grad_packed, w_ref[: PIECES * WIDE])[None]
+
+    @pl.when(first_pair)
     def _():
         grad_normed[here] = part
 
-    @pl.when(pair > 0)
+    @pl.when(jnp.logical_not(first_pair))
     def _():
         grad_normed[here] += part
 
-    @pl.when(pair == pl.num_programs(0) - 1)
+    @pl.when(last_pair)
     def _():
         rows = dot(reorder((ROWS, TPC), 0), x_ref[0])
         pulled, d_gain = norm_pull(rows, gain_ref[...], grad_normed[here][0])
@@ -314,6 +329,264 @@
         @pl.when(clip > 0)
         def _():
             d_gain_ref[...] += d_gain
+
+
+class Scatter:
+    def __init__(self, name, order, source, total, from_core, from_one, from_two, from_z, result, out, links, sem, here):
+        self.name, self.order, self.links, self.here = name, order, links, here
+        self.total, self.from_core, self.from_one, self.from_two, self.from_z = (
+            total, from_core, from_one, from_two, from_z
+        )
+        self.result = result
+        z, y, core, x, beside, above, sibling, along = here
+        links.add(name + "c", source.at[:, :, 1 - core], from_core, sibling)
+        self.own = pltpu.make_async_copy(source.at[:, :, core], total, sem.at[0])
+        self.done = pltpu.make_async_copy(result, out, sem.at[1])
+        if order == "xyz":
+            links.add(name + "x", total.at[:, :, 1 - x], from_one, beside)
+            links.add(name + "y", total.at[:, 1 - y, x], from_two, above)
+            for shift in (1, 2, 3):
+                links.add(f"{name}z{shift}", total.at[turn(z, shift), y, x], from_z.at[shift - 1], along[shift - 1])
+        else:
+            links.add(name + "y", total.at[:, 1 - y], from_one, above)
+            for shift in (1, 2, 3):
+                links.add(f"{name}z{shift}", total.at[turn(z, shift), y], from_z.at[shift - 1], along[shift - 1])
+            links.add(name + "x", total.at[z, y, 1 - x], from_two, beside)
+
+    def stage(self, axis):
+        return [f"{self.name}z{shift}" for shift in (1, 2, 3)] if axis == "z" else [self.name + axis]
+
+    def begin(self):
+        self.links.start(self.name + "c")
+        self.own.start()
+
+    def step(self, at):
+        z, y, core, x = self.here[:4]
+        total = self.total
+        axis = ("c" + self.order)[at]
+        self.links.arrived(*self.stage(axis))
+        if axis == "c":
+            self.own.wait()
+
+            @pl.loop(0, 4)
+            def _(row):
+                for column in (0, 1):
+                    for head in (0, 1):
+                        total[row, column, head] = add_low(total[row, column, head], self.from_core[row, column, head])
+
+        elif at == 1:
+
+            @pl.loop(0, 4)
+            def _(row):
+                for other in (0, 1):
+                    spot = (row, other, x) if self.order == "xyz" else (row, y, other)
+                    total[spot] = add_low(total[spot], self.from_one[row, other])
+
+        elif axis == "y":
+
+            @pl.loop(0, 4)
+            def _(row):
+                total[row, y, x] = add_low(total[row, y, x], self.from_two[row])
+
+        elif axis == "z" and at == 2:
+            for head in (0, 1):
+                part = total[z, y, head].astype(F32)
+                for shift in range(3):
+                    part = part + self.from_z[shift, head].astype(F32)
+                total[z, y, head] = part.astype(BF16)
+        else:
+            part = total[z, y, x].astype(F32)
+            if axis == "z":
+                for shift in range(3):
+                    part = part + self.from_z[shift].astype(F32)
+            else:
+                part = part + self.from_two[...].astype(F32)
+            self.result[...] = part
+            self.done.start()
+        if at < 3:
+            self.links.start(*self.stage(self.order[at]))
+
+
+def add_low(one, other):
+    return (one.astype(F32) + other.astype(F32)).astype(BF16)
+
+
+def unpad(ref, into, more=None):
+    for piece in range(ref.shape[0] // WIDE):
+        rows = ref[WIDE * piece : WIDE * piece + HD]
+        narrow = slice(HD * piece, HD * (piece + 1))
+        if more is not None:
+            rows = rows + more[narrow].astype(F32)
+        into[narrow] = rows.astype(BF16)
+
+
+BACKWARD_COPIES = 48
+THIRD = 384
+PART = 96
+
+
+def backward_links_kernel(
+    x_ref, w_ref, mem_ref, side_ref, main_ref, taps_ref, gain_ref,
+    packed_ref, keys_ref, att_ref, log_ref, normed_ref, grad_ref, grad_low_ref, gain_two_ref,
+    d_first, d_second,
+    d_x_ref, small_out, first_out, second_out, w_out,
+    grad_normed, d_gain, d_w, d_taps,
+    far_sent, far_got, own, own_core, own_y, own_z, whole,
+    small_mine, small_far, small_x, small_core, small_y, small_z,
+    first_total, first_core, first_one, first_two, first_z, first_result,
+    second_total, second_core, second_one, second_two, second_z, second_result,
+    send, recv, near,
+):
+    step = pl.program_id(0)
+    last = pl.num_programs(0) - 1
+    z, y, core, x, at = place()
+    links = Links(send, recv)
+    beside, above, sibling = at(z, y, core, 1 - x), at(z, 1 - y, core, x), at(z, y, 1 - core, x)
+    along = [at(turn(z, shift), y, core, x) for shift in (1, 2, 3)]
+    here = (z, y, core, x, beside, above, sibling, along)
+    first = Scatter(
+        "f", "xyz", d_first, first_total, first_core, first_one, first_two, first_z, first_result, first_out,
+        links, near.at[pl.ds(0, 2)], here,
+    )
+    second = Scatter(
+        "s", "yzx", d_second, second_total, second_core, second_one, second_two, second_z, second_result, second_out,
+        links, near.at[pl.ds(2, 2)], here,
+    )
+
+    def lanes(core):
+        return pl.ds(pl.multiple_of(core * THIRD, THIRD), THIRD)
+
+    def rows(y, z):
+        return pl.ds(pl.multiple_of(y * THIRD + z * PART, PART), PART)
+
+    def half(y):
+        return pl.ds(pl.multiple_of(y * THIRD, THIRD), THIRD)
+
+    for i in (0, 1):
+        links.add(f"far{i}", far_sent.at[i], far_got.at[i], beside)
+        links.add(f"rc{i}", own.at[i, :, lanes(1 - core)], own_core.at[i], sibling)
+        links.add(f"ry{i}", own.at[i, half(1 - y), lanes(core)], own_y.at[i], above)
+        for shift in (1, 2, 3):
+            links.add(
+                f"rz{i}{shift}", own.at[i, rows(y, turn(z, shift)), lanes(core)], own_z.at[i, shift - 1], along[shift - 1]
+            )
+        piece = whole.at[i, rows(y, z), lanes(core)]
+        for shift in (1, 2, 3):
+            links.add(f"gz{i}{shift}", piece, piece, along[shift - 1])
+        piece = whole.at[i, half(y), lanes(core)]
+        links.add(f"gy{i}", piece, piece, above)
+        piece = whole.at[i, :, lanes(core)]
+        links.add(f"gc{i}", piece, piece, sibling)
+    links.add("mx", small_far, small_x, beside)
+    links.add("mc", small_mine, small_core, sibling)
+    links.add("my", small_core, small_y, above)
+    for shift in (1, 2, 3):
+        links.add(f"mz{shift}", small_z.at[z], small_z.at[z], along[shift - 1])
+
+    @pl.when(step == 0)
+    def _():
+        greet([beside, above, sibling] + along)
+        first.begin()
+        second.begin()
+
+    backward_step(
+        lax.rem(step, 4), step < 4, step >= 12,
+        w_ref.at[0], d_w, d_taps.at[lax.div(step, 4)],
+        x_ref, mem_ref, side_ref, main_ref, taps_ref, gain_ref,
+        packed_ref, keys_ref, att_ref, log_ref, normed_ref, grad_ref, grad_low_ref,
+        d_x_ref, d_gain, grad_normed,
+    )
+
+    def sum_core(i):
+        links.arrived(f"rc{i}")
+        own[i, :, lanes(core)] = add_low(own[i, :, lanes(core)], own_core[i])
+        links.start(f"ry{i}")
+
+    def sum_y(i):
+        links.arrived(f"ry{i}")
+        own[i, half(y), lanes(core)] = add_low(own[i, half(y), lanes(core)], own_y[i])
+        links.start(*[f"rz{i}{shift}" for shift in (1, 2, 3)])
+
+    def sum_z(i):
+        links.arrived(*[f"rz{i}{shift}" for shift in (1, 2, 3)])
+        part = own[i, rows(y, z), lanes(core)].astype(F32)
+        for shift in range(3):
+            part = part + own_z[i, shift].astype(F32)
+        whole[i, rows(y, z), lanes(core)] = part.astype(BF16)
+        links.start(*[f"gz{i}{shift}" for shift in (1, 2, 3)])
+
+    def spread_y(i):
+        links.arrived(*[f"gz{i}{shift}" for shift in (1, 2, 3)])
+        links.start(f"gy{i}")
+
+    def spread_core(i):
+        links.arrived(f"gy{i}")
+        links.start(f"gc{i}")
+
+    def far(i):
+        unpad(d_w, far_sent.at[i])
+        links.start(f"far{i}")
+
+    def mine(i):
+        links.arrived(f"far{i}")
+        unpad(d_w, own.at[i], far_got.at[i])
+        links.start(f"rc{i}")
+
+    plan = {
+        1: [lambda: first.step(0)],
+        2: [lambda: second.step(0)],
+        3: [lambda: far(0)],
+        7: [lambda: far(1), lambda: first.step(1)],
+        8: [lambda: second.step(1)],
+        10: [lambda: first.step(2)],
+        11: [lambda: mine(0)],
+        12: [lambda: sum_core(0)],
+        13: [lambda: sum_y(0), lambda: first.step(3)],
+        14: [lambda: sum_z(0), lambda: second.step(2)],
+    }
+    for when, acts in plan.items():
+
+        @pl.when(step == when)
+        def _(acts=acts):
+            for act in acts:
+                act()
+
+    @pl.when(step == last)
+    def _():
+        mine(1)
+        for i, target in ((2, small_mine), (0, small_far)):
+            target[...] = jnp.zeros_like(target)
+            target[0:1] = d_gain[...]
+            target[1:2] = gain_two_ref[...]
+            for j in (0, 1):
+                target[8:16, WIDE * j : WIDE * (j + 1)] = d_taps[i + j].reshape(8, WIDE)
+        links.start("mx")
+        spread_y(0)
+        sum_core(1)
+        links.arrived("mx")
+        small_mine[...] += small_x[...]
+        links.start("mc")
+        spread_core(0)
+        sum_y(1)
+        links.arrived("mc")
+        small_core[...] += small_mine[...]
+        links.start("my")
+        second.step(3)
+        sum_z(1)
+        links.arrived("my")
+        small_z[pl.ds(z, 1)] = (small_y[...] + small_core[...])[None]
+        links.start("mz1", "mz2", "mz3")
+        spread_y(1)
+        spread_core(1)
+        links.arrived("mz1", "mz2", "mz3")
+        small_out[...] = (small_z[0] + small_z[1]) + (small_z[2] + small_z[3])
+        links.arrived("gc0", "gc1")
+        save = pltpu.make_async_copy(whole, w_out, near.at[4])
+        save.start()
+        save.wait()
+        first.done.wait()
+        second.done.wait()
+        links.sent()
 
 
 VMEM_LIMIT = 60 << 20
@@ -727,6 +1000,98 @@
     )(x, w, mem, side, main, taps, gain, packed, keys, att, log, normed, grad, grad_low)
 
 
+def attention_backward_links(
+    x, w, mem, side, main, taps, gain, packed, keys, att, log, normed, grad, grad_low, gain_two, d_first, d_second
+):
+    clips, width = x.shape[0], x.shape[2]
+    packed_width = PIECES * WIDE
+    weight_rows = w.shape[1]
+    low_rows = weight_rows // WIDE * HD
+    pair_at = lambda s: lax.rem(lax.div(s, 4) + 2, 4)
+    clip_at = lambda s: lax.rem(s, 4)
+    late = lambda s: jnp.where(s < 12, 0, s - 12)
+    anywhere = pl.BlockSpec(memory_space=pl.ANY)
+    per_step = lambda s: (pair_at(s), clip_at(s), 0, 0)
+    small = (16, width)
+
+    def scatter_scratch(shape, order):
+        one, two, last = ((4, 2), (4,), (3,)) if order == "xyz" else ((4, 2), (), (3, 2))
+        return [
+            pltpu.VMEM(lead + shape, BF16) for lead in ((4, 2, 2), (4, 2, 2), one, two, last)
+        ] + [pltpu.VMEM(shape, F32)]
+
+    first_shape, second_shape = d_first.shape[4:], d_second.shape[4:]
+    return pl.pallas_call(
+        backward_links_kernel,
+        grid=(4 * clips,),
+        in_specs=[
+            pl.BlockSpec((1, TPC, width), lambda s: (late(s), 0, 0)),
+            pl.BlockSpec((1, weight_rows, width), lambda s: (pair_at(s), 0, 0)),
+            pl.BlockSpec(
+                (None, 1, PAIR, 2 * HD, MAIN),
+                lambda s: (lax.div(pair_at(s), 2), clip_at(s), lax.rem(pair_at(s), 2), 0, 0),
+            ),
+            pl.BlockSpec((1, 1, SIDE), lambda s: (clip_at(s), 0, 0)),
+            pl.BlockSpec((1, 1, MAIN), lambda s: (clip_at(s), 0, 0)),
+            pl.BlockSpec((1, PAIR, 4, WIDE), lambda s: (pair_at(s), 0, 0, 0)),
+            pl.BlockSpec((1, width), lambda s: (0, 0)),
+            pl.BlockSpec((1, 1, ROWS, packed_width), per_step),
+            pl.BlockSpec((1, 1, PAIR, 2, SIDE, WIDE), lambda s: per_step(s) + (0, 0)),
+            pl.BlockSpec((1, 1, ROWS, PAIR * WIDE), per_step),
+            pl.BlockSpec((1, 1, ROWS, WIDE), per_step),
+            pl.BlockSpec((1, ROWS, width), lambda s: (clip_at(s), 0, 0)),
+            pl.BlockSpec((ROWS, width), lambda s: (late(s), 0)),
+            pl.BlockSpec((ROWS, width), lambda s: (clip_at(s), 0)),
+            pl.BlockSpec((1, width), lambda s: (0, 0)),
+            anywhere,
+            anywhere,
+        ],
+        out_specs=[
+            pl.BlockSpec((1, TPC, width), lambda s: (late(s), 0, 0)),
+            pl.BlockSpec(small, lambda s: (0, 0)),
+            anywhere,
+            anywhere,
+            anywhere,
+        ],
+        out_shape=[
+            shaped((clips, TPC, width), BF16),
+            shaped(small, F32),
+            shaped(first_shape, F32),
+            shaped(second_shape, F32),
+            shaped((2, low_rows, width), BF16),
+        ],
+        scratch_shapes=[
+            pltpu.VMEM((clips, ROWS, width), F32),
+            pltpu.VMEM((1, width), F32),
+            pltpu.VMEM((weight_rows, width), F32),
+            pltpu.VMEM((4, PAIR, 4, WIDE), F32),
+            pltpu.VMEM((2, low_rows, width), BF16),
+            pltpu.VMEM((2, low_rows, width), BF16),
+            pltpu.VMEM((2, low_rows, width), BF16),
+            pltpu.VMEM((2, low_rows, THIRD), BF16),
+            pltpu.VMEM((2, THIRD, THIRD), BF16),
+            pltpu.VMEM((2, 3, PART, THIRD), BF16),
+            pltpu.VMEM((2, low_rows, width), BF16),
+        ]
+        + [pltpu.VMEM(small, F32)] * 5
+        + [pltpu.VMEM((4,) + small, F32)]
+        + scatter_scratch(first_shape, "xyz")
+        + scatter_scratch(second_shape, "yzx")
+        + [
+            pltpu.SemaphoreType.DMA((BACKWARD_COPIES,)),
+            pltpu.SemaphoreType.DMA((BACKWARD_COPIES,)),
+            pltpu.SemaphoreType.DMA((5,)),
+        ],
+        compiler_params=pltpu.CompilerParams(
+            dimension_semantics=("arbitrary",),
+            vmem_limit_bytes=VMEM_LIMIT,
+            collective_id=1,
+            has_side_effects=True,
+        ),
+        name="attention_backward_links",
+    )(x, w, mem, side, main, taps, gain, packed, keys, att, log, normed, grad, grad_low, gain_two, d_first, d_second)
+
+
 def group_gather(own, heads, fetch=None):
     blocks = [fetch(own, 0) if fetch else own]
     for shift in range(1, heads):
@@ -837,6 +1202,30 @@
         middle.reshape(clips * ROWS, width),
         gain_two,
     )
+    if linked:
+        d_x, small, d_first, d_second, d_w = attention_backward_links(
+            x, w_all, mem_all, side_mask, main_mask, taps_all, gain_one,
+            packed, keys, att, log, normed, grad, grad_low, d_gain_two,
+            d_first.reshape(4, 2, 2, 2, -1, d_first.shape[1]), d_second.reshape(4, 2, 2, 2, -1, width),
+        )
+        qkv_rows = PAIR * 3 * HD
+        d_qkv = d_w[:, :qkv_rows].astype(F32).reshape(own_heads, 3 * HD, width)
+        d_proj = d_w[:, qkv_rows:].astype(F32).reshape(own_heads, HD, width)
+        d_taps = small[8:, : 2 * WIDE].reshape(PAIR, 4, 2, WIDE).transpose(2, 0, 1, 3)[..., :HD]
+        share = width // (batches * heads)
+        start = (lax.axis_index("batch") * heads + me) * share
+        d_gains = lax.dynamic_slice_in_dim(small[:2], start, share, axis=1)
+        return (
+            outputs.reshape(inputs.shape),
+            d_x.reshape(inputs.shape),
+            d_qkv.transpose(2, 0, 1),
+            d_proj,
+            d_taps.reshape(own_heads, 4, HD),
+            d_gains[0],
+            d_gains[1],
+            d_first,
+            d_second,
+        )
     d_x, d_w, d_taps, d_gain_one = attention_backward(
         x, w_all, mem_all, side_mask, main_mask, taps_all, gain_one,
         packed, keys, att, log, normed, grad, grad_low,

time: 599 us -> 376 us (0.63)
  waiting for transfers between devices: 195 us -> 0 us
  blocking collectives: 80.5 us -> 0 us
  Pallas kernels: 274 us -> 349 us
  between operations: 15.7 us -> 0.73 us
  other arithmetic: 15 us -> 7.7 us
    reduce_scatter x2 -> x0, waiting for transfers between devices: 108 us -> none  [the longest x1 108 us: local(): lax.psum_scatter(d_second, both, scatter_dimension=0, tiled=True)]
    pallas_call x1, Pallas kernels: 71.1 us -> 146 us  [attention_backward_links(): pl.pallas_call(backward_links_kernel, grid=(4 * clips,), in_specs=[pl.Blo...]
    ppermute x3 -> x0, waiting for transfers between devices: 48.8 us -> none  [group_sum(): lax.ppermute(blocks[shift].astype(BF16), 'head', [(src, (src + shift) % h...]
    unnamed x1 -> x0, blocking collectives: 47.9 us -> none
    psum x1 -> x0, waiting for transfers between devices: 37.1 us -> none  [local(): lax.psum(group_sum(list(grads), heads).astype(BF16), 'batch').astype(F32)]
    psum x1 -> x0, blocking collectives: 32.6 us -> none  [local(): lax.psum(group_sum(list(grads), heads).astype(BF16), 'batch').astype(F32)]
  transfers between devices with their start and end apart: 6 -> 0, of which waited for: 3 -> 0; matrix products, arithmetic and copies ran while one was open for 2% -> 0% of each run, Pallas kernels for 0% -> 0%
where the time goes in v3:
time: 376 us; the launch traced here: 374 us
  Pallas kernels  349 us (93%)
  local copies, waits for them, and re-layouts  17.1 us (5%)
  other arithmetic  7.7 us (2%)
    pallas_call x1, Pallas kernels, attention_backward_links(): pl.pallas_call(backward_links_kernel, grid=(4 * clips,), in_specs=[pl.Blo...  146 us
    pallas_call x1, Pallas kernels, attention_forward_links(): pl.pallas_call(forward_links_kernel, grid=(4 * clips,), in_specs=[pl.Bloc...  122 us
    pallas_call x1, Pallas kernels, mlp(): pl.pallas_call(mlp_kernel, grid=(hidden // tile,), in_specs=[once((rows,...  80.9 us

profile of v3, /device:TPU:0, one launch (start us, length us, event | category | flops | bytes accessed | tf_op | source)
XLA Modules:
  0.0 374.2 jit_solution(8729893579928016788)
XLA Ops:
  0.7 0.7 broadcast_compare_fusion
  1.4 0.7 or_select_fusion.side_ref
  2.0 1.3 reshape.272.gain_one_ref.gain_ref
  3.3 1.3 reshape.273.gain_two_ref.gain_ref
  4.6 0.7 compare_select_fusion.main_ref
  5.2 0.7 pad.20
  5.9 0.6 convert.6.taps_own
  6.5 1.1 pad.18
  7.7 1.6 slice.32
  9.2 0.7 copy.20
  9.9 0.7 pad_bitcast_fusion.tail_own
  10.6 1.7 pad.17
  12.3 1.9 pad_maximum_fusion.w_own
  14.1 122.0 %attention_forward_links.1 = (bf16[4,4,400,768]{3,2,1,0:T(8,128)(2,1)}, bf16[4,4,2,2,256,128]{5,4,3,2,1,0:T(8,128)(2,1)}, bf16[4,4,400,256]{3,2,1,0:T(8,128)(2,1...) custom-call(bf16[4,392,768]{2,1,0:T(8,128)(2,1)} %bitcast.44, ...), custom_call_target="tpu_custom_call" | custom-call | tf_op jit(solution)/shard_map/attention_forward_links/pallas_call | solution.py:800
  136.2 80.9 %mlp.1 = (bf16[4,392,768]{2,1,0:T(8,128)(2,1)}, f32[1600,768]{1,0:T(8,128)}, bf16[1600,768]{1,0:T(8,128)(2,1)}, bf16[768,3072]{1,0:T(8,128)(2,1)}, bf16[3072,768]{1,0:T(8,128)(2,1)}, /*index=5*/f32[1,768]{1,0:T(1,128)}) custom-call(bf16[1600,768]{1,0:T(8,128)(2,1)} %bitcast.55, bf16[4,392,768]{2,1,0:T(8,128)(2,1)} %bitcast.57, bf16[768,3072]{1,0:T(8,128)(2,1)} %bitcast.52, ...), custom_call_target="tpu_custom_call" | custom-call | tf_op jit(solution)/shard_map/mlp/pallas_call | solution.py:915
  217.1 145.7 %attention_backward_links.1 = (bf16[4,392,768]{2,1,0:T(8,128)(2,1)}, f32[16,768]{1,0:T(8,128)}, f32[24,3072]{1,0:T(8,128)}, f32[96,768]{1,0:T(8,128)}, bf16[2,768,768]{2,1,0:T(8,128)(2,1)}) custom-call(bf16[4,392,768]{2,1,0:T(8,128)(2,1)} %bitcast.45, bf16[4,1024,768]{2,1,0:T(8,128)(2,1)} %get-tuple-element.37.w_ref, ...), custom_call_target="tpu_custom_call" | custom-call | tf_op jit(solution)/shard_map/attention_backward_links/pallas_call | solution.py:1024
  362.8 0.7 slice.29
  363.6 0.7 slice.27
  364.3 0.1 constant_dynamic-slice_fusion
  364.3 0.6 copy.21
  364.9 0.5 slice_bitcast_fusion
  365.5 1.1 slice.26
  366.6 1.6 slice.25
  368.2 0.0 copy-start
  368.2 1.1 convert.8
  369.3 2.1 convert_bitcast_fusion
  371.4 0.0 copy-done
  371.4 1.4 copy.27
  372.8 0.0 copy-done.2
  372.8 0.7 copy.28
  373.5 0.0 copy-done.1
  373.5 0.7 copy.29
  (5 shorter events, 0.0 us)
Async XLA Ops:
  368.2 3.2 copy-start
  371.4 1.4 copy-start.2
  371.4 2.1 copy-start.1

commit v4 on v3

--- a/solution.py
+++ b/solution.py
@@ -67,30 +67,46 @@
     return pulled, jnp.sum(grad * unit, axis=0, keepdims=True)
 
 
+def as_row(ref):
+    return ref[...].reshape(1, -1)
+
+
+def widen(taps):
+    return jnp.concatenate([taps, jnp.zeros((taps.shape[0], WIDE - taps.shape[1]), F32)], axis=1)
+
+
+def mask_rows(index):
+    slot = lax.broadcasted_iota(jnp.int32, (1, MAIN), 1) // PTOK
+    main = jnp.where(index > slot, 0.0, NEG)
+    spot = lax.broadcasted_iota(jnp.int32, (1, SIDE), 1)
+    tail_open = (spot >= HALF) & (spot < HALF + REST) & (index > (TPC - 1) // PTOK)
+    return jnp.where((spot < PTOK) | tail_open, 0.0, NEG), main
+
+
 def value_columns(memory_t):
     return jnp.concatenate([memory_t[HD:], jnp.zeros((WIDE - HD, memory_t.shape[1]), BF16)], axis=0)
 
 
 def forward_kernel(
-    x_ref, w_ref, mem_ref, tail_ref, side_ref, main_ref, taps_ref, gain_one_ref, gain_two_ref,
-    packed_ref, keys_ref, att_ref, log_ref, normed_ref, middle_ref, normed_two_ref,
-    x_rows, normed_rows, branch,
+    x_ref, cot_ref, w_ref, mem_ref, tail_ref, side_ref, main_ref, taps_ref, gain_one_ref, gain_two_ref,
+    packed_ref, keys_ref, att_ref, log_ref, normed_ref, middle_ref, normed_two_ref, cot_out,
+    x_rows, normed_rows, branch, logs,
 ):
     forward_step(
-        pl.program_id(0), pl.program_id(1), pl.num_programs(0),
-        w_ref.at[0], mem_ref.at[0], tail_ref.at[0], taps_ref.at[0],
-        x_ref, side_ref, main_ref, gain_one_ref, gain_two_ref,
-        packed_ref, keys_ref, att_ref, log_ref, normed_ref, middle_ref, normed_two_ref,
-        x_rows, normed_rows, branch,
+        pl.program_id(0), pl.program_id(1), pl.num_programs(0), (side_ref[0], main_ref[0]),
+        w_ref.at[0, : PIECES * WIDE], w_ref.at[0, PIECES * WIDE :], mem_ref.at[0], tail_ref.at[0], taps_ref.at[0],
+        x_ref, cot_ref, gain_one_ref, gain_two_ref,
+        packed_ref, keys_ref, att_ref, log_ref, normed_ref, middle_ref, normed_two_ref, cot_out,
+        x_rows, normed_rows, branch, logs,
     )
 
 
 def forward_step(
-    pair, clip, pairs,
-    w_ref, mem_ref, tail_ref, taps_ref,
-    x_ref, side_ref, main_ref, gain_one_ref, gain_two_ref,
-    packed_ref, keys_ref, att_ref, log_ref, normed_ref, middle_ref, normed_two_ref,
-    x_rows, normed_rows, branch,
+    pair, clip, pairs, masks,
+    qkv_ref, proj_ref, mem_ref, tail_ref, taps_ref,
+    x_ref, cot_ref, gain_one_ref, gain_two_ref,
+    packed_ref, keys_ref, att_ref, log_ref, normed_ref, middle_ref, normed_two_ref, cot_out,
+    x_rows, normed_rows, branch, log_rows,
 ):
     here = pl.ds(clip, 1)
 
@@ -99,12 +115,13 @@
         rows = dot(reorder((ROWS, TPC), 0), x_ref[0])
         x_rows[here] = rows.astype(BF16)[None]
         unit, _ = norm_parts(rows)
-        low = (unit * gain_one_ref[...]).astype(BF16)
+        low = (unit * as_row(gain_one_ref)).astype(BF16)
         normed_rows[here] = low[None]
         normed_ref[0] = low
+        log_rows[here] = jnp.zeros((1, ROWS, WIDE), F32)
 
     normed = normed_rows[here][0]
-    packed = dot_nt(normed, w_ref[: PIECES * WIDE])
+    packed = dot_nt(normed, qkv_ref[...].reshape(-1, normed.shape[1]))
     packed_ref[0, 0] = packed.astype(BF16)
     logs = []
     outs = []
@@ -114,7 +131,7 @@
         key = packed[:, base + WIDE : base + 2 * WIDE]
         value = packed[:, base + 2 * WIDE : base + 3 * WIDE]
         query_low = query.astype(BF16)
-        taps = taps_ref[head]
+        taps = widen(taps_ref[head])
         zeros = jnp.zeros((SIDE - HALF - REST, WIDE), F32)
         pooled_key = taps[0:1] * key[:HALF] + taps[1:2] * key[HALF:]
         pooled_value = taps[2:3] * value[:HALF] + taps[3:4] * value[HALF:]
@@ -124,8 +141,8 @@
         keys_ref[0, 0, head, 0] = side_key
         keys_ref[0, 0, head, 1] = side_value
         memory_t = mem_ref[head]
-        score_side = dot_nt(query_low, side_key) * (SCORE * LOG2E) + side_ref[0]
-        score_main = dot(query_low, memory_t[:WIDE]) * (SCORE * LOG2E) + main_ref[0]
+        score_side = dot_nt(query_low, side_key) * (SCORE * LOG2E) + masks[0]
+        score_main = dot(query_low, memory_t[:WIDE]) * (SCORE * LOG2E) + masks[1]
         top = jnp.maximum(
             jnp.max(score_side, axis=-1, keepdims=True), jnp.max(score_main, axis=-1, keepdims=True)
         )
@@ -139,9 +156,9 @@
         logs.append(top + jnp.log2(total))
     attended = jnp.concatenate(outs, axis=1).astype(BF16)
     att_ref[0, 0] = attended
-    lane = lax.broadcasted_iota(jnp.int32, (ROWS, WIDE), 1)
-    log_ref[0, 0] = jnp.where(lane == 0, logs[0], logs[1])
-    part = dot(attended, w_ref[PIECES * WIDE :])[None]
+    lane = lax.broadcasted_iota(jnp.int32, (ROWS, WIDE), 1) - PAIR * pair
+    log_rows[here] = jnp.where(lane == 0, logs[0], jnp.where(lane == 1, logs[1], log_rows[here][0]))[None]
+    part = dot(attended, proj_ref[...].reshape(-1, normed.shape[1]))[None]
 
     @pl.when(pair == 0)
     def _():
@@ -156,96 +173,101 @@
         middle = x_rows[here][0].astype(F32) + branch[here][0]
         middle_ref[0] = middle
         unit, _ = norm_parts(middle)
-        normed_two_ref[0] = (unit * gain_two_ref[...]).astype(BF16)
+        normed_two_ref[0] = (unit * as_row(gain_two_ref)).astype(BF16)
+        log_ref[0] = log_rows[here][0]
+        cot_out[0] = dot(reorder((ROWS, TPC), 0), cot_ref[0]).astype(BF16)
 
 
 def mlp_kernel(
     normed_ref, cot_ref, first_ref, second_ref, middle_ref, gain_ref,
-    out_ref, grad_ref, grad_low_ref, d_first_ref, d_second_ref, d_gain_ref,
-    cot_rows, cot_t, normed_t, total, grad_normed, active, grad_hidden,
+    out_ref, grad_ref, d_first_ref, d_second_ref, d_gain_ref,
+    middle, total, grad_normed, active, grad_hidden, near,
 ):
-    tile = pl.program_id(0)
-    clips = cot_ref.shape[0]
-    wide = normed_ref.shape[1]
-
-    @pl.when(tile == 0)
-    def _():
-        swap = reorder((ROWS, TPC), 0)
-
-        @pl.loop(0, clips)
-        def _(clip):
-            here = pl.ds(pl.multiple_of(clip * ROWS, ROWS), ROWS)
-            cot_rows[here, :] = dot(swap, cot_ref[clip]).astype(BF16)
-            total[here, :] = middle_ref[here, :]
-            grad_normed[here, :] = jnp.zeros((ROWS, wide), F32)
-
-        for lanes in range(0, wide, WIDE):
-            cot_t[lanes : lanes + WIDE, :] = cot_rows[:, lanes : lanes + WIDE].T
-            normed_t[lanes : lanes + WIDE, :] = normed_ref[:, lanes : lanes + WIDE].T
-
-    first = first_ref[...]
-    second = second_ref[...]
-
-    @pl.loop(0, clips)
-    def _(clip):
-        here = pl.ds(pl.multiple_of(clip * ROWS, ROWS), ROWS)
-        hidden = dot(normed_ref[here, :], first)
-        grad_active = dot_nt(cot_rows[here, :], second)
-        bell = jnp.exp2(hidden * hidden * (-0.5 * LOG2E))
-        step = 1.0 / (1.0 + (0.3275911 * math.sqrt(0.5)) * jnp.abs(hidden))
-        tail = step * (0.5 * 1.061405429) + (0.5 * -1.453152027)
-        tail = step * tail + (0.5 * 1.421413741)
-        tail = step * tail + (0.5 * -0.284496736)
-        tail = step * tail + (0.5 * 0.254829592)
-        tail = step * tail * bell
-        cumulative = jnp.where(hidden < 0.0, tail, 1.0 - tail)
-        slope = cumulative + hidden * bell * 0.3989422804014327
-        active_low = (hidden * cumulative).astype(BF16)
-        hidden_low = (slope * grad_active).astype(BF16)
-        active[here, :] = active_low
-        grad_hidden[here, :] = hidden_low
-        total[here, :] += dot(active_low, second)
-        grad_normed[here, :] += dot_nt(hidden_low, first)
-
-    d_first_ref[...] = dot(normed_t[...], grad_hidden[...]).astype(BF16)
-    d_second_ref[...] = dot(cot_t[...], active[...]).astype(BF16).T
-
-    @pl.when(tile == pl.num_programs(0) - 1)
-    def _():
-        back = reorder((TPC, ROWS), 1)
+    step = pl.program_id(0)
+    clips = middle.shape[0] // ROWS
+    tiles = pl.num_programs(0) - clips
+    fetch = pltpu.make_async_copy(middle_ref, middle, near.at[0])
+
+    @pl.when(step == 0)
+    def _():
+        fetch.start()
         d_gain_ref[...] = jnp.zeros_like(d_gain_ref)
 
-        @pl.loop(0, clips)
-        def _(clip):
-            here = pl.ds(pl.multiple_of(clip * ROWS, ROWS), ROWS)
-            out_ref[clip] = dot(back, total[here, :].astype(BF16)).astype(BF16)
-            pulled, d_gain = norm_pull(middle_ref[here, :], gain_ref[...], grad_normed[here, :])
-            grad = cot_rows[here, :].astype(F32) + pulled
-            grad_ref[here, :] = grad
-            grad_low_ref[here, :] = grad.astype(BF16)
-            d_gain_ref[...] += d_gain
+    @pl.when(step < tiles)
+    def _():
+        first = first_ref[...]
+        second = second_ref[...]
+
+        @pl.loop(0, middle.shape[0] // CHUNK)
+        def _(chunk):
+            here = pl.ds(pl.multiple_of(chunk * CHUNK, CHUNK), CHUNK)
+            hidden = dot(normed_ref[here, :], first)
+            grad_active = dot_nt(cot_ref[here, :], second)
+            bell = jnp.exp2(hidden * hidden * (-0.5 * LOG2E))
+            step_size = 1.0 / (1.0 + (0.3275911 * math.sqrt(0.5)) * jnp.abs(hidden))
+            tail = step_size * (0.5 * 1.061405429) + (0.5 * -1.453152027)
+            tail = step_size * tail + (0.5 * 1.421413741)
+            tail = step_size * tail + (0.5 * -0.284496736)
+            tail = step_size * tail + (0.5 * 0.254829592)
+            tail = step_size * tail * bell
+            cumulative = jnp.where(hidden < 0.0, tail, 1.0 - tail)
+            slope = cumulative + hidden * bell * 0.3989422804014327
+            active_low = (hidden * cumulative).astype(BF16)
+            hidden_low = (slope * grad_active).astype(BF16)
+            active[here, :] = active_low
+            grad_hidden[here, :] = hidden_low
+            fed = dot(active_low, second)
+            back = dot_nt(hidden_low, first)
+
+            @pl.when(step == 0)
+            def _():
+                total[here, :] = fed
+                grad_normed[here, :] = back
+
+            @pl.when(step > 0)
+            def _():
+                total[here, :] += fed
+                grad_normed[here, :] += back
+
+        d_first_ref[...] = dot_tn(normed_ref[...], grad_hidden[...]).astype(BF16)
+        d_second_ref[...] = dot_tn(active[...], cot_ref[...]).astype(BF16)
+
+    @pl.when(step == tiles)
+    def _():
+        fetch.wait()
+
+    @pl.when(step >= tiles)
+    def _():
+        here = pl.ds(pl.multiple_of((step - tiles) * ROWS, ROWS), ROWS)
+        values = middle[here, :]
+        out = (values + total[here, :]).astype(BF16)
+        out_ref[0] = dot(reorder((TPC, ROWS), 1), out).astype(BF16)
+        pulled, d_gain = norm_pull(values, as_row(gain_ref), grad_normed[here, :])
+        grad_ref[...] = (cot_ref[here, :].astype(F32) + pulled).astype(BF16)
+        d_gain_ref[...] += d_gain
 
 
 def backward_kernel(
     x_ref, w_ref, mem_ref, side_ref, main_ref, taps_ref, gain_ref,
-    packed_ref, keys_ref, att_ref, log_ref, normed_ref, grad_ref, grad_low_ref,
+    packed_ref, keys_ref, att_ref, log_ref, normed_ref, grad_ref,
     d_x_ref, d_w_ref, d_taps_ref, d_gain_ref,
     grad_normed,
 ):
     backward_step(
-        pl.program_id(1), pl.program_id(0) == 0, pl.program_id(0) == pl.num_programs(0) - 1,
-        w_ref.at[0], d_w_ref.at[0], d_taps_ref.at[0],
-        x_ref, mem_ref, side_ref, main_ref, taps_ref, gain_ref,
-        packed_ref, keys_ref, att_ref, log_ref, normed_ref, grad_ref, grad_low_ref,
+        pl.program_id(0), pl.program_id(1), pl.program_id(0) == 0, pl.program_id(0) == pl.num_programs(0) - 1,
+        (side_ref[0], main_ref[0]),
+        w_ref.at[0, : PIECES * WIDE], w_ref.at[0, PIECES * WIDE :], d_w_ref.at[0], d_taps_ref.at[0],
+        x_ref, mem_ref, taps_ref, gain_ref,
+        packed_ref, keys_ref, att_ref, log_ref, normed_ref, grad_ref,
         d_x_ref, d_gain_ref, grad_normed,
     )
 
 
 def backward_step(
-    clip, first_pair, last_pair,
-    w_ref, d_w_ref, d_taps_ref,
-    x_ref, mem_ref, side_ref, main_ref, taps_ref, gain_ref,
-    packed_ref, keys_ref, att_ref, log_ref, normed_ref, grad_ref, grad_low_ref,
+    pair, clip, first_pair, last_pair, masks,
+    qkv_ref, proj_ref, d_w_ref, d_taps_ref,
+    x_ref, mem_ref, taps_ref, gain_ref,
+    packed_ref, keys_ref, att_ref, log_ref, normed_ref, grad_ref,
     d_x_ref, d_gain_ref, grad_normed,
 ):
     here = pl.ds(clip, 1)
@@ -255,8 +277,10 @@
         d_w_ref[...] = jnp.zeros_like(d_w_ref)
         d_taps_ref[...] = jnp.zeros_like(d_taps_ref)
 
-    grad_branch = grad_low_ref[...]
-    grad_out = dot_nt(grad_branch, w_ref[PIECES * WIDE :])
+    grad_branch = grad_ref[...]
+    lane = lax.broadcasted_iota(jnp.int32, (ROWS, WIDE), 1) - PAIR * pair
+    width = grad_branch.shape[1]
+    grad_out = dot_nt(grad_branch, proj_ref[...].reshape(-1, width))
     d_w_ref[PIECES * WIDE :] += dot_tn(att_ref[0, 0], grad_branch)
     pieces = []
     for head in range(PAIR):
@@ -265,13 +289,13 @@
         key = packed_ref[0, 0, :, base + WIDE : base + 2 * WIDE].astype(F32)
         value = packed_ref[0, 0, :, base + 2 * WIDE : base + 3 * WIDE].astype(F32)
         out_grad = grad_out[:, WIDE * head : WIDE * (head + 1)].astype(BF16)
-        taps = taps_ref[0, head]
+        taps = widen(taps_ref[0, head])
         side_key = keys_ref[0, 0, head, 0]
         side_value = keys_ref[0, 0, head, 1]
         memory_t = mem_ref[0, head]
-        log = log_ref[0, 0, :, head : head + 1]
-        score_side = dot_nt(query, side_key) * (SCORE * LOG2E) + side_ref[0]
-        score_main = dot(query, memory_t[:WIDE]) * (SCORE * LOG2E) + main_ref[0]
+        log = jnp.sum(jnp.where(lane == head, log_ref[0], 0.0), axis=-1, keepdims=True)
+        score_side = dot_nt(query, side_key) * (SCORE * LOG2E) + masks[0]
+        score_main = dot(query, memory_t[:WIDE]) * (SCORE * LOG2E) + masks[1]
         weight_side = jnp.exp2(score_side - log)
         weight_main = jnp.exp2(score_main - log)
         grad_side = dot_nt(out_grad, side_value)
@@ -305,7 +329,7 @@
         )
     grad_packed = jnp.concatenate(pieces, axis=1).astype(BF16)
     d_w_ref[: PIECES * WIDE] += dot_tn(grad_packed, normed_ref[0])
-    part = dot(grad_packed, w_ref[: PIECES * WIDE])[None]
+    part = dot(grad_packed, qkv_ref[...].reshape(-1, width))[None]
 
     @pl.when(first_pair)
     def _():
@@ -318,8 +342,8 @@
     @pl.when(last_pair)
     def _():
         rows = dot(reorder((ROWS, TPC), 0), x_ref[0])
-        pulled, d_gain = norm_pull(rows, gain_ref[...], grad_normed[here][0])
-        d_x = (grad_ref[...] + pulled).astype(BF16)
+        pulled, d_gain = norm_pull(rows, as_row(gain_ref), grad_normed[here][0])
+        d_x = (grad_branch.astype(F32) + pulled).astype(BF16)
         d_x_ref[0] = dot(reorder((TPC, ROWS), 1), d_x).astype(BF16)
 
         @pl.when(clip == 0)
@@ -426,8 +450,8 @@
 
 
 def backward_links_kernel(
-    x_ref, w_ref, mem_ref, side_ref, main_ref, taps_ref, gain_ref,
-    packed_ref, keys_ref, att_ref, log_ref, normed_ref, grad_ref, grad_low_ref, gain_two_ref,
+    index_ref, x_ref, qkv_ref, proj_ref, mem_ref, taps_ref, gain_ref,
+    packed_ref, keys_ref, att_ref, log_ref, normed_ref, grad_ref, gain_two_ref,
     d_first, d_second,
     d_x_ref, small_out, first_out, second_out, w_out,
     grad_normed, d_gain, d_w, d_taps,
@@ -490,10 +514,11 @@
         second.begin()
 
     backward_step(
-        lax.rem(step, 4), step < 4, step >= 12,
-        w_ref.at[0], d_w, d_taps.at[lax.div(step, 4)],
-        x_ref, mem_ref, side_ref, main_ref, taps_ref, gain_ref,
-        packed_ref, keys_ref, att_ref, log_ref, normed_ref, grad_ref, grad_low_ref,
+        lax.rem(lax.div(step, 4) + 2, 4), lax.rem(step, 4), step < 4, step >= 12,
+        mask_rows(index_ref[x, lax.rem(step, 4)]),
+        qkv_ref.at[0], proj_ref.at[0], d_w, d_taps.at[lax.div(step, 4)],
+        x_ref, mem_ref, taps_ref, gain_ref,
+        packed_ref, keys_ref, att_ref, log_ref, normed_ref, grad_ref,
         d_x_ref, d_gain, grad_normed,
     )
 
@@ -606,12 +631,12 @@
     def __init__(self, send, recv):
         self.send, self.recv, self.made = send, recv, {}
 
-    def add(self, name, src, dst, device):
+    def add(self, name, src, dst, device, send_if=None, recv_if=None):
         at = len(self.made)
-        self.made[name] = (src, dst, device, at)
+        self.made[name] = (src, dst, device, at, send_if, recv_if)
 
     def get(self, name):
-        src, dst, device, at = self.made[name]
+        src, dst, device, at = self.made[name][:4]
         return pltpu.make_async_remote_copy(
             src_ref=src,
             dst_ref=dst,
@@ -623,15 +648,21 @@
 
     def start(self, *names):
         for name in names:
-            self.get(name).start()
+            self.only(self.made[name][4], self.get(name).start)
 
     def arrived(self, *names):
         for name in names:
-            self.get(name).wait_recv()
+            self.only(self.made[name][5], self.get(name).wait_recv)
 
     def sent(self):
         for name in self.made:
-            self.get(name).wait_send()
+            self.only(self.made[name][4], self.get(name).wait_send)
+
+    def only(self, condition, act):
+        if condition is None:
+            act()
+        else:
+            pl.when(condition)(lambda: act())
 
 
 def place():
@@ -655,61 +686,74 @@
     return lax.rem(z + shift + 4, 4)
 
 
-FORWARD_COPIES = 48
+FORWARD_COPIES = 96
+SPLIT = HD // 2
 
 
 def forward_links_kernel(
-    x_ref, side_ref, main_ref, gain_one_ref, gain_two_ref,
-    w_own, mem_own, tail_own, taps_own, hidden_own, output_own,
-    packed_ref, keys_ref, att_ref, log_ref, normed_ref, middle_ref, normed_two_ref,
-    first_all, second_all, w_out, mem_out, taps_out,
-    x_rows, normed_rows, branch, w_all, mem_all, tail_all, taps_all,
+    index_ref, x_ref, cot_ref, gain_one_ref, gain_two_ref,
+    qkv_own, proj_own, mem_own, tail_own, taps_own, hidden_own, output_own,
+    packed_ref, keys_ref, att_ref, log_ref, normed_ref, middle_ref, normed_two_ref, cot_out,
+    first_all, second_all, qkv_out, proj_out, mem_out, taps_out,
+    x_rows, normed_rows, branch, logs, qkv_all, proj_all, mem_all, tail_all, taps_all,
     send, recv, near, save,
 ):
     step = pl.program_id(0)
     z, y, core, x, at = place()
     links = Links(send, recv)
     beside, above, sibling = at(z, y, core, 1 - x), at(z, 1 - y, core, x), at(z, y, 1 - core, x)
-    along = [at(turn(z, shift), y, core, x) for shift in (1, 2, 3)]
+    higher, lower = at(turn(z, 1), y, core, x), at(turn(z, -1), y, core, x)
     column = pl.ds(pl.multiple_of(core * MAIN, MAIN), MAIN)
-
-    def slab(z, y):
-        return (lax.div(2 * z + y, 4), pl.ds(pl.multiple_of(lax.rem(2 * z + y, 4) * 256, 256), 256), column)
-
-    def w_far(z, y):
-        pair, rows, lanes = slab(z, y)
-        return w_all.at[2 + pair, rows, lanes]
-
-    links.add("xw", w_own.at[slab(z, y)], w_far(z, y), beside)
-    for shift in (1, 2, 3):
-        links.add(f"zw{shift}", w_far(z, y), w_far(z, y), along[shift - 1])
-    for shift in range(4):
-        links.add(f"yw{shift}", w_far(turn(z, -shift), y), w_far(turn(z, -shift), y), above)
-    far = w_all.at[pl.ds(2, 2), :, column]
-    links.add("cw", far, far, sibling)
     me = ((z * 2 + y) * 2 + core) * 2 + x
+    clips = mem_own.shape[0]
+
+    def split(z, y, *between):
+        rows = pl.ds(pl.multiple_of(y * SPLIT, SPLIT), SPLIT)
+        return (lax.div(z, 2), lax.rem(z, 2)) + between + (rows, column)
+
+    def block(kind, z, y):
+        if kind == "q":
+            return qkv_all.at[pl.ds(2, 2)].at[split(z, y, slice(None))]
+        if kind == "p":
+            return proj_all.at[pl.ds(2, 2)].at[split(z, y)]
+        return (first_all if kind == "0" else second_all).at[pl.ds(((z * 2 + y) * 2 + core) * 2, 2)]
+
+    links.add("xq", qkv_own.at[split(z, y, slice(None))], block("q", z, y), beside)
+    links.add("xp", proj_own.at[split(z, y)], block("p", z, y), beside)
     links.add("x0", hidden_own, first_all.at[me], beside)
     links.add("x1", output_own, second_all.at[me], beside)
-
-    def group(which, z, y):
-        return (first_all, second_all)[which].at[pl.ds(((z * 2 + y) * 2 + core) * 2, 2)]
-
-    for which in (0, 1):
-        for shift in (1, 2, 3):
-            links.add(f"z{shift}{which}", group(which, z, y), group(which, z, y), along[shift - 1])
-        for shift in range(4):
-            from_z = turn(z, -shift)
-            links.add(f"y{shift}{which}", group(which, from_z, y), group(which, from_z, y), above)
-            links.add(f"c{shift}{which}", group(which, from_z, y), group(which, from_z, y), sibling)
-            links.add(f"d{shift}{which}", group(which, from_z, 1 - y), group(which, from_z, 1 - y), sibling)
-    clips = mem_own.shape[0]
+    for kind in "qp01":
+        mine = block(kind, z, y)
+        links.add("y" + kind, mine, mine, above)
+        if kind in "01":
+            links.add("c" + kind, mine, mine, sibling)
+            mine = block(kind, z, 1 - y)
+            links.add("e" + kind, mine, mine, sibling)
+        for hop in (1, 2, 3):
+            below, beyond = z >= hop, z + hop <= 3
+            passed = block(kind, turn(z, 1 - hop), y)
+            links.add(f"u{hop}{kind}", passed, passed, higher, (z <= 2) & (z >= hop - 1), below)
+            passed = block(kind, turn(z, hop - 1), y)
+            links.add(f"d{hop}{kind}", passed, passed, lower, (z >= 1) & (z + hop <= 4), beyond)
+            for side, shift, there in (("u", -hop, below), ("d", hop, beyond)):
+                came = block(kind, turn(z, shift), y)
+                links.add(f"y{side}{hop}{kind}", came, came, above, there, there)
+                if kind in "01":
+                    links.add(f"c{side}{hop}{kind}", came, came, sibling, there, there)
+                    came = block(kind, turn(z, shift), 1 - y)
+                    links.add(f"e{side}{hop}{kind}", came, came, sibling, there, there)
+    far = qkv_all.at[pl.ds(2, 2), :, :, pl.ds(0, HD), column]
+    links.add("cq", far, far, sibling)
+    far = proj_all.at[pl.ds(2, 2), :, pl.ds(0, HD), column]
+    links.add("cp", far, far, sibling)
     for clip in range(clips):
         links.add(f"m{clip}", mem_own.at[clip, 1 - x, :, :, pl.ds(0, MAIN)], mem_all.at[1, clip], beside)
     links.add("tail", tail_own.at[:, 1 - x], tail_all.at[1], beside)
     links.add("taps", taps_own, taps_all.at[pl.ds(2, 2)], beside)
 
     local = [
-        (w_own, w_all.at[pl.ds(0, 2)]),
+        (qkv_own, qkv_all.at[pl.ds(0, 2), :, :, pl.ds(0, HD)]),
+        (proj_own, proj_all.at[pl.ds(0, 2), :, pl.ds(0, HD)]),
         (tail_own.at[:, x], tail_all.at[0]),
         (taps_own, taps_all.at[pl.ds(0, 2)]),
         (hidden_own, first_all.at[me]),
@@ -717,68 +761,110 @@
     ] + [(mem_own.at[clip, x, :, :, pl.ds(0, MAIN)], mem_all.at[0, clip]) for clip in range(clips)]
     local = [pltpu.make_async_copy(src, dst, near.at[i]) for i, (src, dst) in enumerate(local)]
     saved = [
-        (w_all, w_out),
+        (qkv_all, qkv_out),
+        (proj_all, proj_out),
         (taps_all, taps_out),
         (mem_all.at[0], mem_out.at[0]),
-        (mem_all.at[1], mem_out.at[1]),
-    ]
+    ] + [(mem_all.at[1, clip], mem_out.at[1, clip]) for clip in range(clips)]
     saved = [pltpu.make_async_copy(src, dst, save.at[i]) for i, (src, dst) in enumerate(saved)]
 
     @pl.when(step == 0)
     def _():
-        greet([beside, above, sibling] + along)
-        links.start("xw", "taps", "tail", "x0", "x1")
+        greet([beside, above, sibling, higher, lower])
+        links.start("xq", "xp", "taps", "tail", "x0", "x1")
         for copy in local:
             copy.start()
+
+        @pl.loop(0, 4)
+        def _(pair):
+            for head in range(PAIR):
+                for piece in range(3):
+                    qkv_all[pair, head, piece, HD:] = jnp.zeros((WIDE - HD, qkv_all.shape[-1]), BF16)
+                proj_all[pair, head, HD:] = jnp.zeros((WIDE - HD, qkv_all.shape[-1]), BF16)
+
         for copy in local:
             copy.wait()
 
-    def both(*names):
-        return [name + str(which) for name in names for which in (0, 1)]
+    def hop(number, kinds):
+        for kind in kinds:
+            links.arrived(f"u{number}{kind}", f"d{number}{kind}")
+            if number < 3:
+                links.start(f"u{number + 1}{kind}", f"d{number + 1}{kind}")
+            links.start(f"yu{number}{kind}", f"yd{number}{kind}")
+            if kind in "01":
+                links.start(f"cu{number}{kind}", f"cd{number}{kind}")
+
+    def begin(kinds):
+        for kind in kinds:
+            links.arrived("x" + kind)
+            links.start("u1" + kind, "d1" + kind, "y" + kind)
+            if kind in "01":
+                links.start("c" + kind)
+
+    def across(number, kinds):
+        for kind in kinds:
+            for side in ("u", "d") if number else ("",):
+                name = f"{side}{number}{kind}" if number else kind
+                links.arrived("y" + name)
+                if kind in "01":
+                    links.start("e" + name)
+
+    def weights():
+        for number in range(4):
+            across(number, "qp")
+        links.start("cq", "cp")
+        links.arrived("cq", "cp", "tail", "taps")
+
+    def memory(clip):
+        links.arrived(f"m{clip}")
+        saved[4 + clip].start()
 
     plan = {
-        2: (["xw"], ["zw1", "zw2", "zw3", "yw0"]),
-        3: (["x0", "x1"], both("z1", "z2", "z3", "y0", "c0") + ["m0", "m1"]),
-        5: (["zw1", "zw2", "zw3"], ["yw1", "yw2", "yw3"]),
-        6: ([], ["m2", "m3"]),
-        7: (["yw0", "yw1", "yw2", "yw3"], ["cw"]),
-        8: (["cw", "tail", "taps", "m0"], []),
-        9: (both("z1"), both("y1", "c1")),
-        10: (["m1"] + both("z2"), both("y2", "c2")),
-        12: (["m2"], []),
-        13: (both("y0", "y1"), both("d0", "d1")),
-        14: (["m3"] + both("z3"), both("y3", "c3")),
+        1: [saved[3].start],
+        2: [lambda: begin("qp"), lambda: links.start("m0")],
+        3: [lambda: begin("01"), lambda: links.start("m1")],
+        4: [lambda: hop(1, "qp")],
+        5: [lambda: links.start("m2")],
+        6: [lambda: hop(2, "qp"), lambda: links.start("m3")],
+        7: [lambda: hop(3, "qp")],
+        8: [lambda: hop(1, "0"), weights, lambda: memory(0)],
+        9: [lambda: hop(1, "1")] + [copy.start for copy in saved[:3]],
+        10: [lambda: hop(2, "0"), lambda: memory(1)],
+        11: [lambda: hop(2, "1"), lambda: across(0, "01")],
+        12: [lambda: across(1, "0"), lambda: memory(2)],
+        13: [lambda: hop(3, "0"), lambda: across(1, "1")],
+        14: [lambda: hop(3, "1"), lambda: across(2, "0"), lambda: memory(3)],
     }
-    for when, (awaited, started) in plan.items():
+    for when, acts in plan.items():
 
         @pl.when(step == when)
-        def _(awaited=awaited, started=started):
-            links.arrived(*awaited)
-            links.start(*started)
-
-    @pl.when(step == 14)
-    def _():
-        for copy in saved:
-            copy.start()
+        def _(acts=acts):
+            for act in acts:
+                act()
 
     pair, clip = pair_of(step), clip_of(step)
     side = lax.div(pair, 2)
     heads = pl.ds(lax.rem(pair, 2) * PAIR, PAIR)
     forward_step(
-        pair, clip, 4,
-        w_all.at[pair], mem_all.at[side, clip, heads], tail_all.at[side, clip, heads], taps_all.at[pair],
-        x_ref, side_ref, main_ref, gain_one_ref, gain_two_ref,
-        packed_ref, keys_ref, att_ref, log_ref, normed_ref, middle_ref, normed_two_ref,
-        x_rows, normed_rows, branch,
+        pair, clip, 4, mask_rows(index_ref[x, clip]),
+        qkv_all.at[pair], proj_all.at[pair],
+        mem_all.at[side, clip, heads], tail_all.at[side, clip, heads], taps_all.at[pair],
+        x_ref, cot_ref, gain_one_ref, gain_two_ref,
+        packed_ref, keys_ref, att_ref, log_ref, normed_ref, middle_ref, normed_two_ref, cot_out,
+        x_rows, normed_rows, branch, logs,
     )
 
     @pl.when(step == pl.num_programs(0) - 1)
     def _():
-        links.arrived(*both("y2", "y3"))
-        links.start(*both("d2", "d3"))
+        across(2, "1")
+        across(3, "01")
         for copy in saved:
             copy.wait()
-        links.arrived(*both("c0", "c1", "c2", "c3", "d0", "d1", "d2", "d3"))
+        for kind in "01":
+            links.arrived("c" + kind, "e" + kind)
+            for number in (1, 2, 3):
+                for side in "ud":
+                    links.arrived(f"c{side}{number}{kind}", f"e{side}{number}{kind}")
         links.sent()
 
 
@@ -790,7 +876,9 @@
     return jnp.where(step < 8, lax.rem(step, 4), lax.div(step, 2) - 4)
 
 
-def attention_forward_links(x, w, mem, tail, side, main, taps, gain_one, gain_two, hidden_weight, output_weight):
+def attention_forward_links(
+    index, x, cot, qkv, proj, mem, tail, taps, gain_one, gain_two, hidden_weight, output_weight
+):
     clips, width = x.shape[0], x.shape[2]
     packed_width = PIECES * WIDE
     devices = 32
@@ -801,32 +889,35 @@
         forward_links_kernel,
         grid=(4 * clips,),
         in_specs=[
+            pl.BlockSpec(memory_space=pltpu.SMEM),
             pl.BlockSpec((1, TPC, width), lambda s: (early(s), 0, 0)),
-            pl.BlockSpec((1, 1, SIDE), lambda s: (clip_of(s), 0, 0)),
-            pl.BlockSpec((1, 1, MAIN), lambda s: (clip_of(s), 0, 0)),
-            pl.BlockSpec((1, width), lambda s: (0, 0)),
-            pl.BlockSpec((1, width), lambda s: (0, 0)),
-        ] + [anywhere] * 6,
+            pl.BlockSpec((1, TPC, width), lambda s: (late(s), 0, 0)),
+            pl.BlockSpec(gain_one.shape, lambda s: (0,)),
+            pl.BlockSpec(gain_two.shape, lambda s: (0,)),
+        ] + [anywhere] * 7,
         out_specs=[
             pl.BlockSpec((1, 1, ROWS, packed_width), lambda s: (pair_of(s), clip_of(s), 0, 0)),
             pl.BlockSpec((1, 1, PAIR, 2, SIDE, WIDE), lambda s: (pair_of(s), clip_of(s), 0, 0, 0, 0)),
             pl.BlockSpec((1, 1, ROWS, PAIR * WIDE), lambda s: (pair_of(s), clip_of(s), 0, 0)),
-            pl.BlockSpec((1, 1, ROWS, WIDE), lambda s: (pair_of(s), clip_of(s), 0, 0)),
+            pl.BlockSpec((1, ROWS, WIDE), lambda s: (late(s), 0, 0)),
             pl.BlockSpec((1, ROWS, width), lambda s: (early(s), 0, 0)),
             pl.BlockSpec((1, ROWS, width), lambda s: (late(s), 0, 0)),
             pl.BlockSpec((1, ROWS, width), lambda s: (late(s), 0, 0)),
-        ] + [anywhere] * 5,
+            pl.BlockSpec((1, ROWS, width), lambda s: (late(s), 0, 0)),
+        ] + [anywhere] * 6,
         out_shape=[
             shaped((4, clips, ROWS, packed_width), BF16),
             shaped((4, clips, PAIR, 2, SIDE, WIDE), BF16),
             shaped((4, clips, ROWS, PAIR * WIDE), BF16),
-            shaped((4, clips, ROWS, WIDE), F32),
+            shaped((clips, ROWS, WIDE), F32),
             shaped((clips, ROWS, width), BF16),
             shaped((clips, ROWS, width), F32),
             shaped((clips, ROWS, width), BF16),
+            shaped((clips, ROWS, width), BF16),
             shaped((devices,) + hidden_weight.shape, BF16),
             shaped((devices,) + output_weight.shape, BF16),
-            shaped((4,) + w.shape[1:], BF16),
+            shaped((4, PAIR, 3, WIDE, width), BF16),
+            shaped((4, PAIR, WIDE, width), BF16),
             shaped((2, clips, 4, 2 * HD, MAIN), BF16),
             shaped((4,) + taps.shape[1:], F32),
         ],
@@ -834,14 +925,16 @@
             pltpu.VMEM((clips, ROWS, width), BF16),
             pltpu.VMEM((clips, ROWS, width), BF16),
             pltpu.VMEM((clips, ROWS, width), F32),
-            pltpu.VMEM((4,) + w.shape[1:], BF16),
+            pltpu.VMEM((clips, ROWS, WIDE), F32),
+            pltpu.VMEM((4, PAIR, 3, WIDE, width), BF16),
+            pltpu.VMEM((4, PAIR, WIDE, width), BF16),
             pltpu.VMEM((2, clips, 4, 2 * HD, MAIN), BF16),
             pltpu.VMEM((2, clips, 4, 2 * REST, WIDE), BF16),
             pltpu.VMEM((4,) + taps.shape[1:], F32),
             pltpu.SemaphoreType.DMA((FORWARD_COPIES,)),
             pltpu.SemaphoreType.DMA((FORWARD_COPIES,)),
-            pltpu.SemaphoreType.DMA((5 + clips,)),
-            pltpu.SemaphoreType.DMA((4,)),
+            pltpu.SemaphoreType.DMA((6 + clips,)),
+            pltpu.SemaphoreType.DMA((4 + clips,)),
         ],
         compiler_params=pltpu.CompilerParams(
             dimension_semantics=("arbitrary",),
@@ -850,10 +943,10 @@
             has_side_effects=True,
         ),
         name="attention_forward_links",
-    )(x, side, main, gain_one, gain_two, w, mem, tail, taps, hidden_weight, output_weight)
-
-
-def attention_forward(x, w, mem, tail, side, main, taps, gain_one, gain_two):
+    )(index, x, cot, gain_one, gain_two, qkv, proj, mem, tail, taps, hidden_weight, output_weight)
+
+
+def attention_forward(x, cot, w, mem, tail, side, main, taps, gain_one, gain_two):
     clips, pairs = x.shape[0], w.shape[0]
     width = x.shape[2]
     packed_width = PIECES * WIDE
@@ -866,21 +959,23 @@
         grid=(pairs, clips),
         in_specs=[
             pl.BlockSpec((1, TPC, width), lambda p, c: (early(p, c), 0, 0)),
+            pl.BlockSpec((1, TPC, width), lambda p, c: (late(p, c), 0, 0)),
             pl.BlockSpec((1, weight_rows, width), lambda p, c: (p, 0, 0)),
             pl.BlockSpec((1, PAIR, 2 * HD, MAIN), lambda p, c: (c, p, 0, 0)),
             pl.BlockSpec((1, PAIR, 2 * REST, WIDE), lambda p, c: (c, p, 0, 0)),
             pl.BlockSpec((1, 1, SIDE), lambda p, c: (c, 0, 0)),
             pl.BlockSpec((1, 1, MAIN), lambda p, c: (c, 0, 0)),
-            pl.BlockSpec((1, PAIR, 4, WIDE), lambda p, c: (p, 0, 0, 0)),
-            pl.BlockSpec((1, width), lambda p, c: (0, 0)),
-            pl.BlockSpec((1, width), lambda p, c: (0, 0)),
+            pl.BlockSpec((1, PAIR, 4, HD), lambda p, c: (p, 0, 0, 0)),
+            pl.BlockSpec(gain_one.shape, lambda p, c: (0,)),
+            pl.BlockSpec(gain_two.shape, lambda p, c: (0,)),
         ],
         out_specs=[
             pl.BlockSpec((1, 1, ROWS, packed_width), lambda p, c: (p, c, 0, 0)),
             pl.BlockSpec((1, 1, PAIR, 2, SIDE, WIDE), lambda p, c: (p, c, 0, 0, 0, 0)),
             pl.BlockSpec((1, 1, ROWS, PAIR * WIDE), lambda p, c: (p, c, 0, 0)),
-            pl.BlockSpec((1, 1, ROWS, WIDE), lambda p, c: (p, c, 0, 0)),
+            pl.BlockSpec((1, ROWS, WIDE), lambda p, c: (late(p, c), 0, 0)),
             pl.BlockSpec((1, ROWS, width), lambda p, c: (early(p, c), 0, 0)),
+            pl.BlockSpec((1, ROWS, width), lambda p, c: (late(p, c), 0, 0)),
             pl.BlockSpec((1, ROWS, width), lambda p, c: (late(p, c), 0, 0)),
             pl.BlockSpec((1, ROWS, width), lambda p, c: (late(p, c), 0, 0)),
         ],
@@ -888,72 +983,77 @@
             shaped((pairs, clips, ROWS, packed_width), BF16),
             shaped((pairs, clips, PAIR, 2, SIDE, WIDE), BF16),
             shaped((pairs, clips, ROWS, PAIR * WIDE), BF16),
-            shaped((pairs, clips, ROWS, WIDE), F32),
+            shaped((clips, ROWS, WIDE), F32),
             shaped((clips, ROWS, width), BF16),
             shaped((clips, ROWS, width), F32),
+            shaped((clips, ROWS, width), BF16),
             shaped((clips, ROWS, width), BF16),
         ],
         scratch_shapes=[
             pltpu.VMEM((clips, ROWS, width), BF16),
             pltpu.VMEM((clips, ROWS, width), BF16),
             pltpu.VMEM((clips, ROWS, width), F32),
+            pltpu.VMEM((clips, ROWS, WIDE), F32),
         ],
         compiler_params=compiler_params(2),
         name="attention_forward",
-    )(x, w, mem, tail, side, main, taps, gain_one, gain_two)
+    )(x, cot, w, mem, tail, side, main, taps, gain_one, gain_two)
 
 
 def once(shape):
     return pl.BlockSpec(shape, lambda t: (0,) * len(shape), pipeline_mode=pl.Buffered(1))
+
+
+CHUNK = 800
+TILE = 768
 
 
 def mlp(normed, cot, first, second, middle, gain):
     rows, width = normed.shape
     hidden = first.shape[1]
-    clips = cot.shape[0]
-    tile = 512
+    clips = rows // ROWS
+    tiles = hidden // TILE
+    tile_at = lambda t: jnp.minimum(t, tiles - 1)
+    clip_at = lambda t: jnp.maximum(t - tiles, 0)
     return pl.pallas_call(
         mlp_kernel,
-        grid=(hidden // tile,),
+        grid=(tiles + clips,),
         in_specs=[
             once((rows, width)),
-            once((clips, TPC, width)),
-            pl.BlockSpec((width, tile), lambda t: (0, t)),
-            pl.BlockSpec((tile, width), lambda t: (t, 0)),
             once((rows, width)),
-            once((1, width)),
+            pl.BlockSpec((width, TILE), lambda t: (0, tile_at(t))),
+            pl.BlockSpec((TILE, width), lambda t: (tile_at(t), 0)),
+            pl.BlockSpec(memory_space=pl.ANY),
+            pl.BlockSpec(gain.shape, lambda t: (0,)),
         ],
         out_specs=[
-            once((clips, TPC, width)),
-            once((rows, width)),
-            once((rows, width)),
-            pl.BlockSpec((width, tile), lambda t: (0, t)),
-            pl.BlockSpec((tile, width), lambda t: (t, 0)),
+            pl.BlockSpec((1, TPC, width), lambda t: (clip_at(t), 0, 0)),
+            pl.BlockSpec((ROWS, width), lambda t: (clip_at(t), 0)),
+            pl.BlockSpec((width, TILE), lambda t: (0, tile_at(t))),
+            pl.BlockSpec((TILE, width), lambda t: (tile_at(t), 0)),
             once((1, width)),
         ],
         out_shape=[
             shaped((clips, TPC, width), BF16),
-            shaped((rows, width), F32),
             shaped((rows, width), BF16),
             shaped((width, hidden), BF16),
             shaped((hidden, width), BF16),
             shaped((1, width), F32),
         ],
         scratch_shapes=[
-            pltpu.VMEM((rows, width), BF16),
-            pltpu.VMEM((width, rows), BF16),
-            pltpu.VMEM((width, rows), BF16),
             pltpu.VMEM((rows, width), F32),
             pltpu.VMEM((rows, width), F32),
-            pltpu.VMEM((rows, tile), BF16),
-            pltpu.VMEM((rows, tile), BF16),
+            pltpu.VMEM((rows, width), F32),
+            pltpu.VMEM((rows, TILE), BF16),
+            pltpu.VMEM((rows, TILE), BF16),
+            pltpu.SemaphoreType.DMA((1,)),
         ],
         compiler_params=compiler_params(1),
         name="mlp",
     )(normed, cot, first, second, middle, gain)
 
 
-def attention_backward(x, w, mem, side, main, taps, gain, packed, keys, att, log, normed, grad, grad_low):
+def attention_backward(x, w, mem, side, main, taps, gain, packed, keys, att, log, normed, grad):
     clips, pairs = x.shape[0], w.shape[0]
     width = x.shape[2]
     packed_width = PIECES * WIDE
@@ -965,21 +1065,16 @@
         in_specs=[
             pl.BlockSpec((1, TPC, width), lambda p, c: (late(p, c), 0, 0)),
             pl.BlockSpec((1, weight_rows, width), lambda p, c: (p, 0, 0)),
-            pl.BlockSpec((1, PAIR, 2 * HD, MAIN), lambda p, c: (c, p, 0, 0))
-            if mem.ndim == 4
-            else pl.BlockSpec(
-                (None, 1, PAIR, 2 * HD, MAIN), lambda p, c: (lax.div(p, 2), c, lax.rem(p, 2), 0, 0)
-            ),
+            pl.BlockSpec((1, PAIR, 2 * HD, MAIN), lambda p, c: (c, p, 0, 0)),
             pl.BlockSpec((1, 1, SIDE), lambda p, c: (c, 0, 0)),
             pl.BlockSpec((1, 1, MAIN), lambda p, c: (c, 0, 0)),
-            pl.BlockSpec((1, PAIR, 4, WIDE), lambda p, c: (p, 0, 0, 0)),
-            pl.BlockSpec((1, width), lambda p, c: (0, 0)),
+            pl.BlockSpec((1, PAIR, 4, HD), lambda p, c: (p, 0, 0, 0)),
+            pl.BlockSpec(gain.shape, lambda p, c: (0,)),
             pl.BlockSpec((1, 1, ROWS, packed_width), lambda p, c: (p, c, 0, 0)),
             pl.BlockSpec((1, 1, PAIR, 2, SIDE, WIDE), lambda p, c: (p, c, 0, 0, 0, 0)),
             pl.BlockSpec((1, 1, ROWS, PAIR * WIDE), lambda p, c: (p, c, 0, 0)),
-            pl.BlockSpec((1, 1, ROWS, WIDE), lambda p, c: (p, c, 0, 0)),
+            pl.BlockSpec((1, ROWS, WIDE), lambda p, c: (c, 0, 0)),
             pl.BlockSpec((1, ROWS, width), lambda p, c: (c, 0, 0)),
-            pl.BlockSpec((ROWS, width), lambda p, c: (late(p, c), 0)),
             pl.BlockSpec((ROWS, width), lambda p, c: (c, 0)),
         ],
         out_specs=[
@@ -997,15 +1092,15 @@
         scratch_shapes=[pltpu.VMEM((clips, ROWS, width), F32)],
         compiler_params=compiler_params(2),
         name="attention_backward",
-    )(x, w, mem, side, main, taps, gain, packed, keys, att, log, normed, grad, grad_low)
+    )(x, w, mem, side, main, taps, gain, packed, keys, att, log, normed, grad)
 
 
 def attention_backward_links(
-    x, w, mem, side, main, taps, gain, packed, keys, att, log, normed, grad, grad_low, gain_two, d_first, d_second
+    index, x, qkv, proj, mem, taps, gain, packed, keys, att, log, normed, grad, gain_two, d_first, d_second
 ):
     clips, width = x.shape[0], x.shape[2]
     packed_width = PIECES * WIDE
-    weight_rows = w.shape[1]
+    weight_rows = (PIECES + PAIR) * WIDE
     low_rows = weight_rows // WIDE * HD
     pair_at = lambda s: lax.rem(lax.div(s, 4) + 2, 4)
     clip_at = lambda s: lax.rem(s, 4)
@@ -1025,22 +1120,21 @@
         backward_links_kernel,
         grid=(4 * clips,),
         in_specs=[
+            pl.BlockSpec(memory_space=pltpu.SMEM),
             pl.BlockSpec((1, TPC, width), lambda s: (late(s), 0, 0)),
-            pl.BlockSpec((1, weight_rows, width), lambda s: (pair_at(s), 0, 0)),
+            pl.BlockSpec((1,) + qkv.shape[1:], lambda s: (pair_at(s), 0, 0, 0, 0)),
+            pl.BlockSpec((1,) + proj.shape[1:], lambda s: (pair_at(s), 0, 0, 0)),
             pl.BlockSpec(
                 (None, 1, PAIR, 2 * HD, MAIN),
                 lambda s: (lax.div(pair_at(s), 2), clip_at(s), lax.rem(pair_at(s), 2), 0, 0),
             ),
-            pl.BlockSpec((1, 1, SIDE), lambda s: (clip_at(s), 0, 0)),
-            pl.BlockSpec((1, 1, MAIN), lambda s: (clip_at(s), 0, 0)),
-            pl.BlockSpec((1, PAIR, 4, WIDE), lambda s: (pair_at(s), 0, 0, 0)),
-            pl.BlockSpec((1, width), lambda s: (0, 0)),
+            pl.BlockSpec((1, PAIR, 4, HD), lambda s: (pair_at(s), 0, 0, 0)),
+            pl.BlockSpec(gain.shape, lambda s: (0,)),
             pl.BlockSpec((1, 1, ROWS, packed_width), per_step),
             pl.BlockSpec((1, 1, PAIR, 2, SIDE, WIDE), lambda s: per_step(s) + (0, 0)),
             pl.BlockSpec((1, 1, ROWS, PAIR * WIDE), per_step),
-            pl.BlockSpec((1, 1, ROWS, WIDE), per_step),
+            pl.BlockSpec((1, ROWS, WIDE), lambda s: (clip_at(s), 0, 0)),
             pl.BlockSpec((1, ROWS, width), lambda s: (clip_at(s), 0, 0)),
-            pl.BlockSpec((ROWS, width), lambda s: (late(s), 0)),
             pl.BlockSpec((ROWS, width), lambda s: (clip_at(s), 0)),
             pl.BlockSpec((1, width), lambda s: (0, 0)),
             anywhere,
@@ -1089,7 +1183,9 @@
             has_side_effects=True,
         ),
         name="attention_backward_links",
-    )(x, w, mem, side, main, taps, gain, packed, keys, att, log, normed, grad, grad_low, gain_two, d_first, d_second)
+    )(
+        index, x, qkv, proj, mem, taps, gain, packed, keys, att, log, normed, grad, gain_two, d_first, d_second
+    )
 
 
 def group_gather(own, heads, fetch=None):
@@ -1142,33 +1238,19 @@
         qkv_weight.transpose(1, 2, 0).reshape(own_heads, 3, HD, width), ((0, 0), (0, 0), (0, pad), (0, 0))
     )
     proj_rows = jnp.pad(proj_weight, ((0, 0), (0, pad), (0, 0)))
-    taps_own = jnp.pad(pool_weight.astype(F32), ((0, 0), (0, 0), (0, pad)))
+    taps_own = pool_weight.astype(F32)
     memory_t = memory.transpose(0, 1, 3, 4, 2)
     tail_own = memory_t[..., MAIN:].reshape(memory_t.shape[:3] + (2, HD, REST)).swapaxes(4, 5)
     tail_own = jnp.pad(tail_own, ((0, 0),) * 5 + ((0, pad),)).reshape(memory_t.shape[:3] + (2 * REST, WIDE))
 
-    index = mine(clip_index, 0).reshape(clips, 1, 1)
-    main_slot = lax.broadcasted_iota(jnp.int32, (1, 1, MAIN), 2) // PTOK
-    main_mask = jnp.where(index > main_slot, 0.0, NEG).astype(F32)
-    spot = lax.broadcasted_iota(jnp.int32, (1, 1, SIDE), 2)
-    tail_open = (spot >= HALF) & (spot < HALF + REST) & (index > (TPC - 1) // PTOK)
-    side_mask = jnp.where((spot < PTOK) | tail_open, 0.0, NEG).astype(F32)
-
     x = inputs.reshape(clips, TPC, width)
-    gain_one = gain_one.reshape(1, width)
-    gain_two = gain_two.reshape(1, width)
-    w_own = jnp.concatenate(
-        [
-            qkv_rows.reshape(-1, PIECES * WIDE, width),
-            proj_rows.reshape(-1, PAIR * WIDE, width),
-        ],
-        axis=1,
-    ) if own_heads % PAIR == 0 else None
+    cot = cotangent.reshape(clips, TPC, width)
     if linked:
-        (packed, keys, att, log, normed, middle, normed_two, first, second, w_all, mem_all, taps_all) = (
+        (packed, keys, att, log, normed, middle, normed_two, cot_rows, first, second, qkv_all, proj_all, mem_all, taps_all) = (
             attention_forward_links(
-                x, w_own, memory_t, tail_own, side_mask, main_mask,
-                taps_own.reshape(-1, PAIR, 4, WIDE), gain_one, gain_two, hidden_weight, output_weight,
+                clip_index.T, x, cot, qkv_weight.transpose(1, 2, 0).reshape(PAIR, PAIR, 3, HD, width),
+                proj_weight.reshape(PAIR, PAIR, HD, width), memory_t, tail_own,
+                taps_own.reshape(-1, PAIR, 4, HD), gain_one, gain_two, hidden_weight, output_weight,
             )
         )
         first = first.reshape(width, -1)
@@ -1183,7 +1265,7 @@
             ],
             axis=1,
         )
-        taps_all = jnp.concatenate(group_gather(taps_own, heads), axis=0).reshape(pairs, PAIR, 4, WIDE)
+        taps_all = jnp.concatenate(group_gather(taps_own, heads), axis=0).reshape(pairs, PAIR, 4, HD)
         mem_all = jnp.concatenate(group_gather(memory_t, heads, mine), axis=2)
         mem_all = mem_all.reshape(clips, all_heads, 2 * HD, TPC)
         tail = jnp.concatenate(group_gather(tail_own, heads, mine), axis=2)
@@ -1191,12 +1273,15 @@
 
         first = lax.all_gather(hidden_weight, ("batch", "head"), axis=0, tiled=True)
         second = lax.all_gather(output_weight, ("batch", "head"), axis=0, tiled=True)
-        packed, keys, att, log, normed, middle, normed_two = attention_forward(
-            x, w_all, mem_all, tail, side_mask, main_mask, taps_all, gain_one, gain_two
+        index = mine(clip_index, 0).reshape(clips, 1, 1)
+        side_mask, main_mask = mask_rows(index)
+        side_mask, main_mask = side_mask.reshape(clips, 1, SIDE), main_mask.reshape(clips, 1, MAIN)
+        packed, keys, att, log, normed, middle, normed_two, cot_rows = attention_forward(
+            x, cot, w_all, mem_all, tail, side_mask, main_mask, taps_all, gain_one, gain_two
         )
-    outputs, grad, grad_low, d_first, d_second, d_gain_two = mlp(
+    outputs, grad, d_first, d_second, d_gain_two = mlp(
         normed_two.reshape(clips * ROWS, width),
-        cotangent.reshape(clips, TPC, width),
+        cot_rows.reshape(clips * ROWS, width),
         first,
         second,
         middle.reshape(clips * ROWS, width),
@@ -1204,8 +1289,8 @@
     )
     if linked:
         d_x, small, d_first, d_second, d_w = attention_backward_links(
-            x, w_all, mem_all, side_mask, main_mask, taps_all, gain_one,
-            packed, keys, att, log, normed, grad, grad_low, d_gain_two,
+            clip_index.T, x, qkv_all, proj_all, mem_all, taps_all, gain_one,
+            packed, keys, att, log, normed, grad, d_gain_two,
             d_first.reshape(4, 2, 2, 2, -1, d_first.shape[1]), d_second.reshape(4, 2, 2, 2, -1, width),
         )
         qkv_rows = PAIR * 3 * HD
@@ -1228,7 +1313,7 @@
         )
     d_x, d_w, d_taps, d_gain_one = attention_backward(
         x, w_all, mem_all, side_mask, main_mask, taps_all, gain_one,
-        packed, keys, att, log, normed, grad, grad_low,
+        packed, keys, att, log, normed, grad,
     )
     d_proj = d_w[:, PIECES * WIDE :].reshape(heads, own_heads, WIDE, width)[:, :, :HD]
     d_w = d_w[:, : PIECES * WIDE].reshape(heads, own_heads, 3, WIDE, width)[:, :, :, :HD]

time: 376 us -> 316 us (0.84)
  Pallas kernels: 349 us -> 298 us
  local copies, waits for them, and re-layouts: 17.1 us -> 11.3 us
  other arithmetic: 7.7 us -> 3.79 us
    pallas_call x1, Pallas kernels: 122 us -> 94 us  [attention_forward_links(): pl.pallas_call(forward_links_kernel, grid=(4 * clips,), in_specs=[pl.Bloc...]
    pallas_call x1, Pallas kernels: 80.9 us -> 66.8 us  [mlp(): pl.pallas_call(mlp_kernel, grid=(tiles + clips,), in_specs=[once((rows, w...]
    pallas_call x1, Pallas kernels: 146 us -> 138 us  [attention_backward_links(): pl.pallas_call(backward_links_kernel, grid=(4 * clips,), in_specs=[pl.Blo...]
where the time goes in v4:
time: 316 us; the launch traced here: 314 us
  Pallas kernels  298 us (94%)
  local copies, waits for them, and re-layouts  11.3 us (4%)
  other arithmetic  3.79 us (1%)
    pallas_call x1, Pallas kernels, attention_backward_links(): pl.pallas_call(backward_links_kernel, grid=(4 * clips,), in_specs=[pl.Blo...  138 us
    pallas_call x1, Pallas kernels, attention_forward_links(): pl.pallas_call(forward_links_kernel, grid=(4 * clips,), in_specs=[pl.Bloc...  94 us
    pallas_call x1, Pallas kernels, mlp(): pl.pallas_call(mlp_kernel, grid=(tiles + clips,), in_specs=[once((rows, w...  66.8 us

profile of v4, /device:TPU:0, one launch (start us, length us, event | category | flops | bytes accessed | tf_op | source)
XLA Modules:
  0.0 314.3 jit_solution(11828035397283272626)
XLA Ops:
  0.6 0.0 copy-start.3
  0.7 1.6 slice.32
  2.2 0.7 copy.20
  2.9 0.7 pad_bitcast_fusion.tail_own
  3.6 0.0 copy-done.3
  3.6 0.6 convert.4.taps_own
  4.2 94.0 %attention_forward_links.1 = (bf16[4,4,400,768]{3,2,1,0:T(8,128)(2,1)}, bf16[4,4,2,2,256,128]{5,4,3,2,1,0:T(8,128)(2,1)}, bf16[4,4,400,256]{3,2,1,0:T(8,128)(2,1...) custom-call(s32[2,4]{1,0:T(2,128)} %bitcast.61, ...), custom_call_target="tpu_custom_call" | custom-call | tf_op jit(solution)/shard_map/attention_forward_links/pallas_call | solution.py:888
  98.2 66.8 %mlp.1 = (bf16[4,392,768]{2,1,0:T(8,128)(2,1)}, bf16[1600,768]{1,0:T(8,128)(2,1)}, bf16[768,3072]{1,0:T(8,128)(2,1)}, bf16[3072,768]{1,0:T(8,128)(2,1)}, f32[1,768]{1,0:T(1,128)}) custom-call(bf16[1600,768]{1,0:T(8,128)(2,1)} %bitcast.51, bf16[1600,768]{1,0:T(8,128)(2,1)} %bitcast.52, bf16[768,3072]{1,0:T(8,128)(2,1)} %bitcast.49, ...), custom_call_target="tpu_custom_call" | custom-call | tf_op jit(solution)/shard_map/mlp/pallas_call | solution.py:1018
  165.0 137.6 %attention_backward_links.1 = (bf16[4,392,768]{2,1,0:T(8,128)(2,1)}, f32[16,768]{1,0:T(8,128)}, f32[24,3072]{1,0:T(8,128)}, f32[96,768]{1,0:T(8,128)}, bf16[2,768,768]{2,1,0:T(8,128)(2,1)}) custom-call(s32[2,4]{1,0:T(2,128)} %bitcast.62, bf16[4,392,768]{2,1,0:T(8,128)(2,1)} %bitcast.43, bf16[4,2,3,128,768]{4,3,2,1,0:T(8,128)(2,1)} %get-tuple-element.39.qkv_ref, ...), custom_call_target="tpu_custom_call" | custom-call | tf_op jit(solution)/shard_map/attention_backward_links/pallas_call | solution.py:1119
  302.6 1.6 slice.25
  304.2 2.1 convert_bitcast_fusion
  306.3 0.0 copy-start
  306.3 1.3 slice.26
  307.6 1.1 convert.6
  308.7 0.0 copy-start.2
  308.7 0.8 slice.29
  309.5 0.1 constant_dynamic-slice_fusion
  309.6 0.5 slice_bitcast_fusion
  310.1 0.7 slice.27
  310.8 0.6 copy.21
  311.4 0.0 copy-done
  311.4 0.0 copy-start.1
  311.4 1.4 copy.27
  312.8 0.0 copy-done.2
  312.8 0.7 copy.28
  313.5 0.0 copy-done.1
  313.5 0.7 copy.29
  (1 shorter events, 0.0 us)
Async XLA Ops:
  0.6 2.9 copy-start.3
  306.3 5.1 %copy-start = (bf16[4,392,768]{2,1,0:T(8,128)(2,1)S(1)}, bf16[4,392,768]{2,1,0:T(8,128)(2,1)}, u32[]{:S(2)}) copy-start(bf16[4,392,768]{2,1,0:T(8,128)(2,1)} %get-tuple-element.52) | copy-start | bytes 7225348
  308.7 4.1 %copy-start.2 = (f32[24,3072]{1,0:T(8,128)S(1)}, f32[24,3072]{1,0:T(8,128)}, u32[]{:S(2)}) copy-start(f32[24,3072]{1,0:T(8,128)} %get-tuple-element.84) | copy-start | bytes 884740
  311.4 2.1 copy-start.1

commit v5 on v4

--- a/solution.py
+++ b/solution.py
@@ -178,14 +178,237 @@
         cot_out[0] = dot(reorder((ROWS, TPC), 0), cot_ref[0]).astype(BF16)
 
 
-def mlp_kernel(
+def feed(step, chunk, normed_ref, cot_ref, first, second, total, grad_normed, active, grad_hidden):
+    here = pl.ds(chunk * CHUNK, CHUNK)
+    hidden = dot(normed_ref[here, :], first)
+    grad_active = dot_nt(cot_ref[here, :], second)
+    bell = jnp.exp2(hidden * hidden * (-0.5 * LOG2E))
+    near = 1.0 / (1.0 + (0.3275911 * math.sqrt(0.5)) * jnp.abs(hidden))
+    tail = near * (0.5 * 1.061405429) + (0.5 * -1.453152027)
+    tail = near * tail + (0.5 * 1.421413741)
+    tail = near * tail + (0.5 * -0.284496736)
+    tail = near * tail + (0.5 * 0.254829592)
+    tail = near * tail * bell
+    cumulative = jnp.where(hidden < 0.0, tail, 1.0 - tail)
+    slope = cumulative + hidden * bell * 0.3989422804014327
+    active_low = (hidden * cumulative).astype(BF16)
+    hidden_low = (slope * grad_active).astype(BF16)
+    active[here, :] = active_low
+    grad_hidden[here, :] = hidden_low
+    fed = dot(active_low, second)
+    back = dot_nt(hidden_low, first)
+
+    @pl.when(step == 0)
+    def _():
+        total[here, :] = fed
+        grad_normed[here, :] = back
+
+    @pl.when(step > 0)
+    def _():
+        total[here, :] += fed
+        grad_normed[here, :] += back
+
+
+def mlp_kernel(*refs):
+    mlp_step(None, *refs)
+
+
+def mlp_links_kernel(
     normed_ref, cot_ref, first_ref, second_ref, middle_ref, gain_ref,
+    out_ref, grad_ref, d_gain_ref, first_out, second_out, first_left, second_left,
+    middle, total, grad_normed, active, grad_hidden, near, *rest,
+):
+    step = pl.program_id(0)
+    here = place()
+    z, y, core, x, at = here
+    first_refs, second_refs = rest[:5], rest[5:10]
+    first_keep, second_keep, first_result, second_result, send, recv, store = rest[10:]
+    links = Links(send, recv)
+    partners = Partners(here)
+    sums, outs = [], []
+    for tile in range(EARLY):
+        sums.append(
+            (
+                Sum(f"f{tile}", "xy", None, [ref.at[tile] for ref in first_refs], links, partners),
+                Sum(f"s{tile}", "yx", tile, [ref.at[tile] for ref in second_refs], links, partners),
+            )
+        )
+        outs.append(
+            (
+                pltpu.make_async_copy(
+                    first_result.at[tile], first_out.at[:, pl.ds(tile * TILE, TILE)], store.at[2 * tile]
+                ),
+                pltpu.make_async_copy(second_result, second_out, store.at[2 * tile + 1]),
+            )
+        )
+    kept = [
+        [
+            pltpu.make_async_copy(left.at[tile], out.at[tile], store.at[2 * (EARLY + tile) + i])
+            for i, (left, out) in enumerate(((first_keep, first_left), (second_keep, second_left)))
+        ]
+        for tile in range(TILES - EARLY)
+    ]
+
+    def store_grads(d_first, d_second):
+        for tile in range(TILES):
+
+            @pl.when(step == tile)
+            def _(tile=tile):
+                early = tile < EARLY
+                for early_ref, keep_ref, grad in (
+                    (first_refs[0], first_keep, d_first),
+                    (second_refs[0], second_keep, d_second),
+                ):
+                    into = early_ref if early else keep_ref
+                    into[tile if early else tile - EARLY] = grad.reshape(into.shape[1:]).astype(BF16)
+                if not early:
+                    for copy in kept[tile - EARLY]:
+                        copy.start()
+
+    def finish(tile):
+        one, two = sums[tile]
+        one.finish(first_result.at[tile])
+        outs[tile][0].start()
+
+        @pl.when(z == tile)
+        def _():
+            two.finish(second_result)
+            outs[tile][1].start()
+
+    def act(moment):
+        for tile, (one, two) in enumerate(sums):
+            plan = {
+                (tile + 1, 0): [one.begin, two.begin],
+                (tile + 1, 1): [one.core, two.core],
+                (tile + 2, 0): [one.first, two.first],
+                (tile + 2, 1): [one.second, two.second],
+                (tile + 3, 0): [lambda: finish(tile)],
+            }
+            for (when, which), acts in plan.items():
+                if which != moment:
+                    continue
+
+                @pl.when(step == when)
+                def _(acts=acts):
+                    for one_act in acts:
+                        one_act()
+
+    @pl.when(step == 0)
+    def _():
+        greet(partners.all())
+
+    mlp_step(
+        act, normed_ref, cot_ref, first_ref, second_ref, middle_ref, gain_ref,
+        out_ref, grad_ref, store_grads, None, d_gain_ref,
+        middle, total, grad_normed, active, grad_hidden, near,
+    )
+
+    @pl.when(step == pl.num_programs(0) - 1)
+    def _():
+        links.sent()
+        for copies in kept:
+            for copy in copies:
+                copy.wait()
+        for tile, (one, two) in enumerate(outs):
+            one.wait()
+            pl.when(z == tile)(lambda two=two: two.wait())
+
+
+class Partners:
+    def __init__(self, here):
+        self.place = here
+        z, y, core, x, at = here
+        self.x, self.y, self.core = at(z, y, core, 1 - x), at(z, 1 - y, core, x), at(z, y, 1 - core, x)
+        self.along = [at(turn(z, shift), y, core, x) for shift in (1, 2, 3)]
+
+    def all(self):
+        return [self.x, self.y, self.core] + self.along
+
+
+class Sum:
+    def __init__(self, name, order, owner, refs, links, partners):
+        self.name, self.order, self.owner, self.links = name, order, owner, links
+        self.data, self.from_core, self.from_one, self.from_two, self.from_z = refs
+        self.place = z, y, core, x, at = partners.place
+        data = self.data
+        self.planes = data.shape[0]
+        self.names = [name + "c", name + "a", name + "b"] + [f"{name}z{shift}" for shift in (1, 2, 3)]
+        links.add(name + "c", data.at[:, :, 1 - core], self.from_core, partners.core)
+        if order == "xy":
+            links.add(name + "a", data.at[:, :, core, 1 - x], self.from_one, partners.x)
+            links.add(name + "b", data.at[:, 1 - y, core, x], self.from_two, partners.y)
+        else:
+            links.add(name + "a", data.at[:, 1 - y, core], self.from_one, partners.y)
+            links.add(name + "b", data.at[:, y, core, 1 - x], self.from_two, partners.x)
+        for shift in (1, 2, 3):
+            into = self.from_z.at[shift - 1]
+            if owner is None:
+                source = data.at[turn(z, shift), y, core, x]
+                links.add(f"{name}z{shift}", source, into, partners.along[shift - 1])
+            else:
+                links.add(
+                    f"{name}z{shift}", data.at[0, y, core, x], into, at(owner, y, core, x),
+                    z == (owner + shift) % 4, z == owner,
+                )
+
+    def begin(self):
+        self.links.start(self.name + "c")
+
+    def core(self):
+        z, y, core, x, at = self.place
+        self.links.arrived(self.name + "c")
+
+        @pl.loop(0, self.planes)
+        def _(plane):
+            for column in (0, 1):
+                for head in (0, 1):
+                    self.data[plane, column, core, head] = add_low(
+                        self.data[plane, column, core, head], self.from_core[plane, column, head]
+                    )
+
+        self.links.start(self.name + "a")
+
+    def first(self):
+        z, y, core, x, at = self.place
+        self.links.arrived(self.name + "a")
+
+        @pl.loop(0, self.planes)
+        def _(plane):
+            for other in (0, 1):
+                spot = (plane, other, core, x) if self.order == "xy" else (plane, y, core, other)
+                self.data[spot] = add_low(self.data[spot], self.from_one[plane, other])
+
+        self.links.start(self.name + "b")
+
+    def second(self):
+        z, y, core, x, at = self.place
+        self.links.arrived(self.name + "b")
+
+        @pl.loop(0, self.planes)
+        def _(plane):
+            self.data[plane, y, core, x] = add_low(self.data[plane, y, core, x], self.from_two[plane])
+
+        self.links.start(*self.names[3:])
+
+    def finish(self, result):
+        z, y, core, x, at = self.place
+        for name in self.names[3:]:
+            self.links.get(name).wait_recv()
+        part = self.data[z if self.owner is None else 0, y, core, x].astype(F32)
+        for shift in range(3):
+            part = part + self.from_z[shift].astype(F32)
+        result[...] = part
+
+
+def mlp_step(
+    act, normed_ref, cot_ref, first_ref, second_ref, middle_ref, gain_ref,
     out_ref, grad_ref, d_first_ref, d_second_ref, d_gain_ref,
     middle, total, grad_normed, active, grad_hidden, near,
 ):
     step = pl.program_id(0)
     clips = middle.shape[0] // ROWS
     tiles = pl.num_programs(0) - clips
+    chunks = middle.shape[0] // CHUNK
     fetch = pltpu.make_async_copy(middle_ref, middle, near.at[0])
 
     @pl.when(step == 0)
@@ -193,44 +416,26 @@
         fetch.start()
         d_gain_ref[...] = jnp.zeros_like(d_gain_ref)
 
+    if act is not None:
+        act(0)
+
     @pl.when(step < tiles)
     def _():
         first = first_ref[...]
         second = second_ref[...]
-
-        @pl.loop(0, middle.shape[0] // CHUNK)
-        def _(chunk):
-            here = pl.ds(pl.multiple_of(chunk * CHUNK, CHUNK), CHUNK)
-            hidden = dot(normed_ref[here, :], first)
-            grad_active = dot_nt(cot_ref[here, :], second)
-            bell = jnp.exp2(hidden * hidden * (-0.5 * LOG2E))
-            step_size = 1.0 / (1.0 + (0.3275911 * math.sqrt(0.5)) * jnp.abs(hidden))
-            tail = step_size * (0.5 * 1.061405429) + (0.5 * -1.453152027)
-            tail = step_size * tail + (0.5 * 1.421413741)
-            tail = step_size * tail + (0.5 * -0.284496736)
-            tail = step_size * tail + (0.5 * 0.254829592)
-            tail = step_size * tail * bell
-            cumulative = jnp.where(hidden < 0.0, tail, 1.0 - tail)
-            slope = cumulative + hidden * bell * 0.3989422804014327
-            active_low = (hidden * cumulative).astype(BF16)
-            hidden_low = (slope * grad_active).astype(BF16)
-            active[here, :] = active_low
-            grad_hidden[here, :] = hidden_low
-            fed = dot(active_low, second)
-            back = dot_nt(hidden_low, first)
-
-            @pl.when(step == 0)
-            def _():
-                total[here, :] = fed
-                grad_normed[here, :] = back
-
-            @pl.when(step > 0)
-            def _():
-                total[here, :] += fed
-                grad_normed[here, :] += back
-
-        d_first_ref[...] = dot_tn(normed_ref[...], grad_hidden[...]).astype(BF16)
-        d_second_ref[...] = dot_tn(active[...], cot_ref[...]).astype(BF16)
+        for chunk in range(chunks):
+            if act is not None and chunk == 1:
+                act(1)
+            feed(step, chunk, normed_ref, cot_ref, first, second, total, grad_normed, active, grad_hidden)
+        if act is not None:
+            act(2)
+        d_first = dot_tn(normed_ref[...], grad_hidden[...])
+        d_second = dot_tn(active[...], cot_ref[...])
+        if act is not None:
+            d_first_ref(d_first, d_second)
+        else:
+            d_first_ref[...] = d_first.astype(BF16)
+            d_second_ref[...] = d_second.astype(BF16)
 
     @pl.when(step == tiles)
     def _():
@@ -253,23 +458,7 @@
     d_x_ref, d_w_ref, d_taps_ref, d_gain_ref,
     grad_normed,
 ):
-    backward_step(
-        pl.program_id(0), pl.program_id(1), pl.program_id(0) == 0, pl.program_id(0) == pl.num_programs(0) - 1,
-        (side_ref[0], main_ref[0]),
-        w_ref.at[0, : PIECES * WIDE], w_ref.at[0, PIECES * WIDE :], d_w_ref.at[0], d_taps_ref.at[0],
-        x_ref, mem_ref, taps_ref, gain_ref,
-        packed_ref, keys_ref, att_ref, log_ref, normed_ref, grad_ref,
-        d_x_ref, d_gain_ref, grad_normed,
-    )
-
-
-def backward_step(
-    pair, clip, first_pair, last_pair, masks,
-    qkv_ref, proj_ref, d_w_ref, d_taps_ref,
-    x_ref, mem_ref, taps_ref, gain_ref,
-    packed_ref, keys_ref, att_ref, log_ref, normed_ref, grad_ref,
-    d_x_ref, d_gain_ref, grad_normed,
-):
+    pair, clip = pl.program_id(0), pl.program_id(1)
     here = pl.ds(clip, 1)
 
     @pl.when(clip == 0)
@@ -277,22 +466,58 @@
         d_w_ref[...] = jnp.zeros_like(d_w_ref)
         d_taps_ref[...] = jnp.zeros_like(d_taps_ref)
 
-    grad_branch = grad_ref[...]
+    grad_packed = backward_attention(
+        pair, (side_ref[0], main_ref[0]), w_ref.at[0, PIECES * WIDE :], d_taps_ref.at[0],
+        mem_ref.at[0], taps_ref.at[0], packed_ref.at[0, 0], keys_ref.at[0, 0], att_ref.at[0, 0], log_ref, grad_ref,
+    )
+    d_w_ref[0, PIECES * WIDE :] += dot_tn(att_ref[0, 0], grad_ref[...])
+    d_w_ref[0, : PIECES * WIDE] += dot_tn(grad_packed, normed_ref[0])
+    part = dot(grad_packed, w_ref[0, : PIECES * WIDE])[None]
+
+    @pl.when(pair == 0)
+    def _():
+        grad_normed[here] = part
+
+    @pl.when(pair > 0)
+    def _():
+        grad_normed[here] += part
+
+    @pl.when(pair == pl.num_programs(0) - 1)
+    def _():
+        d_x_ref[0], d_gain = input_grad(x_ref[0], grad_normed[here][0], gain_ref, grad_ref[...])
+
+        @pl.when(clip == 0)
+        def _():
+            d_gain_ref[...] = d_gain
+
+        @pl.when(clip > 0)
+        def _():
+            d_gain_ref[...] += d_gain
+
+
+def input_grad(x, grad_normed, gain_ref, grad_branch):
+    rows = dot(reorder((ROWS, TPC), 0), x)
+    pulled, d_gain = norm_pull(rows, as_row(gain_ref), grad_normed)
+    d_x = (grad_branch.astype(F32) + pulled).astype(BF16)
+    return dot(reorder((TPC, ROWS), 1), d_x).astype(BF16), d_gain
+
+
+def backward_attention(
+    pair, masks, proj_ref, d_taps_ref, mem_ref, taps_ref, packed_ref, keys_ref, att_ref, log_ref, grad_ref
+):
     lane = lax.broadcasted_iota(jnp.int32, (ROWS, WIDE), 1) - PAIR * pair
-    width = grad_branch.shape[1]
-    grad_out = dot_nt(grad_branch, proj_ref[...].reshape(-1, width))
-    d_w_ref[PIECES * WIDE :] += dot_tn(att_ref[0, 0], grad_branch)
+    grad_out = dot_nt(grad_ref[...], proj_ref[...].reshape(PAIR * WIDE, -1))
     pieces = []
     for head in range(PAIR):
         base = 3 * WIDE * head
-        query = packed_ref[0, 0, :, base : base + WIDE]
-        key = packed_ref[0, 0, :, base + WIDE : base + 2 * WIDE].astype(F32)
-        value = packed_ref[0, 0, :, base + 2 * WIDE : base + 3 * WIDE].astype(F32)
+        query = packed_ref[:, base : base + WIDE]
+        key = packed_ref[:, base + WIDE : base + 2 * WIDE].astype(F32)
+        value = packed_ref[:, base + 2 * WIDE : base + 3 * WIDE].astype(F32)
         out_grad = grad_out[:, WIDE * head : WIDE * (head + 1)].astype(BF16)
-        taps = widen(taps_ref[0, head])
-        side_key = keys_ref[0, 0, head, 0]
-        side_value = keys_ref[0, 0, head, 1]
-        memory_t = mem_ref[0, head]
+        taps = widen(taps_ref[head])
+        side_key = keys_ref[head, 0]
+        side_value = keys_ref[head, 1]
+        memory_t = mem_ref[head]
         log = jnp.sum(jnp.where(lane == head, log_ref[0], 0.0), axis=-1, keepdims=True)
         score_side = dot_nt(query, side_key) * (SCORE * LOG2E) + masks[0]
         score_main = dot(query, memory_t[:WIDE]) * (SCORE * LOG2E) + masks[1]
@@ -300,9 +525,8 @@
         weight_main = jnp.exp2(score_main - log)
         grad_side = dot_nt(out_grad, side_value)
         grad_main = dot(out_grad, value_columns(memory_t))
-        inner = jnp.sum(weight_side * grad_side, axis=-1, keepdims=True) + jnp.sum(
-            weight_main * grad_main, axis=-1, keepdims=True
-        )
+        mixed = att_ref[:, WIDE * head : WIDE * (head + 1)].astype(F32) - query.astype(F32)
+        inner = jnp.sum(out_grad.astype(F32) * mixed, axis=-1, keepdims=True)
         score_grad_side = (weight_side * (grad_side - inner)).astype(BF16)
         score_grad_main = (weight_main * (grad_main - inner)).astype(BF16)
         grad_query = (
@@ -327,108 +551,7 @@
             ],
             axis=0,
         )
-    grad_packed = jnp.concatenate(pieces, axis=1).astype(BF16)
-    d_w_ref[: PIECES * WIDE] += dot_tn(grad_packed, normed_ref[0])
-    part = dot(grad_packed, qkv_ref[...].reshape(-1, width))[None]
-
-    @pl.when(first_pair)
-    def _():
-        grad_normed[here] = part
-
-    @pl.when(jnp.logical_not(first_pair))
-    def _():
-        grad_normed[here] += part
-
-    @pl.when(last_pair)
-    def _():
-        rows = dot(reorder((ROWS, TPC), 0), x_ref[0])
-        pulled, d_gain = norm_pull(rows, as_row(gain_ref), grad_normed[here][0])
-        d_x = (grad_branch.astype(F32) + pulled).astype(BF16)
-        d_x_ref[0] = dot(reorder((TPC, ROWS), 1), d_x).astype(BF16)
-
-        @pl.when(clip == 0)
-        def _():
-            d_gain_ref[...] = d_gain
-
-        @pl.when(clip > 0)
-        def _():
-            d_gain_ref[...] += d_gain
-
-
-class Scatter:
-    def __init__(self, name, order, source, total, from_core, from_one, from_two, from_z, result, out, links, sem, here):
-        self.name, self.order, self.links, self.here = name, order, links, here
-        self.total, self.from_core, self.from_one, self.from_two, self.from_z = (
-            total, from_core, from_one, from_two, from_z
-        )
-        self.result = result
-        z, y, core, x, beside, above, sibling, along = here
-        links.add(name + "c", source.at[:, :, 1 - core], from_core, sibling)
-        self.own = pltpu.make_async_copy(source.at[:, :, core], total, sem.at[0])
-        self.done = pltpu.make_async_copy(result, out, sem.at[1])
-        if order == "xyz":
-            links.add(name + "x", total.at[:, :, 1 - x], from_one, beside)
-            links.add(name + "y", total.at[:, 1 - y, x], from_two, above)
-            for shift in (1, 2, 3):
-                links.add(f"{name}z{shift}", total.at[turn(z, shift), y, x], from_z.at[shift - 1], along[shift - 1])
-        else:
-            links.add(name + "y", total.at[:, 1 - y], from_one, above)
-            for shift in (1, 2, 3):
-                links.add(f"{name}z{shift}", total.at[turn(z, shift), y], from_z.at[shift - 1], along[shift - 1])
-            links.add(name + "x", total.at[z, y, 1 - x], from_two, beside)
-
-    def stage(self, axis):
-        return [f"{self.name}z{shift}" for shift in (1, 2, 3)] if axis == "z" else [self.name + axis]
-
-    def begin(self):
-        self.links.start(self.name + "c")
-        self.own.start()
-
-    def step(self, at):
-        z, y, core, x = self.here[:4]
-        total = self.total
-        axis = ("c" + self.order)[at]
-        self.links.arrived(*self.stage(axis))
-        if axis == "c":
-            self.own.wait()
-
-            @pl.loop(0, 4)
-            def _(row):
-                for column in (0, 1):
-                    for head in (0, 1):
-                        total[row, column, head] = add_low(total[row, column, head], self.from_core[row, column, head])
-
-        elif at == 1:
-
-            @pl.loop(0, 4)
-            def _(row):
-                for other in (0, 1):
-                    spot = (row, other, x) if self.order == "xyz" else (row, y, other)
-                    total[spot] = add_low(total[spot], self.from_one[row, other])
-
-        elif axis == "y":
-
-            @pl.loop(0, 4)
-            def _(row):
-                total[row, y, x] = add_low(total[row, y, x], self.from_two[row])
-
-        elif axis == "z" and at == 2:
-            for head in (0, 1):
-                part = total[z, y, head].astype(F32)
-                for shift in range(3):
-                    part = part + self.from_z[shift, head].astype(F32)
-                total[z, y, head] = part.astype(BF16)
-        else:
-            part = total[z, y, x].astype(F32)
-            if axis == "z":
-                for shift in range(3):
-                    part = part + self.from_z[shift].astype(F32)
-            else:
-                part = part + self.from_two[...].astype(F32)
-            self.result[...] = part
-            self.done.start()
-        if at < 3:
-            self.links.start(*self.stage(self.order[at]))
+    return jnp.concatenate(pieces, axis=1).astype(BF16)
 
 
 def add_low(one, other):
@@ -444,141 +567,270 @@
         into[narrow] = rows.astype(BF16)
 
 
-BACKWARD_COPIES = 48
-THIRD = 384
-PART = 96
+BACKWARD_COPIES = 96
+CORE_LANES = 384
+UNITS = (("p", 384, 384), ("0", 576, 640), ("1", 576, 640))
+
+
+class AllReduce:
+    def __init__(self, name, refs, links, partners):
+        self.name, self.links = name, links
+        self.own, self.core, self.y, self.z, self.whole = refs
+        self.place = z, y, core, x, at = partners.place
+        self.count = self.own.shape[0]
+        links.add("rc" + name, self.own.at[:, half_lanes(1 - core)], self.core, partners.core)
+        links.add("ry" + name, self.own.at[self.half(1 - y), half_lanes(core)], self.y, partners.y)
+        for shift in (1, 2, 3):
+            source = self.own.at[self.part(y, turn(z, shift)), half_lanes(core)]
+            links.add(f"rz{shift}{name}", source, self.z.at[shift - 1], partners.along[shift - 1])
+            piece = self.whole.at[self.part(y, z), half_lanes(core)]
+            links.add(f"gz{shift}{name}", piece, piece, partners.along[shift - 1])
+        piece = self.whole.at[self.half(y), half_lanes(core)]
+        links.add("gy" + name, piece, piece, partners.y)
+        piece = self.whole.at[:, half_lanes(core)]
+        links.add("gc" + name, piece, piece, partners.core)
+
+    def half(self, y):
+        return pl.ds(pl.multiple_of(y * (self.count // 2), self.count // 2), self.count // 2)
+
+    def part(self, y, z):
+        size = self.count // 8
+        return pl.ds(pl.multiple_of((4 * y + z) * size, size), size)
+
+    def over_z(self, stage):
+        return [f"{stage}{shift}{self.name}" for shift in (1, 2, 3)]
+
+    def begin(self):
+        self.links.start("rc" + self.name)
+
+    def sum_core(self, far):
+        lanes = half_lanes(self.place[2])
+        self.links.arrived("rc" + self.name, "hx" + self.name)
+        rows = far.got.shape[0]
+        total = self.own[:rows, lanes].astype(F32) + self.core[:rows].astype(F32) + far.got[...].astype(F32)
+        self.own[:rows, lanes] = total.astype(BF16)
+        self.links.start("ry" + self.name)
+
+    def sum_y(self):
+        z, y, core, x, at = self.place
+        self.links.arrived("ry" + self.name)
+        spot = (self.half(y), half_lanes(core))
+        self.own[spot] = add_low(self.own[spot], self.y[...])
+        self.links.start(*self.over_z("rz"))
+
+    def sum_z(self):
+        z, y, core, x, at = self.place
+        self.links.arrived(*self.over_z("rz"))
+        spot = (self.part(y, z), half_lanes(core))
+        part = self.own[spot].astype(F32)
+        for shift in range(3):
+            part = part + self.z[shift].astype(F32)
+        self.whole[spot] = part.astype(BF16)
+        self.links.start(*self.over_z("gz"))
+
+    def spread_y(self):
+        self.links.arrived(*self.over_z("gz"))
+        self.links.start("gy" + self.name)
+
+    def spread_core(self):
+        self.links.arrived("gy" + self.name)
+        self.links.start("gc" + self.name)
+
+    def done(self):
+        self.links.arrived("gc" + self.name)
+
+
+class Far:
+    def __init__(self, name, refs, links, partners):
+        self.name, self.links = name, links
+        self.sent, self.core, self.got = refs
+        self.place = z, y, core, x, at = partners.place
+        links.add("hc" + name, self.sent.at[:, half_lanes(1 - core)], self.core, partners.core)
+        links.add("hx" + name, self.sent.at[:, half_lanes(core)], self.got, partners.x)
+
+    def begin(self):
+        self.links.start("hc" + self.name)
+
+    def pass_on(self):
+        lanes = half_lanes(self.place[2])
+        self.links.arrived("hc" + self.name)
+        self.sent[:, lanes] = add_low(self.sent[:, lanes], self.core[...])
+        self.links.start("hx" + self.name)
+
+
+def half_lanes(core):
+    return pl.ds(pl.multiple_of(core * CORE_LANES, CORE_LANES), CORE_LANES)
+
+
+def narrow(value, into, first):
+    for piece in range(value.shape[0] // WIDE):
+        rows = value[WIDE * piece : WIDE * piece + HD]
+        spot = slice(first + HD * piece, first + HD * (piece + 1))
+        into[spot] = rows.astype(BF16)
 
 
 def backward_links_kernel(
     index_ref, x_ref, qkv_ref, proj_ref, mem_ref, taps_ref, gain_ref,
     packed_ref, keys_ref, att_ref, log_ref, normed_ref, grad_ref, gain_two_ref,
     d_first, d_second,
-    d_x_ref, small_out, first_out, second_out, w_out,
-    grad_normed, d_gain, d_w, d_taps,
-    far_sent, far_got, own, own_core, own_y, own_z, whole,
+    d_x_ref, small_out, first_out, second_out, proj_out, qkv_out,
+    grad_packed, d_gain, d_taps,
     small_mine, small_far, small_x, small_core, small_y, small_z,
-    first_total, first_core, first_one, first_two, first_z, first_result,
-    second_total, second_core, second_one, second_two, second_z, second_result,
-    send, recv, near,
+    first_result, second_result, send, recv, near, *rest,
 ):
     step = pl.program_id(0)
     last = pl.num_programs(0) - 1
     z, y, core, x, at = place()
     links = Links(send, recv)
-    beside, above, sibling = at(z, y, core, 1 - x), at(z, 1 - y, core, x), at(z, y, 1 - core, x)
-    along = [at(turn(z, shift), y, core, x) for shift in (1, 2, 3)]
-    here = (z, y, core, x, beside, above, sibling, along)
-    first = Scatter(
-        "f", "xyz", d_first, first_total, first_core, first_one, first_two, first_z, first_result, first_out,
-        links, near.at[pl.ds(0, 2)], here,
+    partners = Partners((z, y, core, x, at))
+    late = TILES - EARLY
+    first_refs, second_refs, rest = rest[:5], rest[5:10], rest[10:]
+    loads = [
+        pltpu.make_async_copy(d_first, first_refs[0], near.at[0]),
+        pltpu.make_async_copy(d_second, second_refs[0], near.at[1]),
+    ]
+    sums = [
+        (
+            Sum(f"f{tile}", "xy", None, [ref.at[tile] for ref in first_refs], links, partners),
+            Sum(f"s{tile}", "yx", EARLY + tile, [ref.at[tile] for ref in second_refs], links, partners),
+        )
+        for tile in range(late)
+    ]
+    first_done = [
+        pltpu.make_async_copy(first_result.at[tile], first_out.at[:, pl.ds(tile * TILE, TILE)], near.at[2 + tile])
+        for tile in range(late)
+    ]
+    second_done = pltpu.make_async_copy(second_result, second_out, near.at[2 + late])
+    units, far = {}, {}
+    for i, (name, rows, _) in enumerate(UNITS):
+        refs = rest[8 * i : 8 * i + 8]
+        units[name] = AllReduce(name, refs[:5], links, partners)
+        far[name] = Far(name, refs[5:], links, partners)
+    save = [
+        pltpu.make_async_copy(units[name].whole.at[pl.ds(0, rows)], out, near.at[3 + late + i])
+        for i, ((name, rows, _), out) in enumerate(zip(UNITS, (proj_out, qkv_out.at[0], qkv_out.at[1])))
+    ]
+    links.add("mx", small_far, small_x, partners.x)
+    links.add("mc", small_mine, small_core, partners.core)
+    links.add("my", small_core, small_y, partners.y)
+    for shift in (1, 2, 3):
+        links.add(f"mz{shift}", small_z.at[z], small_z.at[z], partners.along[shift - 1])
+
+    def proj_grads():
+        grad = grad_ref[...].reshape(-1, grad_ref.shape[2])
+        return [dot_tn(att_ref[pair].reshape(-1, PAIR * WIDE), grad) for pair in (0, 1)]
+
+    def far_proj():
+        for pair, value in enumerate(proj_grads()):
+            narrow(value, far["p"].sent, 192 * pair)
+        far["p"].begin()
+
+    def own_proj():
+        for pair, value in enumerate(proj_grads()):
+            narrow(value, units["p"].own, 192 * pair)
+        units["p"].begin()
+
+    def qkv_grad():
+        width = normed_ref.shape[2]
+        grad = grad_packed[lax.div(step, 4)].reshape(-1, PIECES * WIDE)
+        return dot_tn(grad, normed_ref[...].reshape(-1, width))
+
+    def far_qkv(name):
+        narrow(qkv_grad(), far[name].sent, 0)
+        far[name].begin()
+
+    def own_qkv(name):
+        narrow(qkv_grad(), units[name].own, 0)
+        units[name].begin()
+
+    def begin():
+        greet(partners.all())
+        for copy in loads:
+            copy.start()
+        d_gain[...] = jnp.zeros_like(d_gain)
+        d_taps[...] = jnp.zeros_like(d_taps)
+        for name in ("0", "1"):
+            padding = units[name].own.shape[0] - 576
+            units[name].own[576:] = jnp.zeros((padding, units[name].own.shape[1]), BF16)
+
+    def begin_sums():
+        for copy in loads:
+            copy.wait()
+        for pair in sums:
+            for one in pair:
+                one.begin()
+
+    def all_sums(stage):
+        for pair in sums:
+            for one in pair:
+                getattr(one, stage)()
+
+    def finish():
+        for tile, (one, two) in enumerate(sums):
+            one.finish(first_result.at[tile])
+            first_done[tile].start()
+
+            @pl.when(z == EARLY + tile)
+            def _(two=two):
+                two.finish(second_result)
+                second_done.start()
+
+    def at_steps(plan):
+        for when, acts in plan.items():
+
+            @pl.when(step == when)
+            def _(acts=acts):
+                for act in acts:
+                    act()
+
+    at_steps({0: [begin, far_proj], 8: [own_proj]})
+
+    @pl.when(step < 16)
+    def _():
+        pair = lax.rem(lax.div(step, 4) + 2, 4)
+        clip = lax.rem(step, 4)
+        here = pl.ds(clip, 1)
+        grad_packed[lax.div(step, 4), here] = backward_attention(
+            pair, mask_rows(index_ref[x, clip]), proj_ref.at[0], d_taps.at[lax.div(step, 4)],
+            mem_ref.at[0], taps_ref.at[0], packed_ref.at[0, 0], keys_ref.at[0, 0], att_ref.at[lax.rem(pair, 2), clip], log_ref,
+            grad_ref.at[clip],
+        )[None]
+
+    @pl.when(step >= 16)
+    def _():
+        clip = step - 16
+        grad = [
+            dot(grad_packed[slot, clip], qkv_ref[(slot + 2) % 4].reshape(PIECES * WIDE, -1)) for slot in range(4)
+        ]
+        grad = (grad[0] + grad[1]) + (grad[2] + grad[3])
+        d_x_ref[0], gain = input_grad(x_ref[0], grad, gain_ref, grad_ref[clip])
+        d_gain[...] += gain
+
+    p, zero, one = (units[name] for name, _, _ in UNITS)
+    at_steps(
+        {
+            0: [begin_sums],
+            1: [far["p"].pass_on],
+            2: [lambda: all_sums("core")],
+            3: [lambda: far_qkv("0")],
+            4: [far["0"].pass_on],
+            5: [lambda: all_sums("first")],
+            7: [lambda: far_qkv("1"), lambda: all_sums("second")],
+            8: [far["1"].pass_on],
+            9: [lambda: p.sum_core(far["p"])],
+            10: [finish],
+            11: [lambda: own_qkv("0"), p.sum_y],
+            12: [lambda: zero.sum_core(far["0"])],
+            13: [p.sum_z],
+            14: [zero.sum_y, p.spread_y],
+            15: [lambda: own_qkv("1"), zero.sum_z, p.spread_core],
+            16: [lambda: one.sum_core(far["1"])],
+            17: [zero.spread_y, p.done, save[0].start],
+        }
     )
-    second = Scatter(
-        "s", "yzx", d_second, second_total, second_core, second_one, second_two, second_z, second_result, second_out,
-        links, near.at[pl.ds(2, 2)], here,
-    )
-
-    def lanes(core):
-        return pl.ds(pl.multiple_of(core * THIRD, THIRD), THIRD)
-
-    def rows(y, z):
-        return pl.ds(pl.multiple_of(y * THIRD + z * PART, PART), PART)
-
-    def half(y):
-        return pl.ds(pl.multiple_of(y * THIRD, THIRD), THIRD)
-
-    for i in (0, 1):
-        links.add(f"far{i}", far_sent.at[i], far_got.at[i], beside)
-        links.add(f"rc{i}", own.at[i, :, lanes(1 - core)], own_core.at[i], sibling)
-        links.add(f"ry{i}", own.at[i, half(1 - y), lanes(core)], own_y.at[i], above)
-        for shift in (1, 2, 3):
-            links.add(
-                f"rz{i}{shift}", own.at[i, rows(y, turn(z, shift)), lanes(core)], own_z.at[i, shift - 1], along[shift - 1]
-            )
-        piece = whole.at[i, rows(y, z), lanes(core)]
-        for shift in (1, 2, 3):
-            links.add(f"gz{i}{shift}", piece, piece, along[shift - 1])
-        piece = whole.at[i, half(y), lanes(core)]
-        links.add(f"gy{i}", piece, piece, above)
-        piece = whole.at[i, :, lanes(core)]
-        links.add(f"gc{i}", piece, piece, sibling)
-    links.add("mx", small_far, small_x, beside)
-    links.add("mc", small_mine, small_core, sibling)
-    links.add("my", small_core, small_y, above)
-    for shift in (1, 2, 3):
-        links.add(f"mz{shift}", small_z.at[z], small_z.at[z], along[shift - 1])
-
-    @pl.when(step == 0)
-    def _():
-        greet([beside, above, sibling] + along)
-        first.begin()
-        second.begin()
-
-    backward_step(
-        lax.rem(lax.div(step, 4) + 2, 4), lax.rem(step, 4), step < 4, step >= 12,
-        mask_rows(index_ref[x, lax.rem(step, 4)]),
-        qkv_ref.at[0], proj_ref.at[0], d_w, d_taps.at[lax.div(step, 4)],
-        x_ref, mem_ref, taps_ref, gain_ref,
-        packed_ref, keys_ref, att_ref, log_ref, normed_ref, grad_ref,
-        d_x_ref, d_gain, grad_normed,
-    )
-
-    def sum_core(i):
-        links.arrived(f"rc{i}")
-        own[i, :, lanes(core)] = add_low(own[i, :, lanes(core)], own_core[i])
-        links.start(f"ry{i}")
-
-    def sum_y(i):
-        links.arrived(f"ry{i}")
-        own[i, half(y), lanes(core)] = add_low(own[i, half(y), lanes(core)], own_y[i])
-        links.start(*[f"rz{i}{shift}" for shift in (1, 2, 3)])
-
-    def sum_z(i):
-        links.arrived(*[f"rz{i}{shift}" for shift in (1, 2, 3)])
-        part = own[i, rows(y, z), lanes(core)].astype(F32)
-        for shift in range(3):
-            part = part + own_z[i, shift].astype(F32)
-        whole[i, rows(y, z), lanes(core)] = part.astype(BF16)
-        links.start(*[f"gz{i}{shift}" for shift in (1, 2, 3)])
-
-    def spread_y(i):
-        links.arrived(*[f"gz{i}{shift}" for shift in (1, 2, 3)])
-        links.start(f"gy{i}")
-
-    def spread_core(i):
-        links.arrived(f"gy{i}")
-        links.start(f"gc{i}")
-
-    def far(i):
-        unpad(d_w, far_sent.at[i])
-        links.start(f"far{i}")
-
-    def mine(i):
-        links.arrived(f"far{i}")
-        unpad(d_w, own.at[i], far_got.at[i])
-        links.start(f"rc{i}")
-
-    plan = {
-        1: [lambda: first.step(0)],
-        2: [lambda: second.step(0)],
-        3: [lambda: far(0)],
-        7: [lambda: far(1), lambda: first.step(1)],
-        8: [lambda: second.step(1)],
-        10: [lambda: first.step(2)],
-        11: [lambda: mine(0)],
-        12: [lambda: sum_core(0)],
-        13: [lambda: sum_y(0), lambda: first.step(3)],
-        14: [lambda: sum_z(0), lambda: second.step(2)],
-    }
-    for when, acts in plan.items():
-
-        @pl.when(step == when)
-        def _(acts=acts):
-            for act in acts:
-                act()
 
     @pl.when(step == last)
     def _():
-        mine(1)
         for i, target in ((2, small_mine), (0, small_far)):
             target[...] = jnp.zeros_like(target)
             target[0:1] = d_gain[...]
@@ -586,35 +838,38 @@
             for j in (0, 1):
                 target[8:16, WIDE * j : WIDE * (j + 1)] = d_taps[i + j].reshape(8, WIDE)
         links.start("mx")
-        spread_y(0)
-        sum_core(1)
+        one.sum_y()
         links.arrived("mx")
         small_mine[...] += small_x[...]
         links.start("mc")
-        spread_core(0)
-        sum_y(1)
+        zero.spread_core()
         links.arrived("mc")
         small_core[...] += small_mine[...]
         links.start("my")
-        second.step(3)
-        sum_z(1)
+        one.sum_z()
         links.arrived("my")
         small_z[pl.ds(z, 1)] = (small_y[...] + small_core[...])[None]
         links.start("mz1", "mz2", "mz3")
-        spread_y(1)
-        spread_core(1)
+        zero.done()
+        save[1].start()
+        one.spread_y()
         links.arrived("mz1", "mz2", "mz3")
         small_out[...] = (small_z[0] + small_z[1]) + (small_z[2] + small_z[3])
-        links.arrived("gc0", "gc1")
-        save = pltpu.make_async_copy(whole, w_out, near.at[4])
-        save.start()
-        save.wait()
-        first.done.wait()
-        second.done.wait()
+        one.spread_core()
+        one.done()
+        save[2].start()
+        for copy in save + first_done:
+            copy.wait()
+        for tile in range(late):
+            pl.when(z == EARLY + tile)(lambda: second_done.wait())
         links.sent()
 
 
 VMEM_LIMIT = 60 << 20
+CHUNK = 800
+TILE = 768
+TILES = 4
+EARLY = 2
 
 
 def compiler_params(dims):
@@ -756,9 +1011,10 @@
         (proj_own, proj_all.at[pl.ds(0, 2), :, pl.ds(0, HD)]),
         (tail_own.at[:, x], tail_all.at[0]),
         (taps_own, taps_all.at[pl.ds(0, 2)]),
+        (mem_own.at[0, x, :, :, pl.ds(0, MAIN)], mem_all.at[0, 0]),
         (hidden_own, first_all.at[me]),
         (output_own, second_all.at[me]),
-    ] + [(mem_own.at[clip, x, :, :, pl.ds(0, MAIN)], mem_all.at[0, clip]) for clip in range(clips)]
+    ] + [(mem_own.at[clip, x, :, :, pl.ds(0, MAIN)], mem_all.at[0, clip]) for clip in range(1, clips)]
     local = [pltpu.make_async_copy(src, dst, near.at[i]) for i, (src, dst) in enumerate(local)]
     saved = [
         (qkv_all, qkv_out),
@@ -782,8 +1038,13 @@
                     qkv_all[pair, head, piece, HD:] = jnp.zeros((WIDE - HD, qkv_all.shape[-1]), BF16)
                 proj_all[pair, head, HD:] = jnp.zeros((WIDE - HD, qkv_all.shape[-1]), BF16)
 
-        for copy in local:
+        for copy in local[:5]:
             copy.wait()
+
+    def settle():
+        for copy in local[5:]:
+            copy.wait()
+        saved[3].start()
 
     def hop(number, kinds):
         for kind in kinds:
@@ -820,7 +1081,7 @@
         saved[4 + clip].start()
 
     plan = {
-        1: [saved[3].start],
+        1: [settle],
         2: [lambda: begin("qp"), lambda: links.start("m0")],
         3: [lambda: begin("01"), lambda: links.start("m1")],
         4: [lambda: hop(1, "qp")],
@@ -894,7 +1155,10 @@
             pl.BlockSpec((1, TPC, width), lambda s: (late(s), 0, 0)),
             pl.BlockSpec(gain_one.shape, lambda s: (0,)),
             pl.BlockSpec(gain_two.shape, lambda s: (0,)),
-        ] + [anywhere] * 7,
+        ] + [anywhere] * 5 + [
+            pl.BlockSpec(hidden_weight.shape, lambda s: (0, 0)),
+            pl.BlockSpec(output_weight.shape, lambda s: (0, 0)),
+        ],
         out_specs=[
             pl.BlockSpec((1, 1, ROWS, packed_width), lambda s: (pair_of(s), clip_of(s), 0, 0)),
             pl.BlockSpec((1, 1, PAIR, 2, SIDE, WIDE), lambda s: (pair_of(s), clip_of(s), 0, 0, 0, 0)),
@@ -1004,10 +1268,6 @@
     return pl.BlockSpec(shape, lambda t: (0,) * len(shape), pipeline_mode=pl.Buffered(1))
 
 
-CHUNK = 800
-TILE = 768
-
-
 def mlp(normed, cot, first, second, middle, gain):
     rows, width = normed.shape
     hidden = first.shape[1]
@@ -1050,6 +1310,75 @@
         ],
         compiler_params=compiler_params(1),
         name="mlp",
+    )(normed, cot, first, second, middle, gain)
+
+
+def sum_scratch(lead, planes, shape):
+    return [
+        pltpu.VMEM(lead + dims + shape, BF16)
+        for dims in ((planes, 2, 2, 2), (planes, 2, 2), (planes, 2), (planes,), (3,))
+    ]
+
+
+def mlp_links(normed, cot, first, second, middle, gain):
+    rows, width = normed.shape
+    hidden = first.shape[1]
+    clips = rows // ROWS
+    tile_at = lambda t: jnp.minimum(t, TILES - 1)
+    clip_at = lambda t: jnp.maximum(t - TILES, 0)
+    first_rows, second_rows = width // 32, hidden // 32
+    anywhere = pl.BlockSpec(memory_space=pl.ANY)
+    return pl.pallas_call(
+        mlp_links_kernel,
+        grid=(TILES + clips,),
+        in_specs=[
+            once((rows, width)),
+            once((rows, width)),
+            pl.BlockSpec((width, TILE), lambda t: (0, tile_at(t))),
+            pl.BlockSpec((TILE, width), lambda t: (tile_at(t), 0)),
+            anywhere,
+            pl.BlockSpec(gain.shape, lambda t: (0,)),
+        ],
+        out_specs=[
+            pl.BlockSpec((1, TPC, width), lambda t: (clip_at(t), 0, 0)),
+            pl.BlockSpec((ROWS, width), lambda t: (clip_at(t), 0)),
+            once((1, width)),
+        ] + [anywhere] * 4,
+        out_shape=[
+            shaped((clips, TPC, width), BF16),
+            shaped((rows, width), BF16),
+            shaped((1, width), F32),
+            shaped((first_rows, EARLY * TILE), F32),
+            shaped((second_rows, width), F32),
+            shaped((TILES - EARLY, 4, 2, 2, 2, first_rows, TILE), BF16),
+            shaped((TILES - EARLY, 1, 2, 2, 2, second_rows, width), BF16),
+        ],
+        scratch_shapes=[
+            pltpu.VMEM((rows, width), F32),
+            pltpu.VMEM((rows, width), F32),
+            pltpu.VMEM((rows, width), F32),
+            pltpu.VMEM((rows, TILE), BF16),
+            pltpu.VMEM((rows, TILE), BF16),
+            pltpu.SemaphoreType.DMA((1,)),
+        ]
+        + sum_scratch((EARLY,), 4, (first_rows, TILE))
+        + sum_scratch((EARLY,), 1, (second_rows, width))
+        + [
+            pltpu.VMEM((TILES - EARLY, 4, 2, 2, 2, first_rows, TILE), BF16),
+            pltpu.VMEM((TILES - EARLY, 1, 2, 2, 2, second_rows, width), BF16),
+            pltpu.VMEM((EARLY, first_rows, TILE), F32),
+            pltpu.VMEM((second_rows, width), F32),
+            pltpu.SemaphoreType.DMA((12 * EARLY,)),
+            pltpu.SemaphoreType.DMA((12 * EARLY,)),
+            pltpu.SemaphoreType.DMA((2 * TILES,)),
+        ],
+        compiler_params=pltpu.CompilerParams(
+            dimension_semantics=("arbitrary",),
+            vmem_limit_bytes=VMEM_LIMIT,
+            collective_id=2,
+            has_side_effects=True,
+        ),
+        name="mlp_links",
     )(normed, cot, first, second, middle, gain)
 
 
@@ -1100,29 +1429,32 @@
 ):
     clips, width = x.shape[0], x.shape[2]
     packed_width = PIECES * WIDE
-    weight_rows = (PIECES + PAIR) * WIDE
-    low_rows = weight_rows // WIDE * HD
-    pair_at = lambda s: lax.rem(lax.div(s, 4) + 2, 4)
-    clip_at = lambda s: lax.rem(s, 4)
-    late = lambda s: jnp.where(s < 12, 0, s - 12)
+    steps = 4 * clips
+    early = lambda s: jnp.minimum(s, steps - 1)
+    pair_at = lambda s: lax.rem(lax.div(early(s), clips) + 2, 4)
+    clip_at = lambda s: lax.rem(early(s), clips)
+    late = lambda s: jnp.maximum(s - steps, 0)
     anywhere = pl.BlockSpec(memory_space=pl.ANY)
     per_step = lambda s: (pair_at(s), clip_at(s), 0, 0)
     small = (16, width)
-
-    def scatter_scratch(shape, order):
-        one, two, last = ((4, 2), (4,), (3,)) if order == "xyz" else ((4, 2), (), (3, 2))
-        return [
-            pltpu.VMEM(lead + shape, BF16) for lead in ((4, 2, 2), (4, 2, 2), one, two, last)
-        ] + [pltpu.VMEM(shape, F32)]
-
-    first_shape, second_shape = d_first.shape[4:], d_second.shape[4:]
+    left = d_first.shape[0]
+    first_shape, second_shape = d_first.shape[-2:], d_second.shape[-2:]
+    units = []
+    for _, rows, padded in UNITS:
+        units += [
+            pltpu.VMEM(shape, BF16)
+            for shape in (
+                (padded, width), (padded, CORE_LANES), (padded // 2, CORE_LANES), (3, padded // 8, CORE_LANES), (padded, width),
+                (rows, width), (rows, CORE_LANES), (rows, CORE_LANES),
+            )
+        ]
     return pl.pallas_call(
         backward_links_kernel,
-        grid=(4 * clips,),
+        grid=(steps + clips,),
         in_specs=[
             pl.BlockSpec(memory_space=pltpu.SMEM),
             pl.BlockSpec((1, TPC, width), lambda s: (late(s), 0, 0)),
-            pl.BlockSpec((1,) + qkv.shape[1:], lambda s: (pair_at(s), 0, 0, 0, 0)),
+            once(qkv.shape),
             pl.BlockSpec((1,) + proj.shape[1:], lambda s: (pair_at(s), 0, 0, 0)),
             pl.BlockSpec(
                 (None, 1, PAIR, 2 * HD, MAIN),
@@ -1132,10 +1464,10 @@
             pl.BlockSpec(gain.shape, lambda s: (0,)),
             pl.BlockSpec((1, 1, ROWS, packed_width), per_step),
             pl.BlockSpec((1, 1, PAIR, 2, SIDE, WIDE), lambda s: per_step(s) + (0, 0)),
-            pl.BlockSpec((1, 1, ROWS, PAIR * WIDE), per_step),
+            pl.BlockSpec((2, clips, ROWS, PAIR * WIDE), lambda s: (lax.div(pair_at(s), 2), 0, 0, 0)),
             pl.BlockSpec((1, ROWS, WIDE), lambda s: (clip_at(s), 0, 0)),
-            pl.BlockSpec((1, ROWS, width), lambda s: (clip_at(s), 0, 0)),
-            pl.BlockSpec((ROWS, width), lambda s: (clip_at(s), 0)),
+            once((clips, ROWS, width)),
+            once((clips, ROWS, width)),
             pl.BlockSpec((1, width), lambda s: (0, 0)),
             anywhere,
             anywhere,
@@ -1143,39 +1475,32 @@
         out_specs=[
             pl.BlockSpec((1, TPC, width), lambda s: (late(s), 0, 0)),
             pl.BlockSpec(small, lambda s: (0, 0)),
-            anywhere,
-            anywhere,
-            anywhere,
-        ],
+        ] + [anywhere] * 4,
         out_shape=[
             shaped((clips, TPC, width), BF16),
             shaped(small, F32),
-            shaped(first_shape, F32),
+            shaped((first_shape[0], left * TILE), F32),
             shaped(second_shape, F32),
-            shaped((2, low_rows, width), BF16),
+            shaped((UNITS[0][1], width), BF16),
+            shaped((2, UNITS[1][1], width), BF16),
         ],
         scratch_shapes=[
-            pltpu.VMEM((clips, ROWS, width), F32),
+            pltpu.VMEM((4, clips, ROWS, packed_width), BF16),
             pltpu.VMEM((1, width), F32),
-            pltpu.VMEM((weight_rows, width), F32),
             pltpu.VMEM((4, PAIR, 4, WIDE), F32),
-            pltpu.VMEM((2, low_rows, width), BF16),
-            pltpu.VMEM((2, low_rows, width), BF16),
-            pltpu.VMEM((2, low_rows, width), BF16),
-            pltpu.VMEM((2, low_rows, THIRD), BF16),
-            pltpu.VMEM((2, THIRD, THIRD), BF16),
-            pltpu.VMEM((2, 3, PART, THIRD), BF16),
-            pltpu.VMEM((2, low_rows, width), BF16),
         ]
         + [pltpu.VMEM(small, F32)] * 5
-        + [pltpu.VMEM((4,) + small, F32)]
-        + scatter_scratch(first_shape, "xyz")
-        + scatter_scratch(second_shape, "yzx")
         + [
+            pltpu.VMEM((4,) + small, F32),
+            pltpu.VMEM((left,) + first_shape, F32),
+            pltpu.VMEM(second_shape, F32),
             pltpu.SemaphoreType.DMA((BACKWARD_COPIES,)),
             pltpu.SemaphoreType.DMA((BACKWARD_COPIES,)),
-            pltpu.SemaphoreType.DMA((5,)),
-        ],
+            pltpu.SemaphoreType.DMA((6 + left,)),
+        ]
+        + sum_scratch((left,), 4, first_shape)
+        + sum_scratch((left,), 1, second_shape)
+        + units,
         compiler_params=pltpu.CompilerParams(
             dimension_semantics=("arbitrary",),
             vmem_limit_bytes=VMEM_LIMIT,
@@ -1183,9 +1508,7 @@
             has_side_effects=True,
         ),
         name="attention_backward_links",
-    )(
-        index, x, qkv, proj, mem, taps, gain, packed, keys, att, log, normed, grad, gain_two, d_first, d_second
-    )
+    )(index, x, qkv, proj, mem, taps, gain, packed, keys, att, log, normed, grad, gain_two, d_first, d_second)
 
 
 def group_gather(own, heads, fetch=None):
@@ -1279,23 +1602,24 @@
         packed, keys, att, log, normed, middle, normed_two, cot_rows = attention_forward(
             x, cot, w_all, mem_all, tail, side_mask, main_mask, taps_all, gain_one, gain_two
         )
-    outputs, grad, d_first, d_second, d_gain_two = mlp(
-        normed_two.reshape(clips * ROWS, width),
-        cot_rows.reshape(clips * ROWS, width),
-        first,
-        second,
-        middle.reshape(clips * ROWS, width),
-        gain_two,
+    rows = clips * ROWS
+    mlp_args = (
+        normed_two.reshape(rows, width), cot_rows.reshape(rows, width), first, second, middle.reshape(rows, width), gain_two
     )
     if linked:
-        d_x, small, d_first, d_second, d_w = attention_backward_links(
+        outputs, grad, d_gain_two, d_first, d_second, first_left, second_left = mlp_links(*mlp_args)
+    else:
+        outputs, grad, d_first, d_second, d_gain_two = mlp(*mlp_args)
+    if linked:
+        d_x, small, last_first, last_second, d_proj, d_qkv = attention_backward_links(
             clip_index.T, x, qkv_all, proj_all, mem_all, taps_all, gain_one,
-            packed, keys, att, log, normed, grad, d_gain_two,
-            d_first.reshape(4, 2, 2, 2, -1, d_first.shape[1]), d_second.reshape(4, 2, 2, 2, -1, width),
+            packed, keys, att, log, normed, grad.reshape(clips, ROWS, width), d_gain_two,
+            first_left, second_left,
         )
-        qkv_rows = PAIR * 3 * HD
-        d_qkv = d_w[:, :qkv_rows].astype(F32).reshape(own_heads, 3 * HD, width)
-        d_proj = d_w[:, qkv_rows:].astype(F32).reshape(own_heads, HD, width)
+        d_first = jnp.concatenate([d_first, last_first], axis=1)
+        d_second = jnp.where(lax.axis_index("batch") // (batches // TILES) >= EARLY, last_second, d_second)
+        d_qkv = d_qkv.astype(F32).reshape(own_heads, 3 * HD, width)
+        d_proj = d_proj.astype(F32).reshape(own_heads, HD, width)
         d_taps = small[8:, : 2 * WIDE].reshape(PAIR, 4, 2, WIDE).transpose(2, 0, 1, 3)[..., :HD]
         share = width // (batches * heads)
         start = (lax.axis_index("batch") * heads + me) * share

time: 316 us -> 312 us (0.987)
  Pallas kernels: 298 us -> 293 us
  other arithmetic: 3.79 us -> 7.81 us
    pallas_call x1, Pallas kernels: 94 us -> 86.1 us  [attention_forward_links(): pl.pallas_call(forward_links_kernel, grid=(4 * clips,), in_specs=[pl.Bloc...]
where the time goes in v5:
time: 312 us; the launch traced here: 310 us
  Pallas kernels  293 us (94%)
  local copies, waits for them, and re-layouts  8.41 us (3%)
  other arithmetic  7.81 us (3%)
    pallas_call x1, Pallas kernels, attention_backward_links(): pl.pallas_call(backward_links_kernel, grid=(steps + clips,), in_specs=[pl...  132 us
    pallas_call x1, Pallas kernels, attention_forward_links(): pl.pallas_call(forward_links_kernel, grid=(4 * clips,), in_specs=[pl.Bloc...  86.1 us
    pallas_call x1, Pallas kernels, mlp_links(): pl.pallas_call(mlp_links_kernel, grid=(TILES + clips,), in_specs=[once((r...  74.9 us

profile of v5, /device:TPU:0, one launch (start us, length us, event | category | flops | bytes accessed | tf_op | source)
XLA Modules:
  0.0 310.1 jit_solution(18211631868276777182)
XLA Ops:
  0.6 0.0 copy-start.5
  0.7 1.6 slice.24
  2.2 0.7 copy.20
  2.9 0.7 pad_bitcast_fusion.tail_own
  3.6 0.0 copy-done.5
  3.6 0.6 convert.4.taps_own
  4.2 86.1 %attention_forward_links.1 = (bf16[4,4,400,768]{3,2,1,0:T(8,128)(2,1)}, bf16[4,4,2,2,256,128]{5,4,3,2,1,0:T(8,128)(2,1)}, bf16[4,4,400,256]{3,2,1,0:T(8,128)(2,1...) custom-call(s32[2,4]{1,0:T(2,128)} %bitcast.60, ...), custom_call_target="tpu_custom_call" | custom-call | tf_op jit(solution)/shard_map/attention_forward_links/pallas_call | solution.py:1149
  90.3 74.9 %mlp_links.1 = (bf16[4,392,768]{2,1,0:T(8,128)(2,1)}, bf16[1600,768]{1,0:T(8,128)(2,1)}, f32[1,768]{1,0:T(1,128)}, f32[24,1536]{1,0:T(8,128)}, f32[96,768]{1,0:T...) custom-call(bf16[1600,768]{1,0:T(8,128)(2,1)} %bitcast.48, ...), custom_call_target="tpu_custom_call" | custom-call | tf_op jit(solution)/shard_map/mlp_links/pallas_call | solution.py:1331
  165.2 0.0 copy-start.3
  165.2 0.0 copy-start.4
  165.3 131.9 %attention_backward_links.1 = (bf16[4,392,768]{2,1,0:T(8,128)(2,1)}, f32[16,768]{1,0:T(8,128)}, f32[24,1536]{1,0:T(8,128)}, f32[96,768]{1,0:T(8,128)}, bf16[384,...) custom-call(s32[2,4]{1,0:T(2,128)} %bitcast.61, bf16[4,392,768]{2,1,0:T(8,128)(2,1)} %bitcast.42, ...), custom_call_target="tpu_custom_call" | custom-call | tf_op jit(solution)/shard_map/attention_backward_links/pallas_call | solution.py:1451
  297.2 0.0 copy-done.3
  297.2 0.8 broadcast_select_fusion
  298.0 0.0 copy-done.4
  298.0 1.6 pad_maximum_fusion
  299.6 0.0 copy-start.2
  299.6 0.0 copy-start
  299.6 3.7 %convert_bitcast_fusion = f32[768,4,288]{0,2,1:T(8,128)} fusion(bf16[4,288,768]{2,1,0:T(8,128)(2,1)} %bitcast.53), kind=kLoop, calls=%fused_computation | loop fusion | flops 884736 | bytes 5308416 | tf_op jit(solution)/shard_map/transpose | solution.py:1630
  303.3 0.0 copy-done.2
  303.3 1.1 convert.6
  304.4 0.7 slice.21
  305.2 0.1 constant_dynamic-slice_fusion
  305.3 0.5 slice_bitcast_fusion
  305.8 0.7 slice.19
  306.5 0.0 copy-start.1
  306.5 0.6 copy.21
  307.1 0.0 copy-done
  307.1 1.4 copy.26
  308.5 0.0 copy-done.1
  308.5 1.4 copy.27
  (1 shorter events, 0.0 us)
Async XLA Ops:
  0.6 2.9 copy-start.5
  165.2 132.0 %copy-start.3 = (f32[96,768]{1,0:T(8,128)S(1)}, f32[96,768]{1,0:T(8,128)}, u32[]{:S(2)}) copy-start(f32[96,768]{1,0:T(8,128)} %get-tuple-element.62) | copy-start | bytes 884740
  165.2 132.7 %copy-start.4 = (f32[24,1536]{1,0:T(8,128)S(1)}, f32[24,1536]{1,0:T(8,128)}, u32[]{:S(2)}) copy-start(f32[24,1536]{1,0:T(8,128)} %get-tuple-element.59) | copy-start | bytes 442372
  299.6 3.7 %copy-start.2 = (bf16[384,768]{1,0:T(8,128)(2,1)S(1)}, bf16[384,768]{1,0:T(8,128)(2,1)}, u32[]{:S(2)}) copy-start(bf16[384,768]{1,0:T(8,128)(2,1)} %get-tuple-element.57) | copy-start | bytes 1769476
  299.6 7.5 %copy-start = (bf16[4,392,768]{2,1,0:T(8,128)(2,1)S(1)}, bf16[4,392,768]{2,1,0:T(8,128)(2,1)}, u32[]{:S(2)}) copy-start(bf16[4,392,768]{2,1,0:T(8,128)(2,1)} %get-tuple-element.41) | copy-start | bytes 7225348
  306.5 2.0 copy-start.1

commit v6 on v5

--- a/solution.py
+++ b/solution.py
@@ -567,73 +567,88 @@
         into[narrow] = rows.astype(BF16)
 
 
-BACKWARD_COPIES = 96
+BACKWARD_COPIES = 112
 CORE_LANES = 384
-UNITS = (("p", 384, 384), ("0", 576, 640), ("1", 576, 640))
+UNITS = (("p", 384, 384, "yz"), ("0", 576, 640, "yz"), ("1", 384, 384, "yz"), ("2", 192, 256, "zy"))
+FAR = (("p", 384), ("0", 576), ("1", 576))
 
 
 class AllReduce:
-    def __init__(self, name, refs, links, partners):
-        self.name, self.links = name, links
-        self.own, self.core, self.y, self.z, self.whole = refs
+    def __init__(self, name, order, refs, links, partners):
+        self.name, self.order, self.links = name, order, links
+        self.own, self.core, self.got_y, self.got_z, self.whole = refs
         self.place = z, y, core, x, at = partners.place
         self.count = self.own.shape[0]
+        mine, lanes = self.part(y, z), half_lanes(core)
         links.add("rc" + name, self.own.at[:, half_lanes(1 - core)], self.core, partners.core)
-        links.add("ry" + name, self.own.at[self.half(1 - y), half_lanes(core)], self.y, partners.y)
+        if order == "yz":
+            to_y, to_z = self.rows(1 - y, 2), [self.part(y, turn(z, shift)) for shift in (1, 2, 3)]
+            spread = self.rows(y, 2)
+        else:
+            to_y, to_z = self.part(1 - y, z), [self.rows(turn(z, shift), 4) for shift in (1, 2, 3)]
+            spread = self.rows(z, 4)
+        links.add("ry" + name, self.own.at[to_y, lanes], self.got_y, partners.y)
+        back_z, back_y = (mine, spread) if order == "yz" else (spread, mine)
+        piece = self.whole.at[back_y, lanes]
+        links.add("gy" + name, piece, piece, partners.y)
         for shift in (1, 2, 3):
-            source = self.own.at[self.part(y, turn(z, shift)), half_lanes(core)]
-            links.add(f"rz{shift}{name}", source, self.z.at[shift - 1], partners.along[shift - 1])
-            piece = self.whole.at[self.part(y, z), half_lanes(core)]
+            links.add(
+                f"rz{shift}{name}", self.own.at[to_z[shift - 1], lanes], self.got_z.at[shift - 1], partners.along[shift - 1]
+            )
+            piece = self.whole.at[back_z, lanes]
             links.add(f"gz{shift}{name}", piece, piece, partners.along[shift - 1])
-        piece = self.whole.at[self.half(y), half_lanes(core)]
-        links.add("gy" + name, piece, piece, partners.y)
-        piece = self.whole.at[:, half_lanes(core)]
+        piece = self.whole.at[:, lanes]
         links.add("gc" + name, piece, piece, partners.core)
 
-    def half(self, y):
-        return pl.ds(pl.multiple_of(y * (self.count // 2), self.count // 2), self.count // 2)
+    def rows(self, at, parts):
+        size = self.count // parts
+        return pl.ds(pl.multiple_of(at * size, size), size)
 
     def part(self, y, z):
-        size = self.count // 8
-        return pl.ds(pl.multiple_of((4 * y + z) * size, size), size)
-
-    def over_z(self, stage):
-        return [f"{stage}{shift}{self.name}" for shift in (1, 2, 3)]
+        return self.rows(4 * y + z if self.order == "yz" else 2 * z + y, 8)
+
+    def stage(self, which, axis):
+        return [f"{which}z{shift}{self.name}" for shift in (1, 2, 3)] if axis == "z" else [which + "y" + self.name]
 
     def begin(self):
         self.links.start("rc" + self.name)
 
     def sum_core(self, far):
         lanes = half_lanes(self.place[2])
-        self.links.arrived("rc" + self.name, "hx" + self.name)
-        rows = far.got.shape[0]
-        total = self.own[:rows, lanes].astype(F32) + self.core[:rows].astype(F32) + far.got[...].astype(F32)
+        self.links.arrived("rc" + self.name)
+        rows = far.shape[0]
+        total = self.own[:rows, lanes].astype(F32) + self.core[:rows].astype(F32) + far[...].astype(F32)
         self.own[:rows, lanes] = total.astype(BF16)
-        self.links.start("ry" + self.name)
-
-    def sum_y(self):
+        self.links.start(*self.stage("r", self.order[0]))
+
+    def taken(self, axis, rows):
+        part = self.own[rows, half_lanes(self.place[2])].astype(F32)
+        for got in [self.got_y] if axis == "y" else [self.got_z.at[shift] for shift in range(3)]:
+            part = part + got[...].astype(F32)
+        return part.astype(BF16)
+
+    def sum_one(self):
         z, y, core, x, at = self.place
-        self.links.arrived("ry" + self.name)
-        spot = (self.half(y), half_lanes(core))
-        self.own[spot] = add_low(self.own[spot], self.y[...])
-        self.links.start(*self.over_z("rz"))
-
-    def sum_z(self):
+        axis = self.order[0]
+        self.links.arrived(*self.stage("r", axis))
+        rows = self.rows(y, 2) if axis == "y" else self.rows(z, 4)
+        self.own[rows, half_lanes(core)] = self.taken(axis, rows)
+        self.links.start(*self.stage("r", self.order[1]))
+
+    def sum_two(self):
         z, y, core, x, at = self.place
-        self.links.arrived(*self.over_z("rz"))
-        spot = (self.part(y, z), half_lanes(core))
-        part = self.own[spot].astype(F32)
-        for shift in range(3):
-            part = part + self.z[shift].astype(F32)
-        self.whole[spot] = part.astype(BF16)
-        self.links.start(*self.over_z("gz"))
-
-    def spread_y(self):
-        self.links.arrived(*self.over_z("gz"))
-        self.links.start("gy" + self.name)
+        axis = self.order[1]
+        self.links.arrived(*self.stage("r", axis))
+        rows = self.part(y, z)
+        self.whole[rows, half_lanes(core)] = self.taken(axis, rows)
+        self.links.start(*self.stage("g", axis))
+
+    def spread_one(self):
+        self.links.arrived(*self.stage("g", self.order[1]))
+        self.links.start(*self.stage("g", self.order[0]))
 
     def spread_core(self):
-        self.links.arrived("gy" + self.name)
+        self.links.arrived(*self.stage("g", self.order[0]))
         self.links.start("gc" + self.name)
 
     def done(self):
@@ -675,7 +690,7 @@
     d_first, d_second,
     d_x_ref, small_out, first_out, second_out, proj_out, qkv_out,
     grad_packed, d_gain, d_taps,
-    small_mine, small_far, small_x, small_core, small_y, small_z,
+    small_mine, small_far, small_got, small_all,
     first_result, second_result, send, recv, near, *rest,
 ):
     step = pl.program_id(0)
@@ -702,23 +717,42 @@
     ]
     second_done = pltpu.make_async_copy(second_result, second_out, near.at[2 + late])
     units, far = {}, {}
-    for i, (name, rows, _) in enumerate(UNITS):
-        refs = rest[8 * i : 8 * i + 8]
-        units[name] = AllReduce(name, refs[:5], links, partners)
-        far[name] = Far(name, refs[5:], links, partners)
+    for i, (name, _, _, order) in enumerate(UNITS):
+        units[name] = AllReduce(name, order, rest[5 * i : 5 * i + 5], links, partners)
+    rest = rest[5 * len(UNITS) :]
+    for i, (name, _) in enumerate(FAR):
+        far[name] = Far(name, rest[3 * i : 3 * i + 3], links, partners)
+    targets = (proj_out, qkv_out.at[0], qkv_out.at[1, pl.ds(0, 384)], qkv_out.at[1, pl.ds(384, 192)])
     save = [
         pltpu.make_async_copy(units[name].whole.at[pl.ds(0, rows)], out, near.at[3 + late + i])
-        for i, ((name, rows, _), out) in enumerate(zip(UNITS, (proj_out, qkv_out.at[0], qkv_out.at[1])))
+        for i, ((name, rows, _, _), out) in enumerate(zip(UNITS, targets))
     ]
-    links.add("mx", small_far, small_x, partners.x)
-    links.add("mc", small_mine, small_core, partners.core)
-    links.add("my", small_core, small_y, partners.y)
-    for shift in (1, 2, 3):
-        links.add(f"mz{shift}", small_z.at[z], small_z.at[z], partners.along[shift - 1])
+    diagonal = at(z, y, 1 - core, 1 - x)
+    links.add("mx", small_far, small_got.at[0], partners.x)
+    links.add("md", small_far, small_got.at[1], diagonal)
+    links.add("mc", small_mine, small_got.at[2], partners.core)
+    spot = 2 * z + y
+    others = []
+    for shift in range(4):
+        for flip in (0, 1):
+            if shift or flip:
+                other = at(turn(z, shift), y + flip - 2 * y * flip, core, x)
+                links.add(f"ms{shift}{flip}", small_all.at[spot], small_all.at[spot], other)
+                others.append(other)
+    spread_small = [f"ms{shift}{flip}" for shift in range(4) for flip in (0, 1) if shift or flip]
 
     def proj_grads():
         grad = grad_ref[...].reshape(-1, grad_ref.shape[2])
         return [dot_tn(att_ref[pair].reshape(-1, PAIR * WIDE), grad) for pair in (0, 1)]
+
+    p, zero, one, two = (units[unit[0]] for unit in UNITS)
+
+    def sum_core(name, *parts):
+        links.arrived("hx" + name)
+        first = 0
+        for part, rows in zip(parts, (384, 192) if len(parts) > 1 else (far[name].got.shape[0],)):
+            part.sum_core(far[name].got.at[pl.ds(first, rows)])
+            first += rows
 
     def far_proj():
         for pair, value in enumerate(proj_grads()):
@@ -740,18 +774,25 @@
         far[name].begin()
 
     def own_qkv(name):
-        narrow(qkv_grad(), units[name].own, 0)
-        units[name].begin()
+        grad = qkv_grad()
+        if name == "0":
+            narrow(grad, zero.own, 0)
+            zero.begin()
+        else:
+            narrow(grad[: 4 * WIDE], one.own, 0)
+            narrow(grad[4 * WIDE :], two.own, 0)
+            one.begin()
+            two.begin()
 
     def begin():
-        greet(partners.all())
+        greet([partners.x, partners.core, diagonal] + others)
         for copy in loads:
             copy.start()
         d_gain[...] = jnp.zeros_like(d_gain)
         d_taps[...] = jnp.zeros_like(d_taps)
-        for name in ("0", "1"):
-            padding = units[name].own.shape[0] - 576
-            units[name].own[576:] = jnp.zeros((padding, units[name].own.shape[1]), BF16)
+        for name, rows, padded, _ in UNITS:
+            if padded > rows:
+                units[name].own[rows:] = jnp.zeros((padded - rows, units[name].own.shape[1]), BF16)
 
     def begin_sums():
         for copy in loads:
@@ -806,7 +847,6 @@
         d_x_ref[0], gain = input_grad(x_ref[0], grad, gain_ref, grad_ref[clip])
         d_gain[...] += gain
 
-    p, zero, one = (units[name] for name, _, _ in UNITS)
     at_steps(
         {
             0: [begin_sums],
@@ -815,17 +855,17 @@
             3: [lambda: far_qkv("0")],
             4: [far["0"].pass_on],
             5: [lambda: all_sums("first")],
-            7: [lambda: far_qkv("1"), lambda: all_sums("second")],
-            8: [far["1"].pass_on],
-            9: [lambda: p.sum_core(far["p"])],
-            10: [finish],
-            11: [lambda: own_qkv("0"), p.sum_y],
-            12: [lambda: zero.sum_core(far["0"])],
-            13: [p.sum_z],
-            14: [zero.sum_y, p.spread_y],
-            15: [lambda: own_qkv("1"), zero.sum_z, p.spread_core],
-            16: [lambda: one.sum_core(far["1"])],
-            17: [zero.spread_y, p.done, save[0].start],
+            7: [lambda: far_qkv("1")],
+            8: [far["1"].pass_on, lambda: all_sums("second")],
+            9: [lambda: sum_core("p", p)],
+            11: [lambda: own_qkv("0"), p.sum_one],
+            12: [lambda: sum_core("0", zero), finish],
+            13: [p.sum_two],
+            14: [zero.sum_one, p.spread_one],
+            15: [lambda: own_qkv("1"), zero.sum_two, p.spread_core],
+            16: [lambda: sum_core("1", one, two), zero.spread_one],
+            17: [one.sum_one, two.sum_one, p.done, save[0].start],
+            18: [one.sum_two, two.sum_two, zero.spread_core],
         }
     )
 
@@ -837,27 +877,25 @@
             target[1:2] = gain_two_ref[...]
             for j in (0, 1):
                 target[8:16, WIDE * j : WIDE * (j + 1)] = d_taps[i + j].reshape(8, WIDE)
-        links.start("mx")
-        one.sum_y()
-        links.arrived("mx")
-        small_mine[...] += small_x[...]
-        links.start("mc")
-        zero.spread_core()
-        links.arrived("mc")
-        small_core[...] += small_mine[...]
-        links.start("my")
-        one.sum_z()
-        links.arrived("my")
-        small_z[pl.ds(z, 1)] = (small_y[...] + small_core[...])[None]
-        links.start("mz1", "mz2", "mz3")
+        links.start("mx", "md", "mc")
+        one.spread_one()
+        two.spread_one()
+        links.arrived("mx", "md", "mc")
+        small_all[pl.ds(spot, 1)] = ((small_mine[...] + small_got[2]) + (small_got[0] + small_got[1]))[None]
+        links.start(*spread_small)
         zero.done()
         save[1].start()
-        one.spread_y()
-        links.arrived("mz1", "mz2", "mz3")
-        small_out[...] = (small_z[0] + small_z[1]) + (small_z[2] + small_z[3])
         one.spread_core()
+        two.spread_core()
+        links.arrived(*spread_small)
+        total = small_all[0]
+        for i in range(1, 8):
+            total = total + small_all[i]
+        small_out[...] = total
         one.done()
+        two.done()
         save[2].start()
+        save[3].start()
         for copy in save + first_done:
             copy.wait()
         for tile in range(late):
@@ -1078,18 +1116,19 @@
 
     def memory(clip):
         links.arrived(f"m{clip}")
+        if clip + 2 < clips:
+            links.start(f"m{clip + 2}")
         saved[4 + clip].start()
 
     plan = {
-        1: [settle],
-        2: [lambda: begin("qp"), lambda: links.start("m0")],
-        3: [lambda: begin("01"), lambda: links.start("m1")],
-        4: [lambda: hop(1, "qp")],
-        5: [lambda: links.start("m2")],
-        6: [lambda: hop(2, "qp"), lambda: links.start("m3")],
-        7: [lambda: hop(3, "qp")],
-        8: [lambda: hop(1, "0"), weights, lambda: memory(0)],
-        9: [lambda: hop(1, "1")] + [copy.start for copy in saved[:3]],
+        1: [settle, lambda: begin("qp"), lambda: links.start("m0")],
+        2: [lambda: begin("01")],
+        3: [lambda: hop(1, "qp")],
+        5: [lambda: hop(2, "qp"), lambda: links.start("m1")],
+        6: [lambda: hop(3, "qp")],
+        7: [lambda: hop(1, "0")],
+        8: [weights, lambda: hop(1, "1"), lambda: memory(0)],
+        9: [copy.start for copy in saved[:3]],
         10: [lambda: hop(2, "0"), lambda: memory(1)],
         11: [lambda: hop(2, "1"), lambda: across(0, "01")],
         12: [lambda: across(1, "0"), lambda: memory(2)],
@@ -1440,14 +1479,17 @@
     left = d_first.shape[0]
     first_shape, second_shape = d_first.shape[-2:], d_second.shape[-2:]
     units = []
-    for _, rows, padded in UNITS:
+    for _, _, padded, order in UNITS:
+        one, three = (2, 8) if order == "yz" else (8, 4)
         units += [
             pltpu.VMEM(shape, BF16)
             for shape in (
-                (padded, width), (padded, CORE_LANES), (padded // 2, CORE_LANES), (3, padded // 8, CORE_LANES), (padded, width),
-                (rows, width), (rows, CORE_LANES), (rows, CORE_LANES),
+                (padded, width), (padded, CORE_LANES), (padded // one, CORE_LANES), (3, padded // three, CORE_LANES),
+                (padded, width),
             )
         ]
+    for _, rows in FAR:
+        units += [pltpu.VMEM(shape, BF16) for shape in ((rows, width), (rows, CORE_LANES), (rows, CORE_LANES))]
     return pl.pallas_call(
         backward_links_kernel,
         grid=(steps + clips,),
@@ -1489,14 +1531,15 @@
             pltpu.VMEM((1, width), F32),
             pltpu.VMEM((4, PAIR, 4, WIDE), F32),
         ]
-        + [pltpu.VMEM(small, F32)] * 5
+        + [pltpu.VMEM(small, F32)] * 2
         + [
-            pltpu.VMEM((4,) + small, F32),
+            pltpu.VMEM((3,) + small, F32),
+            pltpu.VMEM((8,) + small, F32),
             pltpu.VMEM((left,) + first_shape, F32),
             pltpu.VMEM(second_shape, F32),
             pltpu.SemaphoreType.DMA((BACKWARD_COPIES,)),
             pltpu.SemaphoreType.DMA((BACKWARD_COPIES,)),
-            pltpu.SemaphoreType.DMA((6 + left,)),
+            pltpu.SemaphoreType.DMA((7 + left,)),
         ]
         + sum_scratch((left,), 4, first_shape)
         + sum_scratch((left,), 1, second_shape)

time: 312 us -> 305 us (0.978)
  Pallas kernels: 293 us -> 289 us
where the time goes in v6:
time: 305 us; the launch traced here: 306 us
  Pallas kernels  289 us (95%)
  local copies, waits for them, and re-layouts  8.41 us (3%)
  other arithmetic  7.81 us (3%)
    pallas_call x1, Pallas kernels, attention_backward_links(): pl.pallas_call(backward_links_kernel, grid=(steps + clips,), in_specs=[pl...  130 us
    pallas_call x1, Pallas kernels, attention_forward_links(): pl.pallas_call(forward_links_kernel, grid=(4 * clips,), in_specs=[pl.Bloc...  83.8 us
    pallas_call x1, Pallas kernels, mlp_links(): pl.pallas_call(mlp_links_kernel, grid=(TILES + clips,), in_specs=[once((r...  75.4 us

profile of v6, /device:TPU:0, one launch (start us, length us, event | category | flops | bytes accessed | tf_op | source)
XLA Modules:
  0.0 306.0 jit_solution(1420347447512649637)
XLA Ops:
  0.6 0.0 copy-start.5
  0.7 1.6 slice.24
  2.2 0.7 copy.20
  2.9 0.7 pad_bitcast_fusion.tail_own
  3.6 0.0 copy-done.5
  3.6 0.6 convert.4.taps_own
  4.2 83.8 %attention_forward_links.1 = (bf16[4,4,400,768]{3,2,1,0:T(8,128)(2,1)}, bf16[4,4,2,2,256,128]{5,4,3,2,1,0:T(8,128)(2,1)}, bf16[4,4,400,256]{3,2,1,0:T(8,128)(2,1...) custom-call(s32[2,4]{1,0:T(2,128)} %bitcast.60, ...), custom_call_target="tpu_custom_call" | custom-call | tf_op jit(solution)/shard_map/attention_forward_links/pallas_call | solution.py:1188
  88.0 75.4 %mlp_links.1 = (bf16[4,392,768]{2,1,0:T(8,128)(2,1)}, bf16[1600,768]{1,0:T(8,128)(2,1)}, f32[1,768]{1,0:T(1,128)}, f32[24,1536]{1,0:T(8,128)}, f32[96,768]{1,0:T...) custom-call(bf16[1600,768]{1,0:T(8,128)(2,1)} %bitcast.48, ...), custom_call_target="tpu_custom_call" | custom-call | tf_op jit(solution)/shard_map/mlp_links/pallas_call | solution.py:1370
  163.3 0.0 copy-start.3
  163.4 0.0 copy-start.4
  163.4 129.7 %attention_backward_links.1 = (bf16[4,392,768]{2,1,0:T(8,128)(2,1)}, f32[16,768]{1,0:T(8,128)}, f32[24,1536]{1,0:T(8,128)}, f32[96,768]{1,0:T(8,128)}, bf16[384,...) custom-call(s32[2,4]{1,0:T(2,128)} %bitcast.61, bf16[4,392,768]{2,1,0:T(8,128)(2,1)} %bitcast.42, ...), custom_call_target="tpu_custom_call" | custom-call | tf_op jit(solution)/shard_map/attention_backward_links/pallas_call | solution.py:1493
  293.1 0.0 copy-done.3
  293.1 0.8 broadcast_select_fusion
  293.9 0.0 copy-done.4
  293.9 1.6 pad_maximum_fusion
  295.5 0.0 copy-start.2
  295.5 0.0 copy-start
  295.5 3.7 %convert_bitcast_fusion = f32[768,4,288]{0,2,1:T(8,128)} fusion(bf16[4,288,768]{2,1,0:T(8,128)(2,1)} %bitcast.53), kind=kLoop, calls=%fused_computation | loop fusion | flops 884736 | bytes 5308416 | tf_op jit(solution)/shard_map/transpose | solution.py:1673
  299.3 0.0 copy-done.2
  299.3 1.1 convert.6
  300.4 0.7 slice.21
  301.1 0.1 constant_dynamic-slice_fusion
  301.2 0.5 slice_bitcast_fusion
  301.7 0.7 slice.19
  302.4 0.0 copy-start.1
  302.4 0.6 copy.21
  303.0 0.0 copy-done
  303.0 1.4 copy.26
  304.4 0.0 copy-done.1
  304.4 1.4 copy.27
  (1 shorter events, 0.0 us)
Async XLA Ops:
  0.6 2.9 copy-start.5
  163.3 129.8 %copy-start.3 = (f32[96,768]{1,0:T(8,128)S(1)}, f32[96,768]{1,0:T(8,128)}, u32[]{:S(2)}) copy-start(f32[96,768]{1,0:T(8,128)} %get-tuple-element.62) | copy-start | bytes 884740
  163.4 130.5 %copy-start.4 = (f32[24,1536]{1,0:T(8,128)S(1)}, f32[24,1536]{1,0:T(8,128)}, u32[]{:S(2)}) copy-start(f32[24,1536]{1,0:T(8,128)} %get-tuple-element.59) | copy-start | bytes 442372
  295.5 3.7 %copy-start.2 = (bf16[384,768]{1,0:T(8,128)(2,1)S(1)}, bf16[384,768]{1,0:T(8,128)(2,1)}, u32[]{:S(2)}) copy-start(bf16[384,768]{1,0:T(8,128)(2,1)} %get-tuple-element.57) | copy-start | bytes 1769476
  295.5 7.5 %copy-start = (bf16[4,392,768]{2,1,0:T(8,128)(2,1)S(1)}, bf16[4,392,768]{2,1,0:T(8,128)(2,1)}, u32[]{:S(2)}) copy-start(bf16[4,392,768]{2,1,0:T(8,128)(2,1)} %get-tuple-element.41) | copy-start | bytes 7225348
  302.4 2.0 copy-start.1

commit v7 on v6

--- a/solution.py
+++ b/solution.py
@@ -688,7 +688,7 @@
     index_ref, x_ref, qkv_ref, proj_ref, mem_ref, taps_ref, gain_ref,
     packed_ref, keys_ref, att_ref, log_ref, normed_ref, grad_ref, gain_two_ref,
     d_first, d_second,
-    d_x_ref, small_out, first_out, second_out, proj_out, qkv_out,
+    d_x_ref, small_out, taps_out, first_out, second_out, proj_out, qkv_out,
     grad_packed, d_gain, d_taps,
     small_mine, small_far, small_got, small_all,
     first_result, second_result, send, recv, near, *rest,
@@ -764,9 +764,13 @@
             narrow(value, units["p"].own, 192 * pair)
         units["p"].begin()
 
+    def pair_lanes():
+        pair = lax.rem(lax.div(step, 4) + 2, 4)
+        return pl.ds(pl.multiple_of(pair * (PIECES * WIDE), PIECES * WIDE), PIECES * WIDE)
+
     def qkv_grad():
         width = normed_ref.shape[2]
-        grad = grad_packed[lax.div(step, 4)].reshape(-1, PIECES * WIDE)
+        grad = grad_packed[:, :, pair_lanes()].reshape(-1, PIECES * WIDE)
         return dot_tn(grad, normed_ref[...].reshape(-1, width))
 
     def far_qkv(name):
@@ -831,7 +835,7 @@
         pair = lax.rem(lax.div(step, 4) + 2, 4)
         clip = lax.rem(step, 4)
         here = pl.ds(clip, 1)
-        grad_packed[lax.div(step, 4), here] = backward_attention(
+        grad_packed[here, :, pair_lanes()] = backward_attention(
             pair, mask_rows(index_ref[x, clip]), proj_ref.at[0], d_taps.at[lax.div(step, 4)],
             mem_ref.at[0], taps_ref.at[0], packed_ref.at[0, 0], keys_ref.at[0, 0], att_ref.at[lax.rem(pair, 2), clip], log_ref,
             grad_ref.at[clip],
@@ -840,10 +844,7 @@
     @pl.when(step >= 16)
     def _():
         clip = step - 16
-        grad = [
-            dot(grad_packed[slot, clip], qkv_ref[(slot + 2) % 4].reshape(PIECES * WIDE, -1)) for slot in range(4)
-        ]
-        grad = (grad[0] + grad[1]) + (grad[2] + grad[3])
+        grad = dot(grad_packed[clip], qkv_ref[...].reshape(4 * PIECES * WIDE, -1))
         d_x_ref[0], gain = input_grad(x_ref[0], grad, gain_ref, grad_ref[clip])
         d_gain[...] += gain
 
@@ -892,6 +893,10 @@
         for i in range(1, 8):
             total = total + small_all[i]
         small_out[...] = total
+        for pair in (0, 1):
+            for head in range(PAIR):
+                rows = slice(8 + 4 * head, 12 + 4 * head)
+                taps_out[PAIR * pair + head] = total[rows, WIDE * pair : WIDE * pair + HD]
         one.done()
         two.done()
         save[2].start()
@@ -1517,17 +1522,19 @@
         out_specs=[
             pl.BlockSpec((1, TPC, width), lambda s: (late(s), 0, 0)),
             pl.BlockSpec(small, lambda s: (0, 0)),
+            pl.BlockSpec((4, 4, HD), lambda s: (0, 0, 0)),
         ] + [anywhere] * 4,
         out_shape=[
             shaped((clips, TPC, width), BF16),
             shaped(small, F32),
+            shaped((4, 4, HD), F32),
             shaped((first_shape[0], left * TILE), F32),
             shaped(second_shape, F32),
             shaped((UNITS[0][1], width), BF16),
             shaped((2, UNITS[1][1], width), BF16),
         ],
         scratch_shapes=[
-            pltpu.VMEM((4, clips, ROWS, packed_width), BF16),
+            pltpu.VMEM((clips, ROWS, 4 * packed_width), BF16),
             pltpu.VMEM((1, width), F32),
             pltpu.VMEM((4, PAIR, 4, WIDE), F32),
         ]
@@ -1654,7 +1661,7 @@
     else:
         outputs, grad, d_first, d_second, d_gain_two = mlp(*mlp_args)
     if linked:
-        d_x, small, last_first, last_second, d_proj, d_qkv = attention_backward_links(
+        d_x, small, d_taps, last_first, last_second, d_proj, d_qkv = attention_backward_links(
             clip_index.T, x, qkv_all, proj_all, mem_all, taps_all, gain_one,
             packed, keys, att, log, normed, grad.reshape(clips, ROWS, width), d_gain_two,
             first_left, second_left,
@@ -1663,7 +1670,6 @@
         d_second = jnp.where(lax.axis_index("batch") // (batches // TILES) >= EARLY, last_second, d_second)
         d_qkv = d_qkv.astype(F32).reshape(own_heads, 3 * HD, width)
         d_proj = d_proj.astype(F32).reshape(own_heads, HD, width)
-        d_taps = small[8:, : 2 * WIDE].reshape(PAIR, 4, 2, WIDE).transpose(2, 0, 1, 3)[..., :HD]
         share = width // (batches * heads)
         start = (lax.axis_index("batch") * heads + me) * share
         d_gains = lax.dynamic_slice_in_dim(small[:2], start, share, axis=1)
@@ -1672,7 +1678,7 @@
             d_x.reshape(inputs.shape),
             d_qkv.transpose(2, 0, 1),
             d_proj,
-            d_taps.reshape(own_heads, 4, HD),
+            d_taps,
             d_gains[0],
             d_gains[1],
             d_first,

time: 305 us -> 304 us (level)
  no operation moved by 1% of the time
where the time goes in v7:
time: 304 us; the launch traced here: 305 us
  Pallas kernels  289 us (95%)
  other arithmetic  7.81 us (3%)
  local copies, waits for them, and re-layouts  7.7 us (3%)
    pallas_call x1, Pallas kernels, attention_backward_links(): pl.pallas_call(backward_links_kernel, grid=(steps + clips,), in_specs=[pl...  130 us
    pallas_call x1, Pallas kernels, attention_forward_links(): pl.pallas_call(forward_links_kernel, grid=(4 * clips,), in_specs=[pl.Bloc...  83.8 us
    pallas_call x1, Pallas kernels, mlp_links(): pl.pallas_call(mlp_links_kernel, grid=(TILES + clips,), in_specs=[once((r...  75.4 us

profile of v7, /device:TPU:0, one launch (start us, length us, event | category | flops | bytes accessed | tf_op | source)
XLA Modules:
  0.0 305.4 jit_solution(11474098677381008105)
XLA Ops:
  0.6 0.0 copy-start.6
  0.7 1.6 slice.16
  2.2 0.7 copy.20
  2.9 0.7 pad_bitcast_fusion.tail_own
  3.6 0.0 copy-done.6
  3.6 0.6 convert.4.taps_own
  4.2 83.8 %attention_forward_links.1 = (bf16[4,4,400,768]{3,2,1,0:T(8,128)(2,1)}, bf16[4,4,2,2,256,128]{5,4,3,2,1,0:T(8,128)(2,1)}, bf16[4,4,400,256]{3,2,1,0:T(8,128)(2,1...) custom-call(s32[2,4]{1,0:T(2,128)} %bitcast.55, ...), custom_call_target="tpu_custom_call" | custom-call | tf_op jit(solution)/shard_map/attention_forward_links/pallas_call | solution.py:1193
  88.0 75.4 %mlp_links.1 = (bf16[4,392,768]{2,1,0:T(8,128)(2,1)}, bf16[1600,768]{1,0:T(8,128)(2,1)}, f32[1,768]{1,0:T(1,128)}, f32[24,1536]{1,0:T(8,128)}, f32[96,768]{1,0:T...) custom-call(bf16[1600,768]{1,0:T(8,128)(2,1)} %bitcast.45, ...), custom_call_target="tpu_custom_call" | custom-call | tf_op jit(solution)/shard_map/mlp_links/pallas_call | solution.py:1375
  163.3 0.0 copy-start.3
  163.3 0.0 copy-start.4
  163.3 129.8 %attention_backward_links.1 = (bf16[4,392,768]{2,1,0:T(8,128)(2,1)}, f32[16,768]{1,0:T(8,128)}, f32[4,4,96]{2,1,0:T(4,128)}, f32[24,1536]{1,0:T(8,128)}, f32[96,...) custom-call(s32[2,4]{1,0:T(2,128)} %bitcast.56, bf16[4,392,768]{2,1,0:T(8,128)(2,1)} %bitcast.39, ...), custom_call_target="tpu_custom_call" | custom-call | tf_op jit(solution)/shard_map/attention_backward_links/pallas_call | solution.py:1498
  293.2 0.0 copy-done.3
  293.2 0.8 broadcast_select_fusion
  294.0 0.0 copy-done.4
  294.0 1.6 pad_maximum_fusion
  295.6 0.0 copy-start.2
  295.6 0.0 copy-start
  295.6 3.7 %convert_bitcast_fusion = f32[768,4,288]{0,2,1:T(8,128)} fusion(bf16[4,288,768]{2,1,0:T(8,128)(2,1)} %bitcast.50), kind=kLoop, calls=%fused_computation | loop fusion | flops 884736 | bytes 5308416 | tf_op jit(solution)/shard_map/transpose | solution.py:1679
  299.3 0.0 copy-done.2
  299.3 1.1 convert.6
  300.4 0.7 slice.13
  301.2 0.0 copy-start.1
  301.2 0.1 constant_dynamic-slice_fusion
  301.3 0.5 slice_bitcast_fusion
  301.8 0.0 copy-done
  301.8 1.4 copy.26
  303.2 0.0 copy-done.1
  303.2 0.0 copy-start.5
  303.2 1.4 copy.27
  304.6 0.0 copy-done.5
  304.6 0.6 copy.28
Async XLA Ops:
  0.6 2.9 copy-start.6
  163.3 129.9 %copy-start.3 = (f32[96,768]{1,0:T(8,128)S(1)}, f32[96,768]{1,0:T(8,128)}, u32[]{:S(2)}) copy-start(f32[96,768]{1,0:T(8,128)} %get-tuple-element.64) | copy-start | bytes 884740
  163.3 130.6 %copy-start.4 = (f32[24,1536]{1,0:T(8,128)S(1)}, f32[24,1536]{1,0:T(8,128)}, u32[]{:S(2)}) copy-start(f32[24,1536]{1,0:T(8,128)} %get-tuple-element.61) | copy-start | bytes 442372
  295.6 3.7 %copy-start.2 = (bf16[384,768]{1,0:T(8,128)(2,1)S(1)}, bf16[384,768]{1,0:T(8,128)(2,1)}, u32[]{:S(2)}) copy-start(bf16[384,768]{1,0:T(8,128)(2,1)} %get-tuple-element.58) | copy-start | bytes 1769476
  295.6 6.2 %copy-start = (bf16[4,392,768]{2,1,0:T(8,128)(2,1)S(1)}, bf16[4,392,768]{2,1,0:T(8,128)(2,1)}, u32[]{:S(2)}) copy-start(bf16[4,392,768]{2,1,0:T(8,128)(2,1)} %get-tuple-element.42) | copy-start | bytes 7225348
  301.2 2.0 copy-start.1
  303.2 1.4 copy-start.5
